TPU v7x, 32 devices: a whole 2x2x4 slice. The times are simulated.
32 devices in a mesh: chan: 8 (over z, y), batch: 4 (over x, core).
Axes of the slice: x: 2, y: 2, z: 4, core: 2. Of those that a mesh axis runs over, the one named last changes fastest.
Arguments:
- images: bfloat16 [1536, 49, 2048], P('batch', None, 'chan'), may hold values from -6 to 6
- pixel_mask: int32 [1536, 49], P('batch'), may hold values from 0 to 1, as said below
- labels: int32 [1536], P('batch'), may hold values from 0 to 999
- reduce_weight: float32 [512, 2048], P('chan'), may hold values from -0.1875 to 0.1875
- reduce_mask: int32 [512, 2048], P('chan'), may hold values 0 or 1
- spatial_weight: float32 [512, 4608], P('chan'), may hold values from -0.125 to 0.125
- spatial_mask: int32 [512, 4608], P('chan'), may hold values 0 or 1
- head_weight: float32 [512, 1000], P('chan'), may hold values from -1 to 1
- head_bias: float32 [1000], replicated, may hold values from -3 to 3
- norm_params: float32 [4, 512], P(None, 'chan')
- left_stats: float32 [13, 512, 512], P(None, 'chan')
- right_stats: float32 [13, 512, 512], P(None, 'chan')
- left_root: float32 [13, 512, 512], P(None, 'chan'), as said below
- input_side_roots: float32 [13, 512, 512], P(None, 'chan'), as said below
- head_first: float32 [512, 1000], P('chan'), may hold values from -0.0024414062 to 0.0024414062
- head_second: float32 [512, 1000], P('chan'), may hold values from 2.6041667e-09 to 1.0416667e-08
- bias_first: float32 [1000], replicated, may hold values from -0.0048828125 to 0.0048828125
- bias_second: float32 [1000], replicated, may hold values from 1.0416667e-08 to 4.1666667e-08
- norm_first: float32 [4, 512], P(None, 'chan'), may hold values from -0.046875 to 0.046875
- norm_second: float32 [4, 512], P(None, 'chan'), may hold values from 9.375e-07 to 3.75e-06
Outputs:
- loss_sum: float32 [], replicated
- slot_count: float32 [], replicated
- reduce_grad: float32 [512, 2048], P('chan')
- spatial_grad: float32 [512, 4608], P('chan')
- reduce_new: float32 [512, 2048], P('chan')
- spatial_new: float32 [512, 4608], P('chan')
- left_new: float32 [13, 512, 512], P(None, 'chan')
- right_new: float32 [13, 512, 512], P(None, 'chan')
- head_new: float32 [512, 1000], P('chan')
- head_first_new: float32 [512, 1000], P('chan')
- head_second_new: float32 [512, 1000], P('chan')
- bias_new: float32 [1000], replicated
- bias_first_new: float32 [1000], replicated
- bias_second_new: float32 [1000], replicated
- norm_new: float32 [4, 512], P(None, 'chan')
- norm_first_new: float32 [4, 512], P(None, 'chan')
- norm_second_new: float32 [4, 512], P(None, 'chan')
Inputs may be any that keep to these rules, and one draw needn't show every extreme that they name: `pixel_mask`: the last of every 384 slots in a row is used; every used slot has its centre pixel valid. `left_root`: symmetric. `input_side_roots`: symmetric.
All inputs are finite; a program needn't handle non-finite values. No bound on the sum of `reduce_mask` or of `spatial_mask` on one device may be relied on, other than what follows from the above.
Results may differ from a plain program's by a relative error of at most 0.0045.
The roundings to bfloat16 on the way count: a program that leaves them out, or rounds other values in their place, can miss the bound.
Values may be sent and summed in bfloat16 or wider, within the bound.
A program may use at most 640 MiB of HBM per device.

v0:
```python
import jax
import jax.numpy as jnp
from jax import lax
from jax.sharding import PartitionSpec as P

SIDE = 7
SLOTS_DEV = 384
STEP = 10


FULL_PRECISION = lax.Precision.HIGHEST
EPS = 1e-05


def silu_slope(pre):
    sigma = jax.nn.sigmoid(pre)
    return sigma * (1.0 + pre * (1.0 - sigma))


def norm_forward(pre_norm, gain, shift, valid):
    first_sum = jnp.sum(pre_norm * valid, axis=(0, 1))
    second_sum = jnp.sum(pre_norm * pre_norm * valid, axis=(0, 1))
    first_sum, second_sum, count = lax.psum((first_sum, second_sum, jnp.sum(valid)), "batch")
    mean = first_sum / count
    scale = lax.rsqrt(second_sum / count - mean * mean + EPS)
    normed = (pre_norm - mean) * scale
    pre = gain * normed + shift
    return (jax.nn.silu(pre) * valid, (normed, pre, scale, count))


def norm_backward(grad_act, kept, gain, valid):
    normed, pre, scale, count = kept
    d_pre = grad_act * valid * silu_slope(pre)
    shift_gradient, gain_grad = lax.psum(
        (jnp.sum(d_pre, axis=(0, 1)), jnp.sum(d_pre * normed, axis=(0, 1))), "batch"
    )
    d_input = gain * scale / count * (count * d_pre - shift_gradient - normed * gain_grad) * valid
    return (d_input, gain_grad, shift_gradient)


def shift_grid(grid, dy, dx):
    side = grid.shape[1]
    padded = jnp.pad(grid, ((0, 0), (1, 1), (1, 1), (0, 0)))
    return padded[:, 1 + dy : 1 + dy + side, 1 + dx : 1 + dx + side, :]


def spread_back(d_rows, taps, offsets):
    total = jnp.zeros(d_rows.shape[:3] + (taps.shape[2],), jnp.float32)
    for index, (dy, dx) in enumerate(offsets):
        spread = jnp.einsum(
            "syxo,oi->syxi", d_rows, taps[:, index, :], preferred_element_type=jnp.float32
        )
        total = total + shift_grid(spread, -dy, -dx)
    return total


def adam_step(param, grad, first, second, rate, decay):
    first = 0.9 * first + 0.1 * grad
    second = 0.999 * second + 0.001 * grad * grad
    mhat = first / (1.0 - 0.9**STEP)
    vhat = second / (1.0 - 0.999**STEP)
    return (param - rate * (mhat / (jnp.sqrt(vhat) + 1e-08) + decay * param), first, second)


def body(
    images,
    pixel_mask,
    labels,
    reduce_weight,
    reduce_mask,
    spatial_weight,
    spatial_mask,
    head_weight,
    head_bias,
    norm_params,
    left_stats,
    right_stats,
    left_root,
    input_side_roots,
    head_first,
    head_second,
    bias_first,
    bias_second,
    norm_first,
    norm_second,
):
    right_factor_full = lax.all_gather(input_side_roots, "chan", axis=1, tiled=True)
    slots = images.shape[0]
    pixels = images.shape[1]
    side = SIDE
    rows_out = reduce_weight.shape[0]
    width = left_stats.shape[2]
    classes = head_weight.shape[1]
    valid = pixel_mask.astype(jnp.float32)[:, :, None]
    filled = jnp.sum(valid[:, :, 0], axis=1)
    divisor = jnp.maximum(filled, 1.0)
    used = (filled > 0.0).astype(jnp.float32)
    reduce_float = reduce_mask.astype(jnp.float32)
    spatial_float = spatial_mask.astype(jnp.float32)
    reduce_low = (reduce_weight * reduce_float).astype(jnp.bfloat16)
    spatial_taps = (spatial_weight * spatial_float).astype(jnp.bfloat16).reshape(rows_out, 9, width)
    head_low = head_weight.astype(jnp.bfloat16)
    offsets = [(dy, dx) for dy in (-1, 0, 1) for dx in (-1, 0, 1)]
    first_pre = jnp.einsum(
        "spc,oc->spo",
        lax.all_gather(images, "chan", axis=2, tiled=True),
        reduce_low,
        preferred_element_type=jnp.float32,
    )
    first_act, first_kept = norm_forward(first_pre, norm_params[0], norm_params[1], valid)
    hidden = first_act.astype(jnp.bfloat16)
    hidden_full = lax.all_gather(hidden, "chan", axis=2, tiled=True).reshape(
        slots, side, side, width
    )
    second_pre = jnp.zeros((slots, side, side, rows_out), jnp.float32)
    for index, (dy, dx) in enumerate(offsets):
        second_pre = second_pre + jnp.einsum(
            "syxi,oi->syxo",
            shift_grid(hidden_full, dy, dx),
            spatial_taps[:, index, :],
            preferred_element_type=jnp.float32,
        )
    second_act, second_kept = norm_forward(
        second_pre.reshape(slots, pixels, rows_out), norm_params[2], norm_params[3], valid
    )
    pooled = (jnp.sum(second_act, axis=1) / divisor[:, None]).astype(jnp.bfloat16)
    logits = (
        lax.psum(jnp.dot(pooled, head_low, preferred_element_type=jnp.float32), "chan") + head_bias
    )
    onehot = (jnp.arange(classes)[None, :] == labels[:, None]).astype(jnp.float32)
    log_total = jax.nn.logsumexp(logits, axis=1)
    picked = jnp.sum(onehot * logits, axis=1)
    loss_local = jnp.sum(used * (log_total - picked))
    d_logits = (used[:, None] * (jnp.exp(logits - log_total[:, None]) - onehot) / SLOTS_DEV).astype(
        jnp.bfloat16
    )
    head_grad = jnp.einsum("so,sc->oc", pooled, d_logits, preferred_element_type=jnp.float32)
    bias_grad = jnp.sum(d_logits.astype(jnp.float32), axis=0)
    d_pooled = jnp.einsum("sc,oc->so", d_logits, head_low, preferred_element_type=jnp.float32)
    d_act = jnp.broadcast_to((d_pooled / divisor[:, None])[:, None, :], second_act.shape)
    d_second, gain_two, shift_two = norm_backward(d_act, second_kept, norm_params[2], valid)
    d_second = d_second.astype(jnp.bfloat16).reshape(slots, side, side, rows_out)
    tap_grads = []
    for index, (dy, dx) in enumerate(offsets):
        tap_grads.append(
            jnp.einsum(
                "syxi,syxo->oi",
                shift_grid(hidden_full, dy, dx),
                d_second,
                preferred_element_type=jnp.float32,
            )
        )
    spatial_local = jnp.stack(tap_grads, axis=1).reshape(rows_out, 9 * width) * spatial_float
    hidden_part = spread_back(d_second, spatial_taps, offsets)
    d_hidden = lax.psum_scatter(hidden_part, "chan", scatter_dimension=3, tiled=True).reshape(
        slots, pixels, rows_out
    )
    d_first, gain_one, shift_one = norm_backward(d_hidden, first_kept, norm_params[0], valid)
    d_first = d_first.astype(jnp.bfloat16)
    reduce_local = jnp.einsum(
        "spc,spo->oc",
        lax.all_gather(images, "chan", axis=2, tiled=True),
        d_first,
        preferred_element_type=jnp.float32,
    )
    reduce_local = reduce_local * reduce_float
    reduce_grad, spatial_grad, head_grad, bias_grad, loss_sum, slot_count = lax.psum(
        (reduce_local, spatial_local, head_grad, bias_grad, loss_local, jnp.sum(used)), "batch"
    )
    norm_gain_gradient = jnp.stack([gain_one, shift_one, gain_two, shift_two], axis=0)
    tiles_one = reduce_weight.shape[1] // width
    blocks = jnp.concatenate(
        [
            reduce_grad.reshape(rows_out, tiles_one, width).transpose(1, 0, 2),
            spatial_grad.reshape(rows_out, 9, width).transpose(1, 0, 2),
        ],
        axis=0,
    )
    blocks_full = lax.all_gather(blocks, "chan", axis=1, tiled=True)
    left_new = 0.95 * left_stats + jnp.einsum(
        "tak,tbk->tab", blocks, blocks_full, precision=FULL_PRECISION
    )
    own_columns = lax.dynamic_slice_in_dim(
        blocks_full, lax.axis_index("chan") * rows_out, rows_out, 2
    )
    right_new = 0.95 * right_stats + jnp.einsum(
        "tki,tkb->tib", own_columns, blocks_full, precision=FULL_PRECISION
    )
    matrix_product = jnp.einsum("tak,tkb->tab", left_root, blocks_full, precision=FULL_PRECISION)
    matrix_product = jnp.einsum(
        "ghk,gkl->ghl", matrix_product, right_factor_full, precision=FULL_PRECISION
    )
    squares = lax.psum(jnp.sum(matrix_product * matrix_product, axis=(1, 2)), "chan")
    step = matrix_product / jnp.sqrt(squares / (width * width) + 1e-06)[:, None, None]
    step_one = step[:tiles_one].transpose(1, 0, 2).reshape(rows_out, tiles_one * width)
    step_two = step[tiles_one:].transpose(1, 0, 2).reshape(rows_out, 9 * width)
    reduce_new = reduce_weight - 0.02 * reduce_float * (step_one + 0.1 * reduce_weight)
    spatial_new = spatial_weight - 0.02 * spatial_float * (step_two + 0.1 * spatial_weight)
    head_new, head_first_new, head_second_new = adam_step(
        head_weight, head_grad, head_first, head_second, 0.04, 0.1
    )
    bias_new, bias_first_new, bias_second_new = adam_step(
        head_bias, bias_grad, bias_first, bias_second, 0.1, 0.0
    )
    norm_new, norm_first_new, norm_second_new = adam_step(
        norm_params, norm_gain_gradient, norm_first, norm_second, 0.1, 0.0
    )
    return (
        loss_sum,
        slot_count,
        reduce_grad,
        spatial_grad,
        reduce_new,
        spatial_new,
        left_new,
        right_new,
        head_new,
        head_first_new,
        head_second_new,
        bias_new,
        bias_first_new,
        bias_second_new,
        norm_new,
        norm_first_new,
        norm_second_new,
    )


def solution(mesh):
    in_specs = (
        P("batch", None, "chan"),
        P("batch", None),
        P("batch"),
        P("chan", None),
        P("chan", None),
        P("chan", None),
        P("chan", None),
        P("chan", None),
        P(),
        P(None, "chan"),
        P(None, "chan", None),
        P(None, "chan", None),
        P(None, "chan", None),
        P(None, "chan", None),
        P("chan", None),
        P("chan", None),
        P(),
        P(),
        P(None, "chan"),
        P(None, "chan"),
    )
    out_specs = (
        P(),
        P(),
        P("chan", None),
        P("chan", None),
        P("chan", None),
        P("chan", None),
        P(None, "chan", None),
        P(None, "chan", None),
        P("chan", None),
        P("chan", None),
        P("chan", None),
        P(),
        P(),
        P(),
        P(None, "chan"),
        P(None, "chan"),
        P(None, "chan"),
    )
    return jax.shard_map(body, mesh=mesh, in_specs=in_specs, out_specs=out_specs, check_vma=False)
```

profile of v0, /device:TPU:0, one launch (start us, length us, event | category | flops | bytes accessed | tf_op | source)
XLA Modules:
  0.0 3600.1 jit_solution(1091275383558480222)
XLA Ops:
  9.4 1457.9 %all-gather.5.cloned.1.call-done = bf16[384,49,2048]{2,0,1:T(8,128)(2,1)} async-done(((bf16[384,49,256]{2,0,1:T(8,128)(2,1)}), bf16[384,49,2048]{2,0,1:T(8,128)(2,1)}) %all-gather.5.cloned.1.call-update) | async-done | bytes 77070352 | tf_op jit(solution)/shard_map/all_gather | solution.py:106
  1467.3 33.8 multiply_reduce_fusion.4
  1518.5 365.7 %all-gather.7.cloned.1.call-done = bf16[384,49,512]{0,2,1:T(8,128)(2,1)} async-done(((bf16[384,49,64]{0,2,1:T(8,128)(2,1)}), bf16[384,49,512]{0,2,1:T(8,128)(2,1)}) %all-gather.7.cloned.1.call-update) | async-done | bytes 19267600 | tf_op jit(solution)/shard_map/all_gather | solution.py:112
  1929.0 22.8 multiply_reduce_fusion.2
  1965.4 87.8 %all-reduce.17.cloned.1.call-done = f32[384,1000]{0,1:T(8,128)} async-done(((f32[384,1000]{0,1:T(8,128)}), f32[384,1000]{0,1:T(8,128)}) %all-reduce.17.cloned.1.call-update) | async-done | bytes 1536016 | tf_op jit(solution)/shard_map/psum | solution.py:128
  2080.5 15.2 fusion.114
  2095.6 15.1 fusion.118
  2110.7 15.3 fusion.122
  2126.0 15.1 fusion.161
  2141.1 15.5 fusion.126
  2156.6 15.1 fusion.130
  2171.6 15.1 fusion.138
  2186.8 15.1 fusion.134
  2201.9 108.5 %add_add_fusion = f32[384,7,7,512]{3,0,2,1:T(8,128)} fusion(f32[384,7,7,512]{3,0,2,1:T(8,128)} %fusion.114, f32[384,7,7,512]{3,0,2,1:T(8,128)} %fusion.118, f32[384,7,7,512]{3,0,2,1:T(8,128)} %fusion.122, f32[384,7,7,512]{3,0,2,1:T(8,128)} %fusion.161, f32[384,7,7,512]{3,0,2,1:T(8,128)} %fusion.126, f32[384,7,7,512]{3,0,2,1:T(8,128)} %fusion.130, ...), kind=kOutput, calls=%fused_computation.8 | convolution fusion | flops 983040000 | bytes 349290496 | tf_op jit(solution)/shard_map/slice | solution.py:44
  2310.4 41.2 %copy.111 = f32[384,7,7,512]{0,2,1,3:T(8,128)} copy(f32[384,7,7,512]{3,0,2,1:T(8,128)} %add_add_fusion) | data formatting | bytes 77070336 | tf_op jit(solution)/shard_map/add | solution.py:53
  2351.7 25.3 copy.99
  2377.0 91.6 %pad_slice_fusion = (bf16[384,7,7,512]{3,0,2,1:T(8,128)(2,1)}, bf16[384,7,7,512]{3,0,2,1:T(8,128)(2,1)}, bf16[384,7,7,512]{3,0,2,1:T(8,128)(2,1)}, bf16[384,7,7,...) fusion(bf16[384,7,7,512]{3,0,2,1:T(8,128)(2,1)} %copy.99), kind=kLoop, calls=%fused_computation | loop fusion | bytes 173408256 | tf_op jit(solution)/shard_map/slice | solution.py:44
  2468.6 10.8 fusion.47
  2479.5 10.9 fusion.53
  2490.3 11.1 fusion.59
  2512.1 14.0 fusion.95
  2526.0 11.7 fusion.71
  2537.8 11.1 fusion.77
  2574.0 472.4 %reduce-scatter.2.cloned.1.call-done = f32[384,7,7,64]{0,2,1,3:T(8,128)} async-done(((f32[384,7,7,512]{0,2,1,3:T(8,128)}), f32[384,7,7,64]{0,2,1,3:T(8,128)}) %reduce-scatter.2.cloned.1.call-update) | async-done | bytes 4816912 | tf_op jit(solution)/shard_map/reduce_scatter | solution.py:155
  3063.8 30.9 fusion.39
  3094.8 48.0 %all-reduce.19.cloned.1.call-done = (f32[64,2048]{1,0:T(8,128)}, f32[64,4608]{1,0:T(8,128)}, f32[64,1000]{1,0:T(8,128)}) async-done(((f32[64,2048]{1,0:T(8,128)}, f32[64,4608]{1,0:T(8,128)}, f32[64,1000]{1,0:T(8,128)}), (f32[64,2048]{1,0:T(8,128)}, f32[64,4608]{1,0:T(8,128)}, f32[64,1000]{1,0:T(8,128)})) %all-reduce.19.cloned.1.call-update) | async-done | bytes 1959952 | tf_op jit(solution)/shard_map/psum | solution.py:167
  3151.8 185.3 %all-gather.9.cloned.1.call-done = f32[13,512,512]{2,1,0:T(8,128)} async-done(((f32[13,64,512]{2,1,0:T(8,128)}), f32[13,512,512]{2,1,0:T(8,128)}) %all-gather.9.cloned.1.call-update) | async-done | bytes 13631504 | tf_op jit(solution)/shard_map/all_gather | solution.py:179
  3337.1 13.5 fusion.174
  3350.6 176.3 %all-gather.11.cloned.1.call-done = f32[13,512,512]{2,1,0:T(8,128)} async-done(((f32[13,64,512]{2,1,0:T(8,128)}), f32[13,512,512]{2,1,0:T(8,128)}) %all-gather.11.cloned.1.call-update) | async-done | bytes 13631504 | tf_op jit(solution)/shard_map/all_gather | solution.py:87
  3526.9 12.9 multiply_reduce_fusion.6
  3539.9 18.6 psum.136
  3563.4 18.5 multiply_add_fusion.2
  (200 shorter events, 183.0 us)
Async XLA Ops:
  7.2 3329.9 %copy-start = (f32[13,64,512]{2,1,0:T(8,128)S(1)}, f32[13,64,512]{2,1,0:T(8,128)}, u32[]{:S(2)}) copy-start(f32[13,64,512]{2,1,0:T(8,128)} %param.32) | copy-start | bytes 5111812
  7.2 1460.1 %copy-start.10 = (s32[64,2048]{1,0:T(8,128)S(1)}, s32[64,2048]{1,0:T(8,128)}, u32[]{:S(2)}) copy-start(s32[64,2048]{1,0:T(8,128)} %param.24) | copy-start | bytes 1572868
  7.2 1460.1 %copy-start.20 = (f32[64,2048]{1,0:T(8,128)S(1)}, f32[64,2048]{1,0:T(8,128)}, u32[]{:S(2)}) copy-start(f32[64,2048]{1,0:T(8,128)} %param.23) | copy-start | bytes 1572868
  7.2 1460.0 %all-gather.5.cloned.1.call-start = ((), (), s32[]{:S(2)}) async-start(), calls=%async_computation.1 | async-start | bytes 86704128 | tf_op jit(solution)/shard_map/all_gather | solution.py:106
  8.0 1876.2 %all-gather.7.cloned.1.call-start = ((), (), s32[]{:S(2)}) async-start(), calls=%async_computation.2 | async-start | bytes 21676032 | tf_op jit(solution)/shard_map/all_gather | solution.py:112
  8.2 1506.2 %copy-start.16 = (f32[384,49]{0,1:T(8,128)}, f32[384,49]{0,1:T(8,128)S(1)}, u32[]{:S(2)}) copy-start(f32[384,49]{0,1:T(8,128)S(1)} %convert_element_type.76) | copy-start | bytes 225796
  9.4 1499.5 %copy-start.46 = (f32[64]{0:T(128)}, f32[64]{0:T(128)S(1)}, u32[]{:S(2)}) copy-start(f32[64]{0:T(128)S(1)} %get-tuple-element.86) | copy-start | bytes 772
  9.4 1499.5 %copy-start.48 = (f32[64]{0:T(128)}, f32[64]{0:T(128)S(1)}, u32[]{:S(2)}) copy-start(f32[64]{0:T(128)S(1)} %get-tuple-element.87) | copy-start | bytes 772
  1514.2 539.0 %all-reduce.17.cloned.1.call-start = ((), (), s32[]{:S(2)}) async-start(), calls=%async_computation.3 | async-start | bytes 3072000 | tf_op jit(solution)/shard_map/psum | solution.py:128
  1516.9 543.2 %copy-start.35 = (f32[384]{0:T(512)}, f32[384]{0:T(512)S(1)}, u32[]{:S(2)}) copy-start(f32[384]{0:T(512)S(1)} %broadcast_maximum_fusion) | copy-start | bytes 4612
  1518.5 376.0 %copy-start.28 = (bf16[64,1,512]{2,1,0:T(2,128)(2,1)}, bf16[64,1,512]{2,1,0:T(2,128)(2,1)S(1)}, u32[]{:S(2)}) copy-start(bf16[64,1,512]{2,1,0:T(2,128)(2,1)S(1)} %get-tuple-element.84) | copy-start | bytes 196612
  1929.0 30.5 copy-start.50
  1951.7 101.4 %copy-start.33 = (f32[1000]{0:T(1024)S(1)}, f32[1000]{0:T(1024)}, u32[]{:S(2)}) copy-start(f32[1000]{0:T(1024)} %param.28) | copy-start | bytes 12004
  1959.4 95.4 %copy-start.45 = (s32[384]{0:T(512)S(1)}, s32[384]{0:T(512)}, u32[]{:S(2)}) copy-start(s32[384]{0:T(512)} %param.22) | copy-start | bytes 4612
  1965.3 1081.1 %reduce-scatter.2.cloned.1.call-start = ((), (), s32[]{:S(2)}) async-start(), calls=%async_computation.4 | async-start | bytes 49545216 | tf_op jit(solution)/shard_map/reduce_scatter | solution.py:155
  2080.5 106.3 %copy-start.1 = (bf16[384,7,7,64]{0,3,2,1:T(8,128)(2,1)}, bf16[384,7,7,64]{0,3,2,1:T(8,128)(2,1)S(1)}, u32[]{:S(2)}) copy-start(bf16[384,7,7,64]{0,3,2,1:T(8,128)(2,1)S(1)} %multiply_convert_fusion) | copy-start | bytes 7225348
  2186.8 15.1 copy-start.29
  2351.7 791.1 %all-reduce.19.cloned.1.call-start = ((), (), s32[]{:S(2)}) async-start(), calls=%async_computation.7 | async-start | bytes 3932160 | tf_op jit(solution)/shard_map/psum | solution.py:167
  2377.0 91.6 %copy-start.2 = (bf16[384,7,7,64]{0,3,2,1:T(8,128)(2,1)S(1)}, bf16[384,7,7,64]{0,3,2,1:T(8,128)(2,1)}, u32[]{:S(2)}) copy-start(bf16[384,7,7,64]{0,3,2,1:T(8,128)(2,1)} %copy-done.1) | copy-start | bytes 7225348
  2574.0 475.8 %copy-start.17 = (f32[384,49]{0,1:T(8,128)S(1)}, f32[384,49]{0,1:T(8,128)}, u32[]{:S(2)}) copy-start(f32[384,49]{0,1:T(8,128)} %copy-done.16) | copy-start | bytes 225796
  2574.0 475.9 %copy-start.38 = (f32[64]{0:T(128)S(1)}, f32[64]{0:T(128)}, u32[]{:S(2)}) copy-start(f32[64]{0:T(128)} %copy-done.37) | copy-start | bytes 772
  2574.0 475.9 %copy-start.40 = (f32[64]{0:T(128)S(1)}, f32[64]{0:T(128)}, u32[]{:S(2)}) copy-start(f32[64]{0:T(128)} %copy-done.39) | copy-start | bytes 772
  2574.0 475.9 %copy-start.47 = (f32[64]{0:T(128)S(1)}, f32[64]{0:T(128)}, u32[]{:S(2)}) copy-start(f32[64]{0:T(128)} %copy-done.46) | copy-start | bytes 772
  2574.0 475.9 %copy-start.49 = (f32[64]{0:T(128)S(1)}, f32[64]{0:T(128)}, u32[]{:S(2)}) copy-start(f32[64]{0:T(128)} %copy-done.48) | copy-start | bytes 772
  3049.9 13.9 copy-start.11
  3094.7 242.3 %all-gather.9.cloned.1.call-start = ((), (), s32[]{:S(2)}) async-start(), calls=%async_computation.5 | async-start | bytes 15335424 | tf_op jit(solution)/shard_map/all_gather | solution.py:179
  3147.6 379.4 %all-gather.11.cloned.1.call-start = ((), (), s32[]{:S(2)}) async-start(), calls=%async_computation.6 | async-start | bytes 15335424 | tf_op jit(solution)/shard_map/all_gather | solution.py:87
  3561.4 20.5 slice-start
  3562.0 19.9 slice-start.1
  3563.4 18.5 slice-start.2
  3563.4 18.5 slice-start.3
  3563.4 18.5 copy-start.24
  (38 other events, 234.7 us)
Sparse Core Ops, SparseCore 0:
  9.5 1457.7 all-gather.4
  1514.3 369.8 all-gather.6
  1965.5 87.6 all-reduce.16
  2351.8 694.6 reduce-scatter.1
  3094.9 47.8 all-reduce.18
  3147.7 189.3 all-gather.8
  3339.5 187.3 all-gather.10
where the time goes:
time: 3610 us; the launch traced here: 3600 us
  waiting for transfers between devices  2790 us (77%)
  matrix products  519 us (14%)
  local copies, waits for them, and re-layouts  176 us (5%)
  other arithmetic  47.5 us (1%)
  blocking collectives  46.8 us (1%)
    all_gather x1, waiting for transfers between devices, body(): lax.all_gather(images, 'chan', axis=2, tiled=True)  1460 us
    reduce_scatter x1, waiting for transfers between devices, body(): lax.psum_scatter(hidden_part, 'chan', scatter_dimension=3, tiled=True)  472 us
    all_gather x1, waiting for transfers between devices, body(): lax.all_gather(hidden, 'chan', axis=2, tiled=True)  366 us
    slice x8, matrix products, shift_grid(): return padded[:, 1 + dy:1 + dy + side, 1 + dx:1 + dx + side, :]  215 us
    all_gather x1, waiting for transfers between devices, body(): blocks_full = lax.all_gather(blocks, 'chan', axis=1, tiled=True)  185 us
    all_gather x1, waiting for transfers between devices, body(): lax.all_gather(input_side_roots, 'chan', axis=1, tiled=True)  176 us
    dot_general x9, matrix products, body(): jnp.einsum('syxi,syxo->oi', shift_grid(hidden_full, dy, dx), d_second, pr...  102 us
    slice x1, local copies, waits for them, and re-layouts, shift_grid(): return padded[:, 1 + dy:1 + dy + side, 1 + dx:1 + dx + side, :]  91.6 us
  transfers between devices with their start and end apart: 7, of which 7 were waited for; matrix products, arithmetic and copies ran while one was open for 7% of the time, Pallas kernels for 0%

commit v1 on v0

v1 whole, which is shorter than its diff:
```python
import functools

import jax
import jax.numpy as jnp
from jax import lax
from jax.experimental import pallas as pl
from jax.experimental.pallas import tpu as pltpu
from jax.sharding import PartitionSpec as P

SIDE = 7
SLOTS_DEV = 384
STEP = 10

WIDTH = 512
EPS = 1e-05
MESH = pl.DeviceIdType.MESH
ANY = pl.BlockSpec(memory_space=pl.ANY)
VMEM = pl.BlockSpec(memory_space=pltpu.VMEM)
DMA = pltpu.SemaphoreType.DMA
SMALL = 8


def place():
    c, b = lax.axis_index("chan"), lax.axis_index("batch")
    nz, nx = lax.axis_size("chan") // 2, lax.axis_size("batch") // 2
    return (c // 2, lax.rem(c, 2), b // 2, lax.rem(b, 2)), (nz, 2, nx, 2)


def at(z, y, x, core):
    return {"chan": z * 2 + y, "batch": x * 2 + core}


def turned(index, size):
    return [lax.rem(index + k, size) for k in range(1, size)]


def greet(peers):
    barrier = pltpu.get_barrier_semaphore()
    for peer in peers:
        pl.semaphore_signal(barrier, inc=1, device_id=peer, device_id_type=MESH)
    pl.semaphore_wait(barrier, len(peers))


class Copies:
    def __init__(self, send, recv):
        self.send, self.recv, self.used = send, recv, 0

    def start(self, source, target, peer):
        copy = pltpu.make_async_remote_copy(
            source, target, self.send.at[self.used], self.recv.at[self.used],
            device_id=peer, device_id_type=MESH,
        )
        self.used += 1
        copy.start()
        return copy


def small_sum_kernel(own, total, held, send, recv):
    (z, y, x, core), (nz, ny, nx, nc) = place()
    peers = [
        at(lax.rem(z + i, nz), lax.rem(y + j, ny), lax.rem(x + k, nx), lax.rem(core + m, nc))
        for i in range(nz) for j in range(ny) for k in range(nx) for m in range(nc) if i + j + k + m
    ]
    greet(peers)
    copies = Copies(send, recv)
    started = [copies.start(own, held.at[k + 1], peer) for k, peer in enumerate(peers)]
    held[0] = own[...]
    for copy in started:
        copy.wait()
    total[...] = jnp.sum(held[...], axis=0)


def small_sum(rows, cid):
    n = lax.axis_size("chan") * lax.axis_size("batch")
    return pl.pallas_call(
        small_sum_kernel,
        out_shape=jax.ShapeDtypeStruct(rows.shape, jnp.float32),
        in_specs=[VMEM],
        out_specs=VMEM,
        scratch_shapes=[pltpu.VMEM((n,) + rows.shape, jnp.float32), DMA((n - 1,)), DMA((n - 1,))],
        compiler_params=pltpu.CompilerParams(collective_id=cid, has_side_effects=True),
        name="small_sum",
    )(rows)


def chan_sum_kernel(own, total, held, send, recv):
    c, n = lax.axis_index("chan"), lax.axis_size("chan")
    peers = [{"chan": other} for other in turned(c, n)]
    greet(peers)
    copies = Copies(send, recv)
    started = [copies.start(own, held.at[k + 1], peer) for k, peer in enumerate(peers)]
    held[0] = own[...]
    for copy in started:
        copy.wait()
    total[...] = jnp.sum(held[...], axis=0)


def chan_sum(rows, cid):
    n = lax.axis_size("chan")
    return pl.pallas_call(
        chan_sum_kernel,
        out_shape=jax.ShapeDtypeStruct(rows.shape, jnp.float32),
        in_specs=[VMEM],
        out_specs=VMEM,
        scratch_shapes=[pltpu.VMEM((n,) + rows.shape, jnp.float32), DMA((n - 1,)), DMA((n - 1,))],
        compiler_params=pltpu.CompilerParams(collective_id=cid, has_side_effects=True),
        name="chan_sum",
    )(rows)


def spread_kernel(images, weights, norms, images_out, weights_out, norms_out, send, recv, local):
    (z, y, x, core), (nz, ny, nx, nc) = place()
    c, n = lax.axis_index("chan"), lax.axis_size("chan")
    others = turned(c, n)
    greet([{"chan": k} for k in others] + [at(z, y, k, core) for k in turned(x, nx)] + [at(z, y, x, 1 - core)])
    copies = Copies(send, recv)
    quarter = pltpu.make_async_copy(weights.at[x, core], weights_out.at[z, y, x, core], local.at[0])
    quarter.start()
    along_z = [
        copies.start(weights.at[x, core], weights_out.at[z, y, x, core], at(k, y, x, core)) for k in turned(z, nz)
    ]
    rest = [copies.start(norms, norms_out.at[c], {"chan": k}) for k in others]
    rest += [copies.start(images.at[k], images_out.at[c], {"chan": k}) for k in others]
    own = pltpu.make_async_copy(images.at[c], images_out.at[c], local.at[1])
    own.start()
    own_norms = pltpu.make_async_copy(norms, norms_out.at[c], local.at[2])
    own_norms.start()
    quarter.wait()
    for copy in along_z:
        copy.wait()
    part = weights_out.at[:, y, x, core]
    copies.start(part, part, at(z, 1 - y, x, core)).wait()
    part = weights_out.at[:, :, x, core]
    along_x = [copies.start(part, part, at(z, y, k, core)) for k in turned(x, nx)]
    for copy in along_x:
        copy.wait()
    part = weights_out.at[:, :, :, core]
    copies.start(part, part, at(z, y, x, 1 - core)).wait()
    own.wait()
    own_norms.wait()
    for copy in rest:
        copy.wait()


def spread(images, weights, norms):
    nz, nx = lax.axis_size("chan") // 2, lax.axis_size("batch") // 2
    n = lax.axis_size("chan")
    count = (nz - 1) + 2 * (n - 1) + 1 + (nx - 1) + 1
    rows, columns = weights.shape[0] // (2 * nx), weights.shape[1]
    images_out, weights_out, norms_out = pl.pallas_call(
        spread_kernel,
        out_shape=(
            jax.ShapeDtypeStruct(images.shape, images.dtype),
            jax.ShapeDtypeStruct((nz, 2, nx, 2, rows, columns), weights.dtype),
            jax.ShapeDtypeStruct((n,) + norms.shape, norms.dtype),
        ),
        in_specs=[ANY] * 3,
        out_specs=(ANY,) * 3,
        scratch_shapes=[DMA((count,)), DMA((count,)), DMA((3,))],
        compiler_params=pltpu.CompilerParams(collective_id=0, has_side_effects=True),
        name="spread",
    )(images, weights.reshape(nx, 2, rows, columns), norms)
    return images_out, weights_out.reshape(n * weights.shape[0], columns), norms_out


def settle_kernel(wire, spatial, reduce, head, mask, full, own, sums_a, sums_b, core_a, core_b, x_a, x_b, y_a, y_b,
                  z_a, z_b, sx_a, sx_b, sy_a, sy_b, sz_a, sz_b, final, final_low, send, recv, local):
    (z, y, x, core), (nz, ny, nx, nc) = place()
    greet([at(k, y, x, core) for k in turned(z, nz)] + [at(z, 1 - y, x, core)]
          + [at(z, y, k, core) for k in turned(x, nx)] + [at(z, y, x, 1 - core)])
    copies = Copies(send, recv)
    half = sums_a.shape[-1]
    tail = spatial.shape[-1] - half
    mate, mate_y = at(z, y, x, 1 - core), at(z, 1 - y, x, core)
    mates_x, mates_z = turned(x, nx), turned(z, nz)
    groups = [(i, j, k) for i in range(nz) for j in range(ny) for k in range(nx)]
    pieces_a = [(spatial.at[:, :, :, :, :, pl.ds(0, half)], 0, half)]
    pieces_b = [(spatial.at[:, :, :, :, :, pl.ds(half, tail)], 0, tail), (reduce, tail, reduce.shape[-1]),
                (head, tail + reduce.shape[-1], head.shape[-1])]

    def begin(pieces, sums, landing, sem):
        remote, kept = [], []
        for source, start, size in pieces:
            columns = pl.ds(start, size)
            remote.append(copies.start(source.at[:, :, :, 1 - core], landing.at[:, :, :, :, columns], mate))
            copy = pltpu.make_async_copy(source.at[:, :, :, core], sums.at[:, :, :, :, columns], local.at[sem + len(kept)])
            copy.start()
            kept.append(copy)
        return remote + kept

    def ship(source, staged, landing, peer):
        if staged.dtype == jnp.float32:
            return copies.start(source, landing, peer)
        for i in range(staged.shape[0]):
            staged[i] = source[i].astype(staged.dtype)
        return copies.start(staged, landing, peer)

    def add(sums, landing):
        for i in range(landing.shape[0]):
            sums[i] += landing[i].astype(jnp.float32)

    first_a = begin(pieces_a, sums_a, core_a, 0)
    first_b = begin(pieces_b, sums_b, core_b, len(pieces_a))
    for first, sums, landing in ((first_a, sums_a, core_a), (first_b, sums_b, core_b)):
        for copy in first:
            copy.wait()
        for i, j, k in groups:
            sums[i, j, k] += landing[i, j, k]
        if sums is sums_a:
            going_a = []
            for t, k in enumerate(mates_x):
                for j in range(ny):
                    going_a.append(ship(sums.at[:, j, k], sx_a.at[t, j], x_a.at[t, j], at(z, y, k, core)))
        else:
            going_b = [ship(sums.at[:, 1 - y, k], sy_b.at[k], y_b.at[k], mate_y) for k in range(nx)]
    for copy in going_a:
        copy.wait()
    for t in range(nx - 1):
        for j in range(ny):
            add(sums_a.at[:, j, x], x_a.at[t, j])
    going_a = [ship(sums_a.at[:, 1 - y, x], sy_a, y_a, mate_y)]
    for copy in going_b:
        copy.wait()
    for k in range(nx):
        add(sums_b.at[:, y, k], y_b.at[k])
    going_b = [ship(sums_b.at[:, y, k], sx_b.at[t], x_b.at[t], at(z, y, k, core)) for t, k in enumerate(mates_x)]
    for copy in going_a:
        copy.wait()
    add(sums_a.at[:, y, x], y_a)
    going_a = [ship(sums_a.at[pl.ds(k, 1), y, x], sz_a.at[pl.ds(t, 1)], z_a.at[pl.ds(t, 1)], at(k, y, x, core))
               for t, k in enumerate(mates_z)]
    for copy in going_b:
        copy.wait()
    for t in range(nx - 1):
        add(sums_b.at[:, y, x], x_b.at[t])
    going_b = [ship(sums_b.at[pl.ds(k, 1), y, x], sz_b.at[pl.ds(t, 1)], z_b.at[pl.ds(t, 1)], at(k, y, x, core))
               for t, k in enumerate(mates_z)]
    for going, sums, landing, start in ((going_a, sums_a, z_a, 0), (going_b, sums_b, z_b, half)):
        for copy in going:
            copy.wait()
        value = sums[z, y, x]
        for t in range(nz - 1):
            value = value + landing[t].astype(jnp.float32)
        columns = pl.ds(start, half)
        final[:, columns] = value * mask[:, columns]

    wide = full.shape[-1]
    final_low[...] = final[:, :wide].astype(final_low.dtype)
    keep = pltpu.make_async_copy(final_low, full.at[z, y, x, core], local.at[4])
    keep.start()
    keep_own = pltpu.make_async_copy(final, own.at[x, core], local.at[5])
    keep_own.start()
    up = [copies.start(final_low, full.at[z, y, x, core], at(k, y, x, core)) for k in mates_z]
    rows_x = [copies.start(final, own.at[x, core], at(z, y, k, core)) for k in mates_x]
    keep.wait()
    for copy in up:
        copy.wait()
    left, right = pl.ds(0, wide // 2), pl.ds(wide // 2, wide // 2)
    part = full.at[:, y, x, core, :, left]
    going_a = [copies.start(part, part, at(z, y, k, core)) for k in mates_x]
    part = full.at[:, y, x, core, :, right]
    going_b = [copies.start(part, part, mate_y)]
    keep_own.wait()
    for copy in rows_x:
        copy.wait()
    part = own.at[:, core]
    rows_core = copies.start(part, part, mate)
    for copy in going_a:
        copy.wait()
    part = full.at[:, y, :, core, :, left]
    going_a = [copies.start(part, part, mate_y)]
    for copy in going_b:
        copy.wait()
    part = full.at[:, :, x, core, :, right]
    going_b = [copies.start(part, part, at(z, y, k, core)) for k in mates_x]
    for copy in going_a:
        copy.wait()
    part = full.at[:, :, :, core, :, left]
    last = [copies.start(part, part, mate)]
    for copy in going_b:
        copy.wait()
    part = full.at[:, :, :, core, :, right]
    last += [copies.start(part, part, mate), rows_core]
    for copy in last:
        copy.wait()


def settle(spatial, reduce, head, mask, wire):
    nz, nx = lax.axis_size("chan") // 2, lax.axis_size("batch") // 2
    width = spatial.shape[0]
    rows = width // (4 * nz * nx)
    total = spatial.shape[1] + reduce.shape[1] + head.shape[1]
    wide, half = spatial.shape[1] + reduce.shape[1], total // 2
    split = lambda a: a.reshape(nz, 2, nx, 2, rows, a.shape[1])
    f32 = jnp.float32
    big = pltpu.VMEM((nz, 2, nx, rows, half), f32)
    shapes = [(nx - 1, 2, nz, rows, half), (nx - 1, nz, rows, half), (nz, rows, half), (nx, nz, rows, half),
              (nz - 1, rows, half), (nz - 1, rows, half)]
    landing = [pltpu.VMEM(s, wire) for s in shapes]
    staging = [pltpu.VMEM(s if wire != f32 else s[:-2] + (8, 128), wire) for s in shapes]
    count = 4 + 2 * (nx - 1) + nx + 1 + (nx - 1) + 2 * (nz - 1) + (nz - 1) + (nx - 1) + 2 * nx + 1 + 2
    full, own = pl.pallas_call(
        functools.partial(settle_kernel, wire),
        out_shape=(
            jax.ShapeDtypeStruct((nz, 2, nx, 2, rows, wide), jnp.bfloat16),
            jax.ShapeDtypeStruct((nx, 2, rows, total), f32),
        ),
        in_specs=[ANY, ANY, ANY, VMEM],
        out_specs=(ANY, ANY),
        scratch_shapes=[big, big, big, big] + landing + staging
        + [pltpu.VMEM((rows, total), f32), pltpu.VMEM((rows, wide), jnp.bfloat16), DMA((count,)), DMA((count,)), DMA((6,))],
        compiler_params=pltpu.CompilerParams(collective_id=1, has_side_effects=True, vmem_limit_bytes=56 << 20),
        name="settle",
    )(split(spatial), split(reduce), split(head), mask)
    return full.reshape(width, wide), own.reshape(2 * nx * rows, total)


def silu_slope(pre):
    sigma = jax.nn.sigmoid(pre)
    return sigma * (1.0 + pre * (1.0 - sigma))


def adam_step(param, grad, first, second, rate, decay):
    first = 0.9 * first + 0.1 * grad
    second = 0.999 * second + 0.001 * grad * grad
    mhat = first / (1.0 - 0.9**STEP)
    vhat = second / (1.0 - 0.999**STEP)
    return (param - rate * (mhat / (jnp.sqrt(vhat) + 1e-08) + decay * param), first, second)


def own_part(array, axis, name="chan"):
    size = array.shape[axis] // lax.axis_size(name)
    return lax.dynamic_slice_in_dim(array, lax.axis_index(name) * size, size, axis)


def stacked(rows):
    width = rows[0].shape[0]
    rows = [jnp.pad(r, (0, width - r.shape[0])) for r in rows]
    rows += [jnp.zeros((width,), jnp.float32)] * (SMALL - len(rows))
    return jnp.stack(rows)


def two_parts(array):
    high = array.astype(jnp.bfloat16)
    return high, (array - high.astype(jnp.float32)).astype(jnp.bfloat16)


def product(spec, left, right):
    return jnp.einsum(spec, left, right, preferred_element_type=jnp.float32)


def conv_grid(grid, taps, spec):
    return lax.conv_general_dilated(
        grid, taps, (1, 1), ((1, 1), (1, 1)), dimension_numbers=spec, preferred_element_type=jnp.float32
    )


def body(
    images,
    pixel_mask,
    labels,
    reduce_weight,
    reduce_mask,
    spatial_weight,
    spatial_mask,
    head_weight,
    head_bias,
    norm_params,
    left_stats,
    right_stats,
    left_root,
    input_side_roots,
    head_first,
    head_second,
    bias_first,
    bias_second,
    norm_first,
    norm_second,
):
    n = lax.axis_size("chan")
    pixels, channels = images.shape[1:]
    side = SIDE
    rows_out, c_in = reduce_weight.shape
    width = left_stats.shape[2]
    classes = head_weight.shape[1]
    padded = 1024
    slots = images.shape[0] // n
    low = jnp.bfloat16
    f32 = jnp.float32
    reduce_float = reduce_mask.astype(f32)
    spatial_float = spatial_mask.astype(f32)

    by_pixel = images.reshape(n, slots, pixels, channels).transpose(0, 2, 1, 3)
    weights = jnp.concatenate(
        [(spatial_weight * spatial_float).astype(low), (reduce_weight * reduce_float).astype(low),
         jnp.pad(head_weight.astype(low), ((0, 0), (0, padded - classes)))], axis=1)
    norms = jnp.pad(norm_params, ((0, 4), (0, 128 - rows_out)))
    own_images, weights_full, norms_full = spread(by_pixel, weights, norms)
    taps = weights_full[:, : 9 * width].reshape(width, 3, 3, width)
    reduce_low = weights_full[:, 9 * width : 9 * width + c_in]
    head_low = weights_full[:, 9 * width + c_in : 9 * width + c_in + classes]
    norm_full = norms_full[:, :4, :rows_out].transpose(1, 0, 2).reshape(4, width)

    mask_own = own_part(pixel_mask, 0).astype(f32)
    valid = mask_own.T[:, :, None]
    own_labels = own_part(labels, 0)
    filled = jnp.sum(mask_own, axis=1)
    divisor = jnp.maximum(filled, 1.0)
    used = (filled > 0.0).astype(f32)

    first_pre = product("npsc,onc->pso", own_images, reduce_low.reshape(width, n, channels))
    roots_low, _ = lax.optimization_barrier((input_side_roots.astype(low), first_pre[0, 0, 0]))
    right_full = lax.all_gather(roots_low, "chan", axis=1, tiled=True)

    def sums_of(value):
        return jnp.sum(value * valid, axis=(0, 1)), jnp.sum(value * value * valid, axis=(0, 1))

    def forward(pre_norm, sums, count, gain, shift):
        mean = sums[0] / count
        scale = lax.rsqrt(sums[1] / count - mean * mean + EPS)
        normed = (pre_norm - mean) * scale
        pre = gain * normed + shift
        return normed, pre, scale

    stats = small_sum(stacked([*sums_of(first_pre), jnp.full((width,), jnp.sum(valid))]), 2)
    count = stats[2, 0]
    normed_one, pre_one, scale_one = forward(first_pre, stats, count, norm_full[0], norm_full[1])
    hidden = (jax.nn.silu(pre_one) * valid).astype(low).reshape(side, side, slots, width)
    second_pre = conv_grid(hidden, taps, ("HWNC", "OHWI", "HWNC")).reshape(pixels, slots, width)
    stats = small_sum(stacked([*sums_of(second_pre)]), 3)
    normed_two, pre_two, scale_two = forward(second_pre, stats, count, norm_full[2], norm_full[3])
    second_act = jax.nn.silu(pre_two) * valid
    pooled = (jnp.sum(second_act, axis=0) / divisor[:, None]).astype(low)
    logits = jnp.dot(pooled, head_low, preferred_element_type=f32) + head_bias
    onehot = (jnp.arange(classes)[None, :] == own_labels[:, None]).astype(f32)
    log_total = jax.nn.logsumexp(logits, axis=1)
    picked = jnp.sum(onehot * logits, axis=1)
    loss_local = jnp.sum(used * (log_total - picked))
    d_logits = (used[:, None] * (jnp.exp(logits - log_total[:, None]) - onehot) / SLOTS_DEV).astype(low)
    head_local = product("so,sc->oc", pooled, d_logits)
    bias_local = jnp.sum(d_logits.astype(f32), axis=0)
    d_pooled = product("sc,oc->so", d_logits, head_low)
    d_act = jnp.broadcast_to((d_pooled / divisor[:, None])[None], second_act.shape)

    def backward(d_act, normed, pre, scale, gain, cid, extra):
        d_pre = d_act * valid * silu_slope(pre)
        sums = small_sum(
            stacked([jnp.sum(d_pre, axis=(0, 1)), jnp.sum(d_pre * normed, axis=(0, 1))] + extra), cid)
        d_z = gain * scale / count * (count * d_pre - sums[0] - normed * sums[1]) * valid
        return d_z.astype(low), sums

    half = padded // 2
    bias_padded = jnp.pad(bias_local, (0, padded - classes))
    misc = jnp.zeros((width,), f32).at[0].set(loss_local).at[1].set(jnp.sum(used))
    d_second, sums_two = backward(d_act, normed_two, pre_two, scale_two, norm_full[2], 4,
                                  [bias_padded[:half], bias_padded[half:], misc])
    d_second = d_second.reshape(side, side, slots, width)
    spatial_local = lax.conv_general_dilated(
        hidden, d_second, (1, 1), ((1, 1), (1, 1)), dimension_numbers=("HWCN", "HWIO", "HWNC"),
        preferred_element_type=f32,
    )
    spatial_local = spatial_local.transpose(3, 0, 1, 2).reshape(width, 9 * width)
    d_hidden = conv_grid(
        d_second, taps[:, ::-1, ::-1, :], ("HWNC", "IHWO", "HWNC")
    ).reshape(pixels, slots, width)
    d_first, sums_one = backward(d_hidden, normed_one, pre_one, scale_one, norm_full[0], 5, [])
    reduce_local = product("npsc,pso->onc", own_images, d_first).reshape(width, c_in)

    mask_rows = jnp.concatenate([spatial_float, reduce_float, jnp.ones((rows_out, padded), f32)], axis=1)
    full, own = settle(spatial_local, reduce_local, jnp.pad(head_local, ((0, 0), (0, padded - classes))),
                       own_part(mask_rows, 0, "batch"), jnp.float32)
    spatial_grad = own[:, : 9 * width]
    reduce_grad = own[:, 9 * width : 9 * width + c_in]
    head_grad = own[:, 9 * width + c_in : 9 * width + c_in + classes]
    loss_sum, slot_count = sums_two[4, 0], sums_two[4, 1]
    bias_grad = jnp.concatenate([sums_two[2], sums_two[3]])[:classes]
    norm_gain_gradient = own_part(jnp.stack([sums_one[1], sums_one[0], sums_two[1], sums_two[0]]), 1)

    tiles_one = c_in // width
    blocks_of = lambda a: a.reshape(a.shape[0], -1, width).transpose(1, 0, 2)
    in_order = lambda a: jnp.concatenate([a[9:], a[:9]], axis=0)
    blocks = in_order(blocks_of(own[:, : 9 * width + c_in])).astype(low)
    blocks_full = in_order(blocks_of(full))
    left_new = 0.95 * left_stats + product("tak,tbk->tab", blocks, blocks_full)
    right_new = 0.95 * right_stats + product("tki,tkb->tib", own_part(blocks_full, 2), blocks_full)
    left_high, left_rest = two_parts(left_root)
    inner = product("tak,tkb->tab", left_high, blocks_full) + product("tak,tkb->tab", left_rest, blocks_full)
    inner_high, inner_rest = two_parts(inner)
    outer = product("tak,tkb->tab", inner_high, right_full) + product("tak,tkb->tab", inner_rest, right_full)
    squares = jnp.pad(jnp.sum(outer * outer, axis=(1, 2))[:, None] * jnp.ones((1, 128), f32), ((0, 3), (0, 0)))
    squares = chan_sum(squares, 6)[: 9 + tiles_one, 0]
    step = outer / jnp.sqrt(squares / (width * width) + 1e-06)[:, None, None]
    step_one = step[:tiles_one].transpose(1, 0, 2).reshape(rows_out, c_in)
    step_two = step[tiles_one:].transpose(1, 0, 2).reshape(rows_out, 9 * width)
    reduce_new = reduce_weight - 0.02 * reduce_float * (step_one + 0.1 * reduce_weight)
    spatial_new = spatial_weight - 0.02 * spatial_float * (step_two + 0.1 * spatial_weight)
    head_new, head_first_new, head_second_new = adam_step(head_weight, head_grad, head_first, head_second, 0.04, 0.1)
    bias_new, bias_first_new, bias_second_new = adam_step(head_bias, bias_grad, bias_first, bias_second, 0.1, 0.0)
    norm_new, norm_first_new, norm_second_new = adam_step(
        norm_params, norm_gain_gradient, norm_first, norm_second, 0.1, 0.0)
    return (
        loss_sum,
        slot_count,
        reduce_grad,
        spatial_grad,
        reduce_new,
        spatial_new,
        left_new,
        right_new,
        head_new,
        head_first_new,
        head_second_new,
        bias_new,
        bias_first_new,
        bias_second_new,
        norm_new,
        norm_first_new,
        norm_second_new,
    )


FULL_PRECISION = lax.Precision.HIGHEST
BOTH = ("chan", "batch")


def plain_norm_forward(pre_norm, gain, shift, valid):
    first_sum = jnp.sum(pre_norm * valid, axis=(0, 1))
    second_sum = jnp.sum(pre_norm * pre_norm * valid, axis=(0, 1))
    first_sum, second_sum, count = lax.psum((first_sum, second_sum, jnp.sum(valid)), BOTH)
    mean = first_sum / count
    scale = lax.rsqrt(second_sum / count - mean * mean + EPS)
    normed = (pre_norm - mean) * scale
    pre = gain * normed + shift
    return (jax.nn.silu(pre) * valid, (normed, pre, scale, count))


def plain_norm_backward(grad_act, kept, gain, valid):
    normed, pre, scale, count = kept
    d_pre = grad_act * valid * silu_slope(pre)
    shift_gradient, gain_grad = lax.psum(
        (jnp.sum(d_pre, axis=(0, 1)), jnp.sum(d_pre * normed, axis=(0, 1))), BOTH
    )
    d_input = gain * scale / count * (count * d_pre - shift_gradient - normed * gain_grad) * valid
    return (d_input, gain_grad, shift_gradient)


def plain_own_part(array, parts, axis=0):
    size = array.shape[axis] // parts
    return lax.dynamic_slice_in_dim(array, lax.axis_index("chan") * size, size, axis)


def plain_body(
    images,
    pixel_mask,
    labels,
    reduce_weight,
    reduce_mask,
    spatial_weight,
    spatial_mask,
    head_weight,
    head_bias,
    norm_params,
    left_stats,
    right_stats,
    left_root,
    input_side_roots,
    head_first,
    head_second,
    bias_first,
    bias_second,
    norm_first,
    norm_second,
):
    parts = lax.axis_size("chan")
    pixels = images.shape[1]
    side = SIDE
    rows_out = reduce_weight.shape[0]
    width = left_stats.shape[2]
    classes = head_weight.shape[1]
    own_images = lax.all_to_all(images, "chan", 0, 2, tiled=True)
    slots = own_images.shape[0]
    reduce_float = reduce_mask.astype(jnp.float32)
    spatial_float = spatial_mask.astype(jnp.float32)
    gather = lambda a, axis: lax.all_gather(a, "chan", axis=axis, tiled=True)
    reduce_low = gather((reduce_weight * reduce_float).astype(jnp.bfloat16), 0)
    spatial_low = gather((spatial_weight * spatial_float).astype(jnp.bfloat16), 0)
    head_low = gather(head_weight.astype(jnp.bfloat16), 0)
    norm_full = gather(norm_params, 1)
    right_factor_full = gather(input_side_roots, 1)
    valid = plain_own_part(pixel_mask, parts).astype(jnp.float32)[:, :, None]
    own_labels = plain_own_part(labels, parts)
    filled = jnp.sum(valid[:, :, 0], axis=1)
    divisor = jnp.maximum(filled, 1.0)
    used = (filled > 0.0).astype(jnp.float32)
    taps = spatial_low.reshape(width, 3, 3, width)
    first_pre = jnp.einsum("spc,oc->spo", own_images, reduce_low, preferred_element_type=jnp.float32)
    first_act, first_kept = plain_norm_forward(first_pre, norm_full[0], norm_full[1], valid)
    hidden = first_act.astype(jnp.bfloat16).reshape(slots, side, side, width)
    second_pre = conv_grid(hidden, taps, ("NHWC", "OHWI", "NHWC")).reshape(slots, pixels, width)
    second_act, second_kept = plain_norm_forward(second_pre, norm_full[2], norm_full[3], valid)
    pooled = (jnp.sum(second_act, axis=1) / divisor[:, None]).astype(jnp.bfloat16)
    logits = jnp.dot(pooled, head_low, preferred_element_type=jnp.float32) + head_bias
    onehot = (jnp.arange(classes)[None, :] == own_labels[:, None]).astype(jnp.float32)
    log_total = jax.nn.logsumexp(logits, axis=1)
    picked = jnp.sum(onehot * logits, axis=1)
    loss_local = jnp.sum(used * (log_total - picked))
    d_logits = (used[:, None] * (jnp.exp(logits - log_total[:, None]) - onehot) / SLOTS_DEV).astype(
        jnp.bfloat16
    )
    head_grad = jnp.einsum("so,sc->oc", pooled, d_logits, preferred_element_type=jnp.float32)
    bias_grad = jnp.sum(d_logits.astype(jnp.float32), axis=0)
    d_pooled = jnp.einsum("sc,oc->so", d_logits, head_low, preferred_element_type=jnp.float32)
    d_act = jnp.broadcast_to((d_pooled / divisor[:, None])[:, None, :], second_act.shape)
    d_second, gain_two, shift_two = plain_norm_backward(d_act, second_kept, norm_full[2], valid)
    d_second = d_second.astype(jnp.bfloat16).reshape(slots, side, side, width)
    spatial_local = lax.conv_general_dilated(
        hidden, d_second, (1, 1), ((1, 1), (1, 1)), dimension_numbers=("CHWN", "IHWO", "NHWC"),
        preferred_element_type=jnp.float32,
    )
    spatial_local = spatial_local.transpose(3, 1, 2, 0).reshape(width, 9 * width)
    d_hidden = conv_grid(
        d_second, taps[:, ::-1, ::-1, :], ("NHWC", "IHWO", "NHWC")
    ).reshape(slots, pixels, width)
    d_first, gain_one, shift_one = plain_norm_backward(d_hidden, first_kept, norm_full[0], valid)
    d_first = d_first.astype(jnp.bfloat16)
    reduce_local = jnp.einsum("spc,spo->oc", own_images, d_first, preferred_element_type=jnp.float32)
    scatter = lambda a: lax.psum_scatter(a, "chan", scatter_dimension=0, tiled=True)
    reduce_grad, spatial_grad, head_grad = scatter(reduce_local), scatter(spatial_local), scatter(head_grad)
    reduce_grad, spatial_grad, head_grad = lax.psum((reduce_grad, spatial_grad, head_grad), "batch")
    reduce_grad = reduce_grad * reduce_float
    spatial_grad = spatial_grad * spatial_float
    bias_grad, loss_sum, slot_count = lax.psum((bias_grad, loss_local, jnp.sum(used)), BOTH)
    norm_gain_gradient = plain_own_part(jnp.stack([gain_one, shift_one, gain_two, shift_two], axis=0), parts, 1)
    tiles_one = reduce_weight.shape[1] // width
    blocks = jnp.concatenate(
        [
            reduce_grad.reshape(rows_out, tiles_one, width).transpose(1, 0, 2),
            spatial_grad.reshape(rows_out, 9, width).transpose(1, 0, 2),
        ],
        axis=0,
    )
    blocks_full = gather(blocks, 1)
    left_new = 0.95 * left_stats + jnp.einsum(
        "tak,tbk->tab", blocks, blocks_full, precision=FULL_PRECISION
    )
    own_columns = plain_own_part(blocks_full, parts, 2)
    right_new = 0.95 * right_stats + jnp.einsum(
        "tki,tkb->tib", own_columns, blocks_full, precision=FULL_PRECISION
    )
    matrix_product = jnp.einsum("tak,tkb->tab", left_root, blocks_full, precision=FULL_PRECISION)
    matrix_product = jnp.einsum(
        "ghk,gkl->ghl", matrix_product, right_factor_full, precision=FULL_PRECISION
    )
    squares = lax.psum(jnp.sum(matrix_product * matrix_product, axis=(1, 2)), "chan")
    step = matrix_product / jnp.sqrt(squares / (width * width) + 1e-06)[:, None, None]
    step_one = step[:tiles_one].transpose(1, 0, 2).reshape(rows_out, tiles_one * width)
    step_two = step[tiles_one:].transpose(1, 0, 2).reshape(rows_out, 9 * width)
    reduce_new = reduce_weight - 0.02 * reduce_float * (step_one + 0.1 * reduce_weight)
    spatial_new = spatial_weight - 0.02 * spatial_float * (step_two + 0.1 * spatial_weight)
    head_new, head_first_new, head_second_new = adam_step(
        head_weight, head_grad, head_first, head_second, 0.04, 0.1
    )
    bias_new, bias_first_new, bias_second_new = adam_step(
        head_bias, bias_grad, bias_first, bias_second, 0.1, 0.0
    )
    norm_new, norm_first_new, norm_second_new = adam_step(
        norm_params, norm_gain_gradient, norm_first, norm_second, 0.1, 0.0
    )
    return (
        loss_sum,
        slot_count,
        reduce_grad,
        spatial_grad,
        reduce_new,
        spatial_new,
        left_new,
        right_new,
        head_new,
        head_first_new,
        head_second_new,
        bias_new,
        bias_first_new,
        bias_second_new,
        norm_new,
        norm_first_new,
        norm_second_new,
    )


def solution(mesh):
    in_specs = (
        P("batch", None, "chan"),
        P("batch", None),
        P("batch"),
        P("chan", None),
        P("chan", None),
        P("chan", None),
        P("chan", None),
        P("chan", None),
        P(),
        P(None, "chan"),
        P(None, "chan", None),
        P(None, "chan", None),
        P(None, "chan", None),
        P(None, "chan", None),
        P("chan", None),
        P("chan", None),
        P(),
        P(),
        P(None, "chan"),
        P(None, "chan"),
    )
    out_specs = (
        P(),
        P(),
        P("chan", None),
        P("chan", None),
        P("chan", None),
        P("chan", None),
        P(None, "chan", None),
        P(None, "chan", None),
        P("chan", None),
        P("chan", None),
        P("chan", None),
        P(),
        P(),
        P(),
        P(None, "chan"),
        P(None, "chan"),
        P(None, "chan"),
    )
    chan, batch = mesh.shape["chan"], mesh.shape["batch"]
    fits = chan % 2 == 0 and batch % 2 == 0 and WIDTH % (16 * chan * batch) == 0 and SLOTS_DEV % (16 * chan) == 0
    return jax.shard_map(body if fits else plain_body, mesh=mesh, in_specs=in_specs, out_specs=out_specs, check_vma=False)
```

time: 3610 us -> 853 us (0.24)
  waiting for transfers between devices: 2790 us -> 0.02 us
  Pallas kernels: 0 us -> 576 us
  matrix products: 519 us -> 94.2 us
  local copies, waits for them, and re-layouts: 176 us -> 105 us
  blocking collectives: 46.8 us -> 0 us
    all_gather x4 -> x1, waiting for transfers between devices: 2190 us -> 0.01 us  [body(): right_full = lax.all_gather(roots_low, 'chan', axis=1, tiled=True)]
    pallas_call x0 -> x7, Pallas kernels: none -> 576 us  [the longest x1 237 us: spread(): pl.pallas_call(spread_kernel, out_shape=(jax.ShapeDtypeStruct(images.shap...]
    reduce_scatter x1 -> x0, waiting for transfers between devices: 472 us -> none  [body(): lax.psum_scatter(hidden_part, 'chan', scatter_dimension=3, tiled=True)]
    dot_general x28 -> x10, matrix products: 304 us -> 45.5 us  [the longest x9 43.8 us: product(): return jnp.einsum(spec, left, right, preferred_element_type=jnp.float32)]
    slice x8 -> x0, matrix products: 215 us -> none  [shift_grid(): return padded[:, 1 + dy:1 + dy + side, 1 + dx:1 + dx + side, :]]
    psum x2 -> x0, waiting for transfers between devices: 136 us -> none  [the longest x1 87.8 us: body(): lax.psum(jnp.dot(pooled, head_low, preferred_element_type=jnp.float32), '...]
    slice x2 -> x15, local copies, waits for them, and re-layouts: 93.2 us -> 17.5 us  [the longest x1 4.73 us: body(): taps = weights_full[:, :9 * width].reshape(width, 3, 3, width)]
    psum x5 -> x0, blocking collectives: 46.8 us -> none  [the longest x1 18.6 us: body(): lax.psum(jnp.sum(matrix_product * matrix_product, axis=(1, 2)), 'chan')]
  transfers between devices with their start and end apart: 7 -> 1, of which waited for: 7 -> 0; matrix products, arithmetic and copies ran while one was open for 7% -> 28% of each run, Pallas kernels for 0% -> 67%
where the time goes in v1:
time: 853 us; the launch traced here: 841 us
  Pallas kernels  576 us (68%)
  local copies, waits for them, and re-layouts  105 us (12%)
  matrix products  94.2 us (11%)
  other arithmetic  50.2 us (6%)
  between operations  15.2 us (2%)
    pallas_call x1, Pallas kernels, spread(): pl.pallas_call(spread_kernel, out_shape=(jax.ShapeDtypeStruct(images.shap...  237 us
    pallas_call x1, Pallas kernels, settle(): pl.pallas_call(functools.partial(settle_kernel, wire), out_shape=(jax.Sha...  177 us
    pallas_call x4, Pallas kernels, small_sum(): pl.pallas_call(small_sum_kernel, out_shape=jax.ShapeDtypeStruct(rows.shap...  147 us
    dot_general x9, matrix products, product(): return jnp.einsum(spec, left, right, preferred_element_type=jnp.float32)  43.8 us
    conv_general_dilated x2, matrix products, conv_grid(): lax.conv_general_dilated(grid, taps, (1, 1), ((1, 1), (1, 1)), dimension_...  31.3 us
    another operation x2, local copies, waits for them, and re-layouts, settle(): split = lambda a: a.reshape(nz, 2, nx, 2, rows, a.shape[1])  21 us
    another operation x2, local copies, waits for them, and re-layouts, body(): blocks_of = lambda a: a.reshape(a.shape[0], -1, width).transpose(1, 0, 2)  20 us
  transfers between devices with their start and end apart: 1, of which 0 were waited for; matrix products, arithmetic and copies ran while one was open for 28% of the time, Pallas kernels for 67%

profile of v1, /device:TPU:0, one launch (start us, length us, event | category | flops | bytes accessed | tf_op | source)
XLA Modules:
  0.0 841.0 jit_solution(14683277373987136124)
XLA Ops:
  12.8 8.3 copy.80
  24.0 236.6 %spread.1 = (bf16[8,49,48,256]{3,2,1,0:T(8,128)(2,1)}, bf16[4,2,2,2,16,7680]{5,4,3,2,1,0:T(8,128)(2,1)}, f32[8,8,128]{2,1,0:T(8,128)}) custom-call(bf16[8,49,48,256]{3,2,1,0:T(8,128)(2,1)} %bitcast.123, bf16[2,2,16,7680]{3,2,1,0:T(8,128)(2,1)} %bitcast.139, f32[8,128]{1,0:T(8,128)} %pad.28.norms), custom_call_target="tpu_custom_call" | custom-call | tf_op jit(solution)/shard_map/spread/pallas_call | solution.py:150
  262.4 4.7 slice.177
  267.6 2.5 copy.71
  270.9 10.6 %fusion.3 = (f32[512]{0:T(512)S(1)}, f32[512]{0:T(512)S(1)}, f32[49,48,512,1]{2,1,0,3:T(8,128)}) fusion(f32[49,48]{1,0:T(8,128)} %convert_bitcast_fusion, bf16[8,49,48,256]{3,2,1,0:T(8,128)(2,1)} %get-tuple-element.47, bf16[512,8,256,1]{0,2,3,1:T(8,128)(2,1)} %bitcast.145), kind=kOutput, calls=%fused_computation.12 | convolution fusion | flops 4938521600 | bytes 16561344 | tf_op jit(solution)/shard_map/npsc,onc->pso/dot_general | solution.py:349
  282.8 91.2 %small_sum.4 = f32[8,512]{1,0:T(8,128)} custom-call(f32[8,512]{1,0:T(8,128)} %stack.56.own), custom_call_target="tpu_custom_call" | custom-call | tf_op jit(solution)/shard_map/small_sum/pallas_call | solution.py:75
  376.9 6.7 copy.72
  384.9 3.5 multiply_convert_fusion.2
  388.4 15.9 %multiply_reduce_fusion.4 = (f32[512]{0:T(512)S(1)}, f32[512]{0:T(512)S(1)}, f32[7,7,48,512]{3,2,1,0:T(8,128)}) fusion(f32[7,7,48]{2,1,0:T(8,128)S(1)} %mul.441, bf16[7,7,48,512]{3,2,1,0:T(8,128)(2,1)S(1)} %bitcast.143, bf16[512,3,3,512]{0,3,2,1:T(8,128)(2,1)S(1)} %bitcast.133), kind=kOutput, calls=%fused_computation.24 | convolution fusion | flops 9090883584 | bytes 11957440 | tf_op jit(solution)/shard_map/conv_general_dilated | solution.py:353
  404.9 18.4 %small_sum.5 = f32[8,512]{1,0:T(8,128)} custom-call(f32[8,512]{1,0:T(8,128)} %pad_maximum_fusion.2.own), custom_call_target="tpu_custom_call" | custom-call | tf_op jit(solution)/shard_map/small_sum/pallas_call | solution.py:75
  425.6 4.0 multiply_reduce_fusion.2
  435.4 2.8 multiply_reduce_fusion.1
  439.6 18.7 %small_sum.6 = f32[8,512]{1,0:T(8,128)} custom-call(f32[8,512]{1,0:T(8,128)} %stack.66.own), custom_call_target="tpu_custom_call" | custom-call | tf_op jit(solution)/shard_map/small_sum/pallas_call | solution.py:75
  459.8 5.7 multiply_convert_fusion.1
  466.9 15.5 %fusion.61 = f32[7,7,48,512]{3,2,1,0:T(8,128)} fusion(bf16[7,7,48,512]{3,2,1,0:T(8,128)(2,1)S(1)} %multiply_convert_fusion.1, bf16[512,3,3,512]{0,3,2,1:T(8,128)(2,1)} %bitcast.132), kind=kOutput, calls=%fused_computation.142 | convolution fusion | flops 9084862464 | bytes 11943936 | tf_op jit(solution)/shard_map/conv_general_dilated | solution.py:353
  483.3 6.7 fusion.51
  490.6 18.7 %small_sum.7 = f32[8,512]{1,0:T(8,128)} custom-call(f32[8,512]{1,0:T(8,128)} %pad_maximum_fusion.1.own), custom_call_target="tpu_custom_call" | custom-call | tf_op jit(solution)/shard_map/small_sum/pallas_call | solution.py:75
  512.4 11.0 %fusion.15 = f32[512,8,256]{2,0,1:T(8,128)S(1)} fusion(bf16[8,49,48,256]{3,2,1,0:T(8,128)(2,1)} %get-tuple-element.47, f32[49,48,512,1]{2,1,0,3:T(8,128)} %get-tuple-element.100, f32[49,48,512]{2,1,0:T(8,128)S(1)} %copy-done.3, f32[512]{0:T(512)S(1)} %bitcast.169, f32[512]{0:T(512)S(1)} %bitcast.168, f32[]{:T(128)} %bitcast.11, f32[512]{0:T(512)S(1)} %copy-done.27, ...), kind=kOutput, calls=%fused_computation.37 | convolution fusion | flops 4943339520 | bytes 23481540 | tf_op jit(solution)/shard_map/npsc,pso->onc/dot_general | solution.py:349
  523.4 4.5 copy.55
  527.9 4.9 reshape_reshape.10.reduce
  532.8 16.8 %fusion.60 = f32[512,3,3,512]{0,3,2,1:T(8,128)} fusion(bf16[7,7,48,512]{3,2,1,0:T(8,128)(2,1)} %bitcast.144, bf16[7,7,48,512]{3,2,1,0:T(8,128)(2,1)} %copy-done.12), kind=kOutput, calls=%fused_computation.141 | convolution fusion | flops 9084862464 | bytes 14254080 | tf_op jit(solution)/shard_map/transpose | solution.py:462
  549.6 13.8 %copy.52 = f32[512,3,3,512]{3,2,1,0:T(4,128)} copy(f32[512,3,3,512]{0,3,2,1:T(8,128)} %fusion.60) | data formatting | bytes 18874368 | tf_op jit(solution)/shard_map/transpose | solution.py:462
  563.3 16.1 %reshape_reshape.9.spatial = f32[4,2,2,2,16,4608]{5,4,3,2,1,0:T(8,128)} reshape(f32[512,3,3,512]{3,2,1,0:T(4,128)} %copy.52) | data formatting | bytes 18874368 | tf_op jit(solution)/shard_map/reshape;reshape | solution.py:294
  580.3 177.3 %settle.1 = (bf16[4,2,2,2,16,6656]{5,4,3,2,1,0:T(8,128)(2,1)}, f32[2,2,16,7680]{3,2,1,0:T(8,128)}) custom-call(f32[4,2,2,2,16,4608]{5,4,3,2,1,0:T(8,128)} %reshape_reshape.9.spatial, f32[4,2,2,2,16,2048]{5,4,3,2,1,0:T(8,128)} %reshape_reshape.10.reduce, f32[4,2,2,2,16,1024]{5,4,3,2,1,0:T(8,128)} %bitcast.127, f32[16,7680]{1,0:T(8,128)} %fusion.32.mask), custom_call_target="tpu_custom_call" | custom-call | tf_op jit(solution)/shard_map/settle/pallas_call | solution.py:302
  757.7 12.5 %reshape_reshape.11 = bf16[512,13,512]{2,1,0:T(8,128)(2,1)} reshape(bf16[4,2,2,2,16,6656]{5,4,3,2,1,0:T(8,128)(2,1)} %get-tuple-element.50) | data formatting | bytes 13631488 | tf_op jit(solution)/shard_map/reshape;reshape | solution.py:480
  770.2 7.5 copy.81
  791.0 4.3 fusion.27
  795.4 3.4 multiply_add_fusion.3
  798.8 2.6 bitcast_add_fusion
  801.4 3.0 multiply_add_fusion.2
  804.5 4.9 fusion.34
  813.5 15.1 %chan_sum.1 = f32[16,128]{1,0:T(8,128)} custom-call(f32[16,128]{1,0:T(8,128)} %pad.32.own), custom_call_target="tpu_custom_call" | custom-call | tf_op jit(solution)/shard_map/chan_sum/pallas_call | solution.py:100
  (151 shorter events, 57.8 us)
Async XLA Ops:
  7.2 797.3 %all-gather.2.cloned.1.call-start = ((), (), s32[]{:S(2)}) async-start(), calls=%async_computation | async-start | bytes 7667712 | tf_op jit(solution)/shard_map/all_gather | solution.py:413
  12.8 8.4 copy-start.17
  12.8 8.4 copy-start.2
  12.8 8.4 copy-start.8
  12.8 8.5 %copy-start.5 = (s32[64,2048]{1,0:T(8,128)S(1)}, s32[64,2048]{1,0:T(8,128)}, u32[]{:S(2)}) copy-start(s32[64,2048]{1,0:T(8,128)} %param.28) | copy-start | bytes 1572868
  12.8 9.7 %copy-start.22 = (f32[4,64]{1,0:T(4,128)S(1)}, f32[4,64]{1,0:T(4,128)}, u32[]{:S(2)}) copy-start(f32[4,64]{1,0:T(4,128)} %param.33) | copy-start | bytes 3076
  267.1 166.6 %copy-start.28 = (f32[48]{0:T(128)}, f32[48]{0:T(128)S(1)}, u32[]{:S(2)}) copy-start(f32[48]{0:T(128)S(1)} %broadcast_maximum_fusion) | copy-start | bytes 580
  270.9 105.7 %copy-start.21 = (f32[8,8,128]{2,1,0:T(8,128)S(1)}, f32[8,8,128]{2,1,0:T(8,128)}, u32[]{:S(2)}) copy-start(f32[8,8,128]{2,1,0:T(8,128)} %get-tuple-element.46) | copy-start | bytes 98308
  282.1 102.8 %copy-start.19 = (f32[49,48]{1,0:T(8,128)S(1)}, f32[49,48]{1,0:T(8,128)}, u32[]{:S(2)}) copy-start(f32[49,48]{1,0:T(8,128)} %convert_bitcast_fusion) | copy-start | bytes 28228
  383.5 4.9 copy-start.4
  388.4 15.9 %copy-start.11 = (bf16[49,48,512]{2,1,0:T(8,128)(2,1)}, bf16[49,48,512]{2,1,0:T(8,128)(2,1)S(1)}, u32[]{:S(2)}) copy-start(bf16[49,48,512]{2,1,0:T(8,128)(2,1)S(1)} %multiply_convert_fusion.2) | copy-start | bytes 7225348
  404.3 25.3 %copy-start.26 = (f32[1000]{0:T(1024)S(1)}, f32[1000]{0:T(1024)}, u32[]{:S(2)}) copy-start(f32[1000]{0:T(1024)} %param.32) | copy-start | bytes 12004
  404.3 29.3 %copy-start.30 = (f32[48]{0:T(128)S(1)}, f32[48]{0:T(128)}, u32[]{:S(2)}) copy-start(f32[48]{0:T(128)} %compare_convert_fusion) | copy-start | bytes 580
  404.3 31.1 %slice-start.2 = ((s8[4816896]{0:T(1024)(128)(4,1)}), s8[622592]{0:T(1024)(128)(4,1)S(1)}, s32[]{:S(2)}) async-start(s8[4816896]{0:T(1024)(128)(4,1)} %bitcast.121), calls=%async_computation.3 | async-start | bytes 1245184
  425.6 9.8 %slice-start.3 = ((s8[4816896]{0:T(1024)(128)(4,1)}), s8[4194304]{0:T(1024)(128)(4,1)S(1)}, s32[]{:S(2)}) async-start(s8[4816896]{0:T(1024)(128)(4,1)} %bitcast.121), calls=%async_computation.4 | async-start | bytes 8388608
  466.9 15.6 %copy-start.6 = (s32[64,2048]{1,0:T(8,128)S(1)}, s32[64,2048]{1,0:T(8,128)}, u32[]{:S(2)}) copy-start(s32[64,2048]{1,0:T(8,128)} %param.28) | copy-start | bytes 1572868
  483.3 26.0 %copy-start.29 = (f32[48]{0:T(128)S(1)}, f32[48]{0:T(128)}, u32[]{:S(2)}) copy-start(f32[48]{0:T(128)} %copy-done.28) | copy-start | bytes 580
  490.0 22.3 %copy-start.27 = (f32[512]{0:T(512)S(1)}, f32[512]{0:T(512)}, u32[]{:S(2)}) copy-start(f32[512]{0:T(512)} %get-tuple-element.94) | copy-start | bytes 6148
  509.3 3.1 copy-start.3
  512.2 11.2 %copy-start.24 = (f32[1,512]{1,0:T(1,128)}, f32[1,512]{1,0:T(1,128)S(1)}, u32[]{:S(2)}) copy-start(f32[1,512]{1,0:T(1,128)S(1)} %get-tuple-element.86) | copy-start | bytes 6148
  512.2 11.2 %copy-start.25 = (f32[1,512]{1,0:T(1,128)}, f32[1,512]{1,0:T(1,128)S(1)}, u32[]{:S(2)}) copy-start(f32[1,512]{1,0:T(1,128)S(1)} %get-tuple-element.87) | copy-start | bytes 6148
  563.3 16.1 %copy-start.13 = (f32[64,2048]{1,0:T(8,128)S(1)}, f32[64,2048]{1,0:T(8,128)}, u32[]{:S(2)}) copy-start(f32[64,2048]{1,0:T(8,128)} %convert_element_type.83) | copy-start | bytes 1572868
  780.3 5.7 copy-start.23
  788.7 6.6 slice-start
  791.0 4.4 slice-start.1
  791.0 4.4 copy-start.18
  791.0 4.4 copy-start.20
  791.0 4.4 copy-start.31
  795.4 3.4 copy-start.16
  804.5 4.9 copy-start.1
  804.5 5.9 copy-start
  812.8 18.7 %copy-start.9 = (f32[64,4608]{1,0:T(8,128)S(1)}, f32[64,4608]{1,0:T(8,128)}, u32[]{:S(2)}) copy-start(f32[64,4608]{1,0:T(8,128)} %param.29) | copy-start | bytes 3538948
  (5 other events, 9.7 us)
Sparse Core Ops, SparseCore 0:
  10.2 274.5 all-gather.1

commit v2 on v1

--- a/solution.py
+++ b/solution.py
@@ -53,34 +53,6 @@
         self.used += 1
         copy.start()
         return copy
-
-
-def small_sum_kernel(own, total, held, send, recv):
-    (z, y, x, core), (nz, ny, nx, nc) = place()
-    peers = [
-        at(lax.rem(z + i, nz), lax.rem(y + j, ny), lax.rem(x + k, nx), lax.rem(core + m, nc))
-        for i in range(nz) for j in range(ny) for k in range(nx) for m in range(nc) if i + j + k + m
-    ]
-    greet(peers)
-    copies = Copies(send, recv)
-    started = [copies.start(own, held.at[k + 1], peer) for k, peer in enumerate(peers)]
-    held[0] = own[...]
-    for copy in started:
-        copy.wait()
-    total[...] = jnp.sum(held[...], axis=0)
-
-
-def small_sum(rows, cid):
-    n = lax.axis_size("chan") * lax.axis_size("batch")
-    return pl.pallas_call(
-        small_sum_kernel,
-        out_shape=jax.ShapeDtypeStruct(rows.shape, jnp.float32),
-        in_specs=[VMEM],
-        out_specs=VMEM,
-        scratch_shapes=[pltpu.VMEM((n,) + rows.shape, jnp.float32), DMA((n - 1,)), DMA((n - 1,))],
-        compiler_params=pltpu.CompilerParams(collective_id=cid, has_side_effects=True),
-        name="small_sum",
-    )(rows)
 
 
 def chan_sum_kernel(own, total, held, send, recv):
@@ -108,59 +80,408 @@
     )(rows)
 
 
-def spread_kernel(images, weights, norms, images_out, weights_out, norms_out, send, recv, local):
+def dot(left, right, left_dim, right_dim):
+    return lax.dot_general(left, right, (((left_dim,), (right_dim,)), ((), ())), preferred_element_type=jnp.float32)
+
+
+def sigmoid(value):
+    return 1.0 / (1.0 + jnp.exp(-value))
+
+
+def packed(row):
+    return jnp.concatenate([row[:, i : i + 128] for i in range(0, row.shape[1], 128)], axis=0)
+
+
+def unpacked(block):
+    return jnp.concatenate([block[i : i + 1] for i in range(block.shape[0])], axis=1)
+
+
+def step_kernel(
+    images, weights, roots, norms, valid, labels, used, divisor, bias,
+    spatial_out, reduce_out, head_out, totals_out, weights_out, roots_out,
+    own_images, first, second, hidden_pad, grad_pad, turned_grad, taps, reduce_low, head_low,
+    norms_held, pack_one, pack_two, pack_three, pack_four, held_one, held_two, held_three, held_four,
+    partial, pooled_low, d_logits, d_act, head_buf, grad_buf, send, recv, local,
+):
     (z, y, x, core), (nz, ny, nx, nc) = place()
     c, n = lax.axis_index("chan"), lax.axis_size("chan")
+    f32, low = jnp.float32, jnp.bfloat16
+    slots = used.shape[0]
+    side = SIDE
+    line = side * slots
+    wide_line = (side + 1) * slots
+    pixels = side * side
+    rim = (side + 2) * slots
+    body_rows = side * wide_line
+    width = first.shape[1]
+    depth = own_images.shape[-1]
+    everyone = [
+        at(lax.rem(z + i, nz), lax.rem(y + j, ny), lax.rem(x + k, nx), lax.rem(core + m, nc))
+        for i in range(nz) for j in range(ny) for k in range(nx) for m in range(nc) if i + j + k + m
+    ]
+    greet(everyone)
+    copies = Copies(send, recv)
     others = turned(c, n)
-    greet([{"chan": k} for k in others] + [at(z, y, k, core) for k in turned(x, nx)] + [at(z, y, x, 1 - core)])
-    copies = Copies(send, recv)
-    quarter = pltpu.make_async_copy(weights.at[x, core], weights_out.at[z, y, x, core], local.at[0])
-    quarter.start()
-    along_z = [
-        copies.start(weights.at[x, core], weights_out.at[z, y, x, core], at(k, y, x, core)) for k in turned(z, nz)
-    ]
-    rest = [copies.start(norms, norms_out.at[c], {"chan": k}) for k in others]
-    rest += [copies.start(images.at[k], images_out.at[c], {"chan": k}) for k in others]
-    own = pltpu.make_async_copy(images.at[c], images_out.at[c], local.at[1])
+    sources = ((weights, weights_out), (roots, roots_out))
+
+    quarters = []
+    for i, (source, target) in enumerate(sources):
+        copy = pltpu.make_async_copy(source.at[x, core], target.at[z, y, x, core], local.at[i])
+        copy.start()
+        quarters.append(copy)
+    along_z = [[copies.start(source.at[x, core], target.at[z, y, x, core], at(k, y, x, core)) for k in turned(z, nz)]
+               for source, target in sources[:1]]
+    norm_copies = [copies.start(norms, norms_held.at[k + 1], {"chan": other}) for k, other in enumerate(others)]
+    image_copies = [copies.start(images.at[k], own_images.at[c, :, pl.ds(0, line)], {"chan": k}) for k in others]
+    along_z += [[copies.start(source.at[x, core], target.at[z, y, x, core], at(k, y, x, core)) for k in turned(z, nz)]
+                for source, target in sources[1:]]
+    own = pltpu.make_async_copy(images.at[c], own_images.at[c, :, pl.ds(0, line)], local.at[2])
     own.start()
-    own_norms = pltpu.make_async_copy(norms, norms_out.at[c], local.at[2])
-    own_norms.start()
-    quarter.wait()
-    for copy in along_z:
-        copy.wait()
-    part = weights_out.at[:, y, x, core]
-    copies.start(part, part, at(z, 1 - y, x, core)).wait()
-    part = weights_out.at[:, :, x, core]
-    along_x = [copies.start(part, part, at(z, y, k, core)) for k in turned(x, nx)]
-    for copy in along_x:
-        copy.wait()
-    part = weights_out.at[:, :, :, core]
-    copies.start(part, part, at(z, y, x, 1 - core)).wait()
-    own.wait()
-    own_norms.wait()
-    for copy in rest:
-        copy.wait()
-
-
-def spread(images, weights, norms):
-    nz, nx = lax.axis_size("chan") // 2, lax.axis_size("batch") // 2
-    n = lax.axis_size("chan")
-    count = (nz - 1) + 2 * (n - 1) + 1 + (nx - 1) + 1
-    rows, columns = weights.shape[0] // (2 * nx), weights.shape[1]
-    images_out, weights_out, norms_out = pl.pallas_call(
-        spread_kernel,
+    norms_held[0] = norms[...]
+
+    def clear(i, _):
+        rows = pl.ds(pl.multiple_of(i * slots, slots), slots)
+        hidden_pad[rows, :] = jnp.zeros((slots, width), low)
+        grad_pad[rows, :] = jnp.zeros((slots, width), low)
+        return 0
+
+    lax.fori_loop(0, hidden_pad.shape[0] // slots, clear, 0)
+    for k in range(n):
+        for j in range(side):
+            own_images[k, j, pl.ds(line, slots), :] = jnp.zeros((slots, depth), low)
+
+    for i, (source, target) in enumerate(sources):
+        quarters[i].wait()
+        for copy in along_z[i]:
+            copy.wait()
+        part = target.at[:, y, x, core]
+        along_y = copies.start(part, part, at(z, 1 - y, x, core))
+        along_y.wait()
+        part = target.at[:, :, x, core]
+        along_x = [copies.start(part, part, at(z, y, k, core)) for k in turned(x, nx)]
+        for copy in along_x:
+            copy.wait()
+        part = target.at[:, :, :, core]
+        copies.start(part, part, at(z, y, x, 1 - core)).wait()
+        if i == 0:
+            fetched = []
+            start = 0
+            for j, held in enumerate((taps, reduce_low, head_low)):
+                size = held.shape[-1]
+                copy = pltpu.make_async_copy(target.at[:, :, :, :, :, pl.ds(start, size)], held, local.at[3 + j])
+                copy.start()
+                fetched.append(copy)
+                start += size
+            for copy in fetched:
+                copy.wait()
+    taps, reduce_low, head_low = (held.reshape(width, held.shape[-1]) for held in (taps, reduce_low, head_low))
+    for copy in norm_copies:
+        copy.wait()
+    norm_rows = jnp.sum(norms_held[...], axis=0)
+    gain_one, shift_one, gain_two, shift_two = (norm_rows[i : i + 1] for i in range(4))
+
+    def line_rows(j):
+        return pl.ds(pl.multiple_of(j * line, slots), line)
+
+    def pixel_rows(p):
+        return pl.ds(pl.multiple_of(p * slots, slots), slots)
+
+    def padded_pixel(p):
+        j = p // side
+        return pl.ds(pl.multiple_of(rim + (p + j) * slots, slots), slots)
+
+    def across(block):
+        return jnp.concatenate([block] * (width // 128), axis=1)
+
+    def fold(value):
+        return jnp.sum(value.reshape(-1, 8, width), axis=0)
+
+    def total_of(index):
+        return jnp.sum(partial[index], axis=0, keepdims=True)
+
+    def exchange(pack, held):
+        pack_copies = [copies.start(pack, held.at[k + 1], peer) for k, peer in enumerate(everyone)]
+        held[0] = pack[...]
+        return pack_copies
+
+    def settled(pack_copies, held):
+        for copy in pack_copies:
+            copy.wait()
+        return jnp.sum(held[...], axis=0)
+
+    for k in range(n):
+        source = lax.rem(c + n - k, n)
+        if k == 0:
+            own.wait()
+        else:
+            image_copies[k - 1].wait()
+        columns = pl.ds(pl.multiple_of(source * depth, depth), depth)
+
+        def reduce_line(j, _, k=k, source=source, columns=columns):
+            value = dot(own_images[source, j, pl.ds(0, line), :], reduce_low[:, columns], 1, 1)
+            if k:
+                value = first[line_rows(j), :] + value
+            first[line_rows(j), :] = value
+            return 0
+
+        lax.fori_loop(0, side, reduce_line, 0)
+
+    def norm_sums(ref):
+        partial[...] = jnp.zeros(partial.shape, f32)
+
+        def add(p, _):
+            value = ref[pixel_rows(p), :]
+            kept = value * across(valid[pixel_rows(p), :])
+            partial[0] += fold(kept)
+            partial[1] += fold(kept * value)
+            return 0
+
+        lax.fori_loop(0, pixels, add, 0)
+
+    norm_sums(first)
+    all_valid = jnp.sum(valid[...], axis=0, keepdims=True)
+    pack_one[...] = jnp.concatenate(
+        [packed(total_of(0)), packed(total_of(1)), all_valid, jnp.zeros((7, 128), f32)], axis=0)
+    stats = settled(exchange(pack_one, held_one), held_one)
+    rows = width // 128
+    count = jnp.concatenate([stats[2 * rows : 2 * rows + 1]] * rows, axis=1)
+
+    def norm_of(stats):
+        mean = unpacked(stats[:rows]) / count
+        scale = lax.rsqrt(unpacked(stats[rows : 2 * rows]) / count - mean * mean + EPS)
+        return mean, scale
+
+    mean_one, scale_one = norm_of(stats)
+
+    def activate(p, _):
+        normed = (first[pixel_rows(p), :] - mean_one) * scale_one
+        pre = gain_one * normed + shift_one
+        act = pre * sigmoid(pre) * across(valid[pixel_rows(p), :])
+        hidden_pad[padded_pixel(p), :] = act.astype(low)
+        return 0
+
+    lax.fori_loop(0, pixels, activate, 0)
+
+    def conv_line(j, _):
+        value = None
+        for t in range(9):
+            offset = (t // 3 - 1) * wide_line + (t % 3 - 1) * slots
+            rows_in = pl.ds(pl.multiple_of(rim + j * wide_line + offset, slots), line)
+            term = dot(hidden_pad[rows_in, :], taps[:, t * width : (t + 1) * width], 1, 1)
+            value = term if value is None else value + term
+        second[line_rows(j), :] = value
+        return 0
+
+    lax.fori_loop(0, side, conv_line, 0)
+    norm_sums(second)
+    pack_two[...] = jnp.concatenate([packed(total_of(0)), packed(total_of(1))], axis=0)
+    stats = settled(exchange(pack_two, held_two), held_two)
+    mean_two, scale_two = norm_of(stats)
+
+    def pool(p, sums):
+        pooled, slopes, slopes_normed = sums
+        normed = (second[pixel_rows(p), :] - mean_two) * scale_two
+        pre = gain_two * normed + shift_two
+        sigma = sigmoid(pre)
+        kept = across(valid[pixel_rows(p), :])
+        slope = sigma * (1.0 + pre * (1.0 - sigma)) * kept
+        return pooled + pre * sigma * kept, slopes + slope, slopes_normed + slope * normed
+
+    nothing = jnp.zeros((slots, width), f32)
+    pooled, slopes, slopes_normed = lax.fori_loop(0, pixels, pool, (nothing, nothing, nothing))
+    divide = across(divisor[...])
+    pooled_low[...] = (pooled / divide).astype(low)
+    logits = dot(pooled_low[...], head_low[...], 1, 0) + bias[...]
+    classes = logits.shape[1]
+    index = lax.broadcasted_iota(jnp.int32, (slots, classes), 1)
+    onehot = (index == labels[:, :1]).astype(f32)
+    top = jnp.max(logits, axis=1, keepdims=True)
+    log_total = jnp.log(jnp.sum(jnp.exp(logits - top), axis=1, keepdims=True)) + top
+    picked = jnp.sum(onehot * logits, axis=1, keepdims=True)
+    use = used[:, :1]
+    loss = jnp.sum(use * (log_total - picked))
+    d_logits[...] = (use * (jnp.exp(logits - log_total) - onehot) / SLOTS_DEV).astype(low)
+    bias_sum = jnp.sum(d_logits[...].astype(f32), axis=0, keepdims=True)
+    half = width // 2
+
+    def to_pooled(m, _):
+        rows_in = pl.ds(pl.multiple_of(m * half, half), half)
+        d_act[:, rows_in] = dot(d_logits[...], head_low[rows_in, :], 1, 1) / across(divisor[...])[:, :half]
+        return 0
+
+    lax.fori_loop(0, 2, to_pooled, 0)
+    at_class = lax.broadcasted_iota(jnp.int32, (1, classes), 1)
+    bias_sum = jnp.where(at_class == classes - 1, loss, jnp.where(at_class == classes - 2, jnp.sum(use), bias_sum))
+    pack_three[...] = jnp.concatenate(
+        [packed(jnp.sum(d_act[...] * slopes, axis=0, keepdims=True)),
+         packed(jnp.sum(d_act[...] * slopes_normed, axis=0, keepdims=True)), packed(bias_sum)], axis=0)
+    going = exchange(pack_three, held_three)
+
+    def to_head(m, _):
+        columns = pl.ds(pl.multiple_of(m * (classes // 2), 128), classes // 2)
+        head_buf[:, columns] = dot(pooled_low[...], d_logits[:, columns], 0, 0)
+        return 0
+
+    lax.fori_loop(0, 2, to_head, 0)
+    head_copy = pltpu.make_async_copy(head_buf, head_out, local.at[6])
+    head_copy.start()
+    totals_two = settled(going, held_three)
+    shift_grad, gain_grad = unpacked(totals_two[:rows]), unpacked(totals_two[rows : 2 * rows])
+    factor = gain_two * scale_two / count
+
+    def leave_second(p, _):
+        normed = (second[pixel_rows(p), :] - mean_two) * scale_two
+        pre = gain_two * normed + shift_two
+        sigma = sigmoid(pre)
+        kept = across(valid[pixel_rows(p), :])
+        d_pre = d_act[...] * kept * (sigma * (1.0 + pre * (1.0 - sigma)))
+        d_z = factor * (count * d_pre - shift_grad - normed * gain_grad) * kept
+        grad_pad[padded_pixel(p), :] = d_z.astype(low)
+        return 0
+
+    lax.fori_loop(0, pixels, leave_second, 0)
+
+    partial[...] = jnp.zeros(partial.shape, f32)
+
+    def spread_line(j, _):
+        value = None
+        for t in range(9):
+            offset = (t // 3 - 1) * wide_line + (t % 3 - 1) * slots
+            rows_in = pl.ds(pl.multiple_of(rim + j * wide_line - offset, slots), line)
+            term = dot(grad_pad[rows_in, :], taps[:, t * width : (t + 1) * width], 1, 0)
+            value = term if value is None else value + term
+        second[line_rows(j), :] = value
+        return 0
+
+    lax.fori_loop(0, side, spread_line, 0)
+
+    def enter_first(p, _):
+        normed = (first[pixel_rows(p), :] - mean_one) * scale_one
+        pre = gain_one * normed + shift_one
+        sigma = sigmoid(pre)
+        d_pre = second[pixel_rows(p), :] * across(valid[pixel_rows(p), :]) * (sigma * (1.0 + pre * (1.0 - sigma)))
+        second[pixel_rows(p), :] = d_pre
+        partial[0] += fold(d_pre)
+        partial[1] += fold(d_pre * normed)
+        return 0
+
+    lax.fori_loop(0, pixels, enter_first, 0)
+    pack_four[...] = jnp.concatenate([packed(total_of(0)), packed(total_of(1))], axis=0)
+    going = exchange(pack_four, held_four)
+
+    def turn(j, _):
+        rows_in = pl.ds(pl.multiple_of(rim + j * wide_line, slots), wide_line)
+        turned_grad[:, pl.ds(pl.multiple_of(j * wide_line, 128), wide_line)] = grad_pad[rows_in, :].T
+        return 0
+
+    lax.fori_loop(0, side, turn, 0)
+
+    def leave(slot, target, sem):
+        copy = pltpu.make_async_copy(grad_buf.at[slot], target, local.at[sem])
+        copy.start()
+        return copy
+
+    leaving = []
+    for t in range(9):
+        offset = (t // 3 - 1) * wide_line + (t % 3 - 1) * slots
+        slot = t % 2
+        if t >= 2:
+            leaving[t - 2].wait()
+        shifted = hidden_pad.at[pl.ds(rim + offset, body_rows)]
+
+        def tap_rows(m, _, slot=slot, shifted=shifted):
+            rows_out = pl.ds(pl.multiple_of(m * 256, 256), 256)
+            grad_buf[slot, rows_out, :] = dot(turned_grad[rows_out, :], shifted[...], 1, 0)
+            return 0
+
+        lax.fori_loop(0, width // 256, tap_rows, 0)
+        leaving.append(leave(slot, spatial_out.at[:, pl.ds(t * width, width)], 7 + slot))
+
+    totals_one = settled(going, held_four)
+    shift_sum, gain_sum = unpacked(totals_one[:rows]), unpacked(totals_one[rows : 2 * rows])
+    factor_one = gain_one * scale_one / count
+
+    def leave_first(p, _):
+        normed = (first[pixel_rows(p), :] - mean_one) * scale_one
+        kept = across(valid[pixel_rows(p), :])
+        d_z = factor_one * (count * second[pixel_rows(p), :] - shift_sum - normed * gain_sum) * kept
+        grad_pad[padded_pixel(p), :] = d_z.astype(low)
+        return 0
+
+    lax.fori_loop(0, pixels, leave_first, 0)
+    lax.fori_loop(0, side, turn, 0)
+    per = width // depth
+    for t in range(n // per):
+        slot = (9 + t) % 2
+        leaving[9 + t - 2].wait()
+
+        def source_rows(m, _, slot=slot, t=t):
+            rows_out = pl.ds(pl.multiple_of(m * 256, 256), 256)
+            for k in range(per):
+                block = own_images[t * per + k].reshape(body_rows, depth)
+                grad_buf[slot, rows_out, k * depth : (k + 1) * depth] = dot(turned_grad[rows_out, :], block, 1, 0)
+            return 0
+
+        lax.fori_loop(0, width // 256, source_rows, 0)
+        leaving.append(leave(slot, reduce_out.at[:, pl.ds(t * width, width)], 7 + slot))
+    totals_out[...] = jnp.concatenate([totals_two, totals_one], axis=0)
+    head_copy.wait()
+    for copy in leaving[-2:]:
+        copy.wait()
+
+
+def local_step(images, weights, roots, norms, valid, labels, used, divisor, bias):
+    n, nb = lax.axis_size("chan"), lax.axis_size("batch")
+    nz, nx = n // 2, nb // 2
+    slots, width = used.shape[0], norms.shape[1]
+    line, depth, classes = SIDE * slots, images.shape[-1], bias.shape[1]
+    f32, low = jnp.float32, jnp.bfloat16
+    rows = weights.shape[0] // nb
+    grids = ((SIDE * (SIDE + 1) + 2 * (SIDE + 2)) * slots, width)
+    shape = jax.ShapeDtypeStruct
+    gathered = lambda a: shape((nz, 2, nx, 2, rows, a.shape[1]), a.dtype)
+    quarters = lambda a: a.reshape(nx, 2, rows, a.shape[1])
+    held = lambda k: pltpu.VMEM((n * nb, k, 128), f32)
+    pack = lambda k: pltpu.VMEM((k, 128), f32)
+    count = 2 * (nz - 1) + 2 * (n - 1) + 2 * (1 + (nx - 1) + 1) + 4 * (n * nb - 1)
+    two = 2 * width // 128
+    three = two + classes // 128
+    weight = lambda size: pltpu.VMEM((nz, 2, nx, 2, rows, size), low)
+    spatial, reduce, head, totals, weights_full, roots_full = pl.pallas_call(
+        step_kernel,
         out_shape=(
-            jax.ShapeDtypeStruct(images.shape, images.dtype),
-            jax.ShapeDtypeStruct((nz, 2, nx, 2, rows, columns), weights.dtype),
-            jax.ShapeDtypeStruct((n,) + norms.shape, norms.dtype),
+            shape((width, 9 * width), f32),
+            shape((width, n * depth), f32),
+            shape((width, classes), f32),
+            shape((two + three, 128), f32),
+            gathered(weights),
+            gathered(roots),
         ),
-        in_specs=[ANY] * 3,
-        out_specs=(ANY,) * 3,
-        scratch_shapes=[DMA((count,)), DMA((count,)), DMA((3,))],
-        compiler_params=pltpu.CompilerParams(collective_id=0, has_side_effects=True),
-        name="spread",
-    )(images, weights.reshape(nx, 2, rows, columns), norms)
-    return images_out, weights_out.reshape(n * weights.shape[0], columns), norms_out
+        in_specs=[ANY, ANY, ANY, VMEM, VMEM, VMEM, VMEM, VMEM, VMEM],
+        out_specs=(ANY, ANY, ANY, VMEM, ANY, ANY),
+        scratch_shapes=[
+            pltpu.VMEM((n, SIDE, line + slots, depth), low),
+            pltpu.VMEM((SIDE * line, width), f32),
+            pltpu.VMEM((SIDE * line, width), f32),
+            pltpu.VMEM(grids, low),
+            pltpu.VMEM(grids, low),
+            pltpu.VMEM((width, SIDE * (line + slots)), low),
+            weight(9 * width), weight(n * depth), weight(classes),
+            pltpu.VMEM((n,) + norms.shape, f32),
+            pack(two + 8), pack(two), pack(three), pack(two),
+            held(two + 8), held(two), held(three), held(two),
+            pltpu.VMEM((2, 8, width), f32),
+            pltpu.VMEM((slots, width), low),
+            pltpu.VMEM((slots, classes), low),
+            pltpu.VMEM((slots, width), f32),
+            pltpu.VMEM((width, classes), f32),
+            pltpu.VMEM((2, width, width), f32),
+            DMA((count,)), DMA((count,)), DMA((9,)),
+        ],
+        compiler_params=pltpu.CompilerParams(collective_id=0, has_side_effects=True, vmem_limit_bytes=60 << 20),
+        name="step",
+    )(images.reshape(n, SIDE, line, depth), quarters(weights), quarters(roots), norms, valid, labels, used, divisor, bias)
+    return spatial, reduce, head, totals[:three], totals[three:], roots_full.reshape(width, roots.shape[1])
 
 
 def settle_kernel(wire, spatial, reduce, head, mask, full, own, sums_a, sums_b, core_a, core_b, x_a, x_b, y_a, y_b,
@@ -331,13 +652,6 @@
 def own_part(array, axis, name="chan"):
     size = array.shape[axis] // lax.axis_size(name)
     return lax.dynamic_slice_in_dim(array, lax.axis_index(name) * size, size, axis)
-
-
-def stacked(rows):
-    width = rows[0].shape[0]
-    rows = [jnp.pad(r, (0, width - r.shape[0])) for r in rows]
-    rows += [jnp.zeros((width,), jnp.float32)] * (SMALL - len(rows))
-    return jnp.stack(rows)
 
 
 def two_parts(array):
@@ -390,91 +704,32 @@
     reduce_float = reduce_mask.astype(f32)
     spatial_float = spatial_mask.astype(f32)
 
+    spread_out = lambda a: jnp.broadcast_to(a[:, None], (a.shape[0], 128))
     by_pixel = images.reshape(n, slots, pixels, channels).transpose(0, 2, 1, 3)
     weights = jnp.concatenate(
         [(spatial_weight * spatial_float).astype(low), (reduce_weight * reduce_float).astype(low),
          jnp.pad(head_weight.astype(low), ((0, 0), (0, padded - classes)))], axis=1)
-    norms = jnp.pad(norm_params, ((0, 4), (0, 128 - rows_out)))
-    own_images, weights_full, norms_full = spread(by_pixel, weights, norms)
-    taps = weights_full[:, : 9 * width].reshape(width, 3, 3, width)
-    reduce_low = weights_full[:, 9 * width : 9 * width + c_in]
-    head_low = weights_full[:, 9 * width + c_in : 9 * width + c_in + classes]
-    norm_full = norms_full[:, :4, :rows_out].transpose(1, 0, 2).reshape(4, width)
-
+    roots = input_side_roots.astype(low).transpose(1, 0, 2).reshape(rows_out, -1)
+    norms = lax.dynamic_update_slice_in_dim(
+        jnp.zeros((8, width), f32), jnp.pad(norm_params, ((0, 4), (0, 0))), lax.axis_index("chan") * rows_out, 1)
     mask_own = own_part(pixel_mask, 0).astype(f32)
-    valid = mask_own.T[:, :, None]
-    own_labels = own_part(labels, 0)
     filled = jnp.sum(mask_own, axis=1)
-    divisor = jnp.maximum(filled, 1.0)
-    used = (filled > 0.0).astype(f32)
-
-    first_pre = product("npsc,onc->pso", own_images, reduce_low.reshape(width, n, channels))
-    roots_low, _ = lax.optimization_barrier((input_side_roots.astype(low), first_pre[0, 0, 0]))
-    right_full = lax.all_gather(roots_low, "chan", axis=1, tiled=True)
-
-    def sums_of(value):
-        return jnp.sum(value * valid, axis=(0, 1)), jnp.sum(value * value * valid, axis=(0, 1))
-
-    def forward(pre_norm, sums, count, gain, shift):
-        mean = sums[0] / count
-        scale = lax.rsqrt(sums[1] / count - mean * mean + EPS)
-        normed = (pre_norm - mean) * scale
-        pre = gain * normed + shift
-        return normed, pre, scale
-
-    stats = small_sum(stacked([*sums_of(first_pre), jnp.full((width,), jnp.sum(valid))]), 2)
-    count = stats[2, 0]
-    normed_one, pre_one, scale_one = forward(first_pre, stats, count, norm_full[0], norm_full[1])
-    hidden = (jax.nn.silu(pre_one) * valid).astype(low).reshape(side, side, slots, width)
-    second_pre = conv_grid(hidden, taps, ("HWNC", "OHWI", "HWNC")).reshape(pixels, slots, width)
-    stats = small_sum(stacked([*sums_of(second_pre)]), 3)
-    normed_two, pre_two, scale_two = forward(second_pre, stats, count, norm_full[2], norm_full[3])
-    second_act = jax.nn.silu(pre_two) * valid
-    pooled = (jnp.sum(second_act, axis=0) / divisor[:, None]).astype(low)
-    logits = jnp.dot(pooled, head_low, preferred_element_type=f32) + head_bias
-    onehot = (jnp.arange(classes)[None, :] == own_labels[:, None]).astype(f32)
-    log_total = jax.nn.logsumexp(logits, axis=1)
-    picked = jnp.sum(onehot * logits, axis=1)
-    loss_local = jnp.sum(used * (log_total - picked))
-    d_logits = (used[:, None] * (jnp.exp(logits - log_total[:, None]) - onehot) / SLOTS_DEV).astype(low)
-    head_local = product("so,sc->oc", pooled, d_logits)
-    bias_local = jnp.sum(d_logits.astype(f32), axis=0)
-    d_pooled = product("sc,oc->so", d_logits, head_low)
-    d_act = jnp.broadcast_to((d_pooled / divisor[:, None])[None], second_act.shape)
-
-    def backward(d_act, normed, pre, scale, gain, cid, extra):
-        d_pre = d_act * valid * silu_slope(pre)
-        sums = small_sum(
-            stacked([jnp.sum(d_pre, axis=(0, 1)), jnp.sum(d_pre * normed, axis=(0, 1))] + extra), cid)
-        d_z = gain * scale / count * (count * d_pre - sums[0] - normed * sums[1]) * valid
-        return d_z.astype(low), sums
-
-    half = padded // 2
-    bias_padded = jnp.pad(bias_local, (0, padded - classes))
-    misc = jnp.zeros((width,), f32).at[0].set(loss_local).at[1].set(jnp.sum(used))
-    d_second, sums_two = backward(d_act, normed_two, pre_two, scale_two, norm_full[2], 4,
-                                  [bias_padded[:half], bias_padded[half:], misc])
-    d_second = d_second.reshape(side, side, slots, width)
-    spatial_local = lax.conv_general_dilated(
-        hidden, d_second, (1, 1), ((1, 1), (1, 1)), dimension_numbers=("HWCN", "HWIO", "HWNC"),
-        preferred_element_type=f32,
-    )
-    spatial_local = spatial_local.transpose(3, 0, 1, 2).reshape(width, 9 * width)
-    d_hidden = conv_grid(
-        d_second, taps[:, ::-1, ::-1, :], ("HWNC", "IHWO", "HWNC")
-    ).reshape(pixels, slots, width)
-    d_first, sums_one = backward(d_hidden, normed_one, pre_one, scale_one, norm_full[0], 5, [])
-    reduce_local = product("npsc,pso->onc", own_images, d_first).reshape(width, c_in)
+    spatial_local, reduce_local, head_local, sums_two, sums_one, roots_full = local_step(
+        by_pixel, weights, roots, norms, spread_out(mask_own.T.reshape(-1)), spread_out(own_part(labels, 0)),
+        spread_out((filled > 0.0).astype(f32)), spread_out(jnp.maximum(filled, 1.0)),
+        jnp.pad(head_bias, (0, padded - classes), constant_values=-1e30)[None])
 
     mask_rows = jnp.concatenate([spatial_float, reduce_float, jnp.ones((rows_out, padded), f32)], axis=1)
-    full, own = settle(spatial_local, reduce_local, jnp.pad(head_local, ((0, 0), (0, padded - classes))),
-                       own_part(mask_rows, 0, "batch"), jnp.float32)
+    full, own = settle(spatial_local, reduce_local, head_local, own_part(mask_rows, 0, "batch"), jnp.float32)
     spatial_grad = own[:, : 9 * width]
     reduce_grad = own[:, 9 * width : 9 * width + c_in]
     head_grad = own[:, 9 * width + c_in : 9 * width + c_in + classes]
-    loss_sum, slot_count = sums_two[4, 0], sums_two[4, 1]
-    bias_grad = jnp.concatenate([sums_two[2], sums_two[3]])[:classes]
-    norm_gain_gradient = own_part(jnp.stack([sums_one[1], sums_one[0], sums_two[1], sums_two[0]]), 1)
+    of_norms = jnp.stack([a.reshape(-1) for a in (sums_one[4:], sums_one[:4], sums_two[4:8], sums_two[:4])])
+    norm_gain_gradient = own_part(of_norms, 1)
+    of_head = sums_two[8:].reshape(-1)
+    bias_grad = of_head[:classes]
+    loss_sum, slot_count = of_head[-1], of_head[-2]
+    right_full = roots_full.reshape(width, -1, width)
 
     tiles_one = c_in // width
     blocks_of = lambda a: a.reshape(a.shape[0], -1, width).transpose(1, 0, 2)
@@ -486,7 +741,7 @@
     left_high, left_rest = two_parts(left_root)
     inner = product("tak,tkb->tab", left_high, blocks_full) + product("tak,tkb->tab", left_rest, blocks_full)
     inner_high, inner_rest = two_parts(inner)
-    outer = product("tak,tkb->tab", inner_high, right_full) + product("tak,tkb->tab", inner_rest, right_full)
+    outer = product("tak,ktb->tab", inner_high, right_full) + product("tak,ktb->tab", inner_rest, right_full)
     squares = jnp.pad(jnp.sum(outer * outer, axis=(1, 2))[:, None] * jnp.ones((1, 128), f32), ((0, 3), (0, 0)))
     squares = chan_sum(squares, 6)[: 9 + tiles_one, 0]
     step = outer / jnp.sqrt(squares / (width * width) + 1e-06)[:, None, None]

time: 853 us -> 739 us (0.87)
  matrix products: 94.2 us -> 28.6 us
  Pallas kernels: 576 us -> 626 us
  local copies, waits for them, and re-layouts: 105 us -> 62 us
  other arithmetic: 50.2 us -> 11.1 us
  between operations: 15.2 us -> 1.26 us
    pallas_call x5 -> x1, Pallas kernels: 384 us -> 437 us  [local_step(): pl.pallas_call(step_kernel, out_shape=(shape((width, 9 * width), f32), sh...]
    conv_general_dilated x2 -> x0, matrix products: 31.3 us -> none  [conv_grid(): lax.conv_general_dilated(grid, taps, (1, 1), ((1, 1), (1, 1)), dimension_...]
    transpose x1 -> x0, matrix products: 16.8 us -> none  [body(): spatial_local.transpose(3, 0, 1, 2).reshape(width, 9 * width)]
    dot_general x9 -> x6, matrix products: 43.8 us -> 28.6 us  [product(): return jnp.einsum(spec, left, right, preferred_element_type=jnp.float32)]
    reduce_sum x6 -> x0, other arithmetic: 14.4 us -> none  [the longest x1 6.67 us: backward(): jnp.sum(d_pre, axis=(0, 1))]
    transpose x2 -> x1, local copies, waits for them, and re-layouts: 13.8 us -> 0.48 us  [body(): input_side_roots.astype(low).transpose(1, 0, 2).reshape(rows_out, -1)]
    convert_element_type x4 -> x1, other arithmetic: 12.1 us -> 0.01 us  [body(): (filled > 0.0).astype(f32)]
    slice x8 -> x2, local copies, waits for them, and re-layouts: 11.3 us -> 1.35 us  [the longest x1 0.77 us: body(): sums_two[:4]]
  transfers between devices with their start and end apart: 1 -> 0, of which waited for: 0 -> 0; matrix products, arithmetic and copies ran while one was open for 28% -> 0% of each run, Pallas kernels for 67% -> 0%
where the time goes in v2:
time: 739 us; the launch traced here: 729 us
  Pallas kernels  626 us (85%)
  local copies, waits for them, and re-layouts  62 us (8%)
  matrix products  28.6 us (4%)
  other arithmetic  11.1 us (2%)
    pallas_call x1, Pallas kernels, local_step(): pl.pallas_call(step_kernel, out_shape=(shape((width, 9 * width), f32), sh...  437 us
    pallas_call x1, Pallas kernels, settle(): pl.pallas_call(functools.partial(settle_kernel, wire), out_shape=(jax.Sha...  176 us
    dot_general x6, matrix products, product(): return jnp.einsum(spec, left, right, preferred_element_type=jnp.float32)  28.6 us
    another operation x2, local copies, waits for them, and re-layouts, body(): blocks_of = lambda a: a.reshape(a.shape[0], -1, width).transpose(1, 0, 2)  20.4 us

profile of v2, /device:TPU:0, one launch (start us, length us, event | category | flops | bytes accessed | tf_op | source)
XLA Modules:
  0.0 728.9 jit_solution(640883393734354792)
XLA Ops:
  0.7 0.9 convert_reduce_fusion
  3.0 0.9 convert_bitcast_fusion.1
  3.9 1.4 broadcast_in_dim.18.valid
  7.6 8.3 %copy.45 = bf16[8,48,49,256]{3,1,2,0:T(8,128)(2,1)} copy(bf16[8,48,49,256]{3,1,0,2:T(8,128)(2,1)} %bitcast.49) | data formatting | bytes 19267584 | tf_op jit(solution)/shard_map/reshape | solution.py:708
  16.6 1.5 reshape_reshape.9.roots
  18.2 0.9 copy-done.2
  19.4 1.0 fusion.13
  21.0 436.7 %step.1 = (f32[512,4608]{1,0:T(8,128)}, f32[512,2048]{1,0:T(8,128)}, f32[512,1024]{1,0:T(8,128)}, f32[24,128]{1,0:T(8,128)}, bf16[4,2,2,2,16,7680]{5,4,3,2,1,0:T...) custom-call(bf16[8,7,336,256]{3,2,1,0:T(8,128)(2,1)} %bitcast.46, bf16[2,2,16,7680]{3,2,1,0:T(8,128)(2,1)} %bitcast.57, ...), custom_call_target="tpu_custom_call" | custom-call | tf_op jit(solution)/shard_map/step/pallas_call | solution.py:450
  459.4 0.8 fusion.19.mask
  460.2 176.1 %settle.1 = (bf16[4,2,2,2,16,6656]{5,4,3,2,1,0:T(8,128)(2,1)}, f32[2,2,16,7680]{3,2,1,0:T(8,128)}) custom-call(f32[4,2,2,2,16,4608]{5,4,3,2,1,0:T(8,128)} %bitcast.50, f32[4,2,2,2,16,2048]{5,4,3,2,1,0:T(8,128)} %bitcast.52, f32[4,2,2,2,16,1024]{5,4,3,2,1,0:T(8,128)} %bitcast.62, f32[16,7680]{1,0:T(8,128)} %fusion.19.mask), custom_call_target="tpu_custom_call" | custom-call | tf_op jit(solution)/shard_map/settle/pallas_call | solution.py:623
  636.3 12.9 %reshape_reshape.10 = bf16[512,13,512]{2,1,0:T(8,128)(2,1)} reshape(bf16[4,2,2,2,16,6656]{5,4,3,2,1,0:T(8,128)(2,1)} %get-tuple-element.29) | data formatting | bytes 13631488 | tf_op jit(solution)/shard_map/reshape;reshape | solution.py:735
  649.3 7.5 %copy.68 = bf16[512,13,512]{2,0,1:T(8,128)(2,1)S(1)} copy(bf16[512,13,512]{2,1,0:T(8,128)(2,1)} %reshape_reshape.10) | data formatting | bytes 13631488 | tf_op jit(solution)/shard_map/reshape;reshape | solution.py:735
  657.2 1.3 copy-done.8
  658.5 3.0 multiply_add_fusion
  661.6 1.5 slice.104
  663.3 1.3 copy-done.22
  664.6 3.4 multiply_add_fusion.1
  667.9 1.2 fusion.14
  669.1 1.4 bitcast_add_fusion
  670.5 12.7 %reshape_reshape.11 = bf16[512,13,512]{2,1,0:T(8,128)(2,1)} reshape(bf16[4,2,2,2,16,6656]{5,4,3,2,1,0:T(8,128)(2,1)} %get-tuple-element.30) | data formatting | bytes 13631488 | tf_op jit(solution)/shard_map/reshape;reshape | solution.py:732
  683.2 10.8 %fusion = f32[13,64,512]{2,1,0:T(8,128)S(1)} fusion(bf16[512,13,512]{2,1,0:T(8,128)(2,1)} %reshape_reshape.11, f32[13,64,512]{2,1,0:T(8,128)S(1)} %bitcast_add_fusion), kind=kOutput, calls=%fused_computation.4 | convolution fusion | flops 437911552 | bytes 10223616 | tf_op jit(solution)/shard_map/tak,ktb->tab/dot_general | solution.py:663
  694.1 8.9 %multiply_reduce_fusion = (f32[13]{0:T(128)S(1)}, f32[13,64,512]{2,1,0:T(8,128)}) fusion(f32[13,64,512]{2,1,0:T(8,128)S(1)} %fusion, bf16[512,13,512]{2,1,0:T(8,128)(2,1)S(1)} %copy-done, f32[13,64,512]{2,1,0:T(8,128)S(1)} %bitcast_add_fusion), kind=kOutput, calls=%fused_computation.18 | convolution fusion | flops 437911552 | bytes 11927604 | tf_op jit(solution)/shard_map/tak,ktb->tab/dot_general | solution.py:663
  703.6 13.0 %chan_sum.1 = f32[16,128]{1,0:T(8,128)} custom-call(f32[16,128]{1,0:T(8,128)} %pad.22.own), custom_call_target="tpu_custom_call" | custom-call | tf_op jit(solution)/shard_map/chan_sum/pallas_call | solution.py:72
  716.6 0.8 sqrt_reduce_fusion
  717.4 1.7 broadcast_divide_fusion
  719.4 1.2 copy-done.4
  720.5 1.3 multiply_subtract_fusion
  721.9 0.9 copy-done.7
  722.9 0.9 multiply_subtract_fusion.1
  723.8 1.1 slice.86
  724.9 1.0 multiply_subtract_fusion.2
  725.9 0.8 slice.85
  (77 shorter events, 10.3 us)
Async XLA Ops:
  6.2 9.7 %copy-start.15 = (f32[8,512]{1,0:T(8,128)}, f32[8,512]{1,0:T(8,128)S(1)}, u32[]{:S(2)}) copy-start(f32[8,512]{1,0:T(8,128)S(1)} %dynamic_update_slice.3.norms) | copy-start | bytes 49156
  7.6 8.3 %copy-start.9 = (f32[13,64,512]{2,1,0:T(8,128)S(1)}, f32[13,64,512]{2,1,0:T(8,128)}, u32[]{:S(2)}) copy-start(f32[13,64,512]{2,1,0:T(8,128)} %param.33) | copy-start | bytes 5111812
  16.1 2.0 copy-start.1
  16.1 2.0 copy-start.3
  18.1 1.0 copy-start.2
  18.1 1.2 copy-start.6
  18.1 1.3 copy-start.11
  19.3 1.1 copy-start.16
  21.0 437.5 %copy-start.17 = (f32[4,64]{1,0:T(4,128)S(1)}, f32[4,64]{1,0:T(4,128)}, u32[]{:S(2)}) copy-start(f32[4,64]{1,0:T(4,128)} %param.29) | copy-start | bytes 3076
  21.0 437.5 %copy-start.20 = (f32[4,64]{1,0:T(4,128)S(1)}, f32[4,64]{1,0:T(4,128)}, u32[]{:S(2)}) copy-start(f32[4,64]{1,0:T(4,128)} %param.38) | copy-start | bytes 3076
  21.0 437.5 %copy-start.21 = (f32[4,64]{1,0:T(4,128)S(1)}, f32[4,64]{1,0:T(4,128)}, u32[]{:S(2)}) copy-start(f32[4,64]{1,0:T(4,128)} %param.39) | copy-start | bytes 3076
  657.1 1.5 copy-start.8
  663.1 1.5 copy-start.22
  664.6 3.4 copy-start.10
  683.2 10.8 %copy-start = (bf16[512,13,512]{2,1,0:T(8,128)(2,1)S(1)}, bf16[512,13,512]{2,1,0:T(8,128)(2,1)}, u32[]{:S(2)}) copy-start(bf16[512,13,512]{2,1,0:T(8,128)(2,1)} %reshape_reshape.11) | copy-start | bytes 20447236
  719.3 1.3 copy-start.4
  721.8 1.0 copy-start.7
  721.9 1.9 copy-start.5
  722.9 2.0 copy-start.12
  722.9 2.0 copy-start.13
  722.9 2.0 copy-start.14
  724.9 2.5 copy-start.18
  724.9 2.5 copy-start.19

commit v3 on v2

--- a/solution.py
+++ b/solution.py
@@ -101,7 +101,7 @@
     spatial_out, reduce_out, head_out, totals_out, weights_out, roots_out,
     own_images, first, second, hidden_pad, grad_pad, turned_grad, taps, reduce_low, head_low,
     norms_held, pack_one, pack_two, pack_three, pack_four, held_one, held_two, held_three, held_four,
-    partial, pooled_low, d_logits, d_act, head_buf, grad_buf, send, recv, local,
+    partial, pooling, pooled_low, d_logits, d_act, head_buf, grad_buf, send, recv, local,
 ):
     (z, y, x, core), (nz, ny, nx, nc) = place()
     c, n = lax.axis_index("chan"), lax.axis_size("chan")
@@ -122,19 +122,26 @@
     greet(everyone)
     copies = Copies(send, recv)
     others = turned(c, n)
-    sources = ((weights, weights_out), (roots, roots_out))
-
-    quarters = []
-    for i, (source, target) in enumerate(sources):
-        copy = pltpu.make_async_copy(source.at[x, core], target.at[z, y, x, core], local.at[i])
-        copy.start()
-        quarters.append(copy)
-    along_z = [[copies.start(source.at[x, core], target.at[z, y, x, core], at(k, y, x, core)) for k in turned(z, nz)]
-               for source, target in sources[:1]]
+    across_z = lax.rem(z + nz // 2, nz)
+    near_z = [z // (nz // 2) * (nz // 2) + lax.rem(lax.rem(z, nz // 2) + k, nz // 2) for k in range(1, nz // 2)]
+    mate, mate_y = at(z, y, x, 1 - core), at(z, 1 - y, x, core)
+    mates_x = [at(z, y, k, core) for k in turned(x, nx)]
+
+    def begin_z(source, target, sem):
+        keep = pltpu.make_async_copy(source.at[x, core], target.at[z, y, x, core], local.at[sem])
+        keep.start()
+        peers = [at(k, y, x, core) for k in [across_z] + near_z]
+        return [keep] + [copies.start(source.at[x, core], target.at[z, y, x, core], peer) for peer in peers]
+
+    def pass_z(target, begun):
+        for copy in begun:
+            copy.wait()
+        part = target.at[across_z, y, x, core]
+        return [copies.start(part, part, at(k, y, x, core)) for k in near_z]
+
+    weights_z = pass_z(weights_out, begin_z(weights, weights_out, 0))
     norm_copies = [copies.start(norms, norms_held.at[k + 1], {"chan": other}) for k, other in enumerate(others)]
     image_copies = [copies.start(images.at[k], own_images.at[c, :, pl.ds(0, line)], {"chan": k}) for k in others]
-    along_z += [[copies.start(source.at[x, core], target.at[z, y, x, core], at(k, y, x, core)) for k in turned(z, nz)]
-                for source, target in sources[1:]]
     own = pltpu.make_async_copy(images.at[c], own_images.at[c, :, pl.ds(0, line)], local.at[2])
     own.start()
     norms_held[0] = norms[...]
@@ -150,30 +157,26 @@
         for j in range(side):
             own_images[k, j, pl.ds(line, slots), :] = jnp.zeros((slots, depth), low)
 
-    for i, (source, target) in enumerate(sources):
-        quarters[i].wait()
-        for copy in along_z[i]:
-            copy.wait()
-        part = target.at[:, y, x, core]
-        along_y = copies.start(part, part, at(z, 1 - y, x, core))
-        along_y.wait()
-        part = target.at[:, :, x, core]
-        along_x = [copies.start(part, part, at(z, y, k, core)) for k in turned(x, nx)]
-        for copy in along_x:
-            copy.wait()
-        part = target.at[:, :, :, core]
-        copies.start(part, part, at(z, y, x, 1 - core)).wait()
-        if i == 0:
-            fetched = []
-            start = 0
-            for j, held in enumerate((taps, reduce_low, head_low)):
-                size = held.shape[-1]
-                copy = pltpu.make_async_copy(target.at[:, :, :, :, :, pl.ds(start, size)], held, local.at[3 + j])
-                copy.start()
-                fetched.append(copy)
-                start += size
-            for copy in fetched:
-                copy.wait()
+    for copy in weights_z:
+        copy.wait()
+    part = weights_out.at[:, y, x, core]
+    copies.start(part, part, mate_y).wait()
+    part = weights_out.at[:, :, x, core]
+    along_x = [copies.start(part, part, peer) for peer in mates_x]
+    for copy in along_x:
+        copy.wait()
+    part = weights_out.at[:, :, :, core]
+    copies.start(part, part, mate).wait()
+    fetched = []
+    start = 0
+    for j, held in enumerate((taps, reduce_low, head_low)):
+        size = held.shape[-1]
+        copy = pltpu.make_async_copy(weights_out.at[:, :, :, :, :, pl.ds(start, size)], held, local.at[3 + j])
+        copy.start()
+        fetched.append(copy)
+        start += size
+    for copy in fetched:
+        copy.wait()
     taps, reduce_low, head_low = (held.reshape(width, held.shape[-1]) for held in (taps, reduce_low, head_low))
     for copy in norm_copies:
         copy.wait()
@@ -252,6 +255,7 @@
         return mean, scale
 
     mean_one, scale_one = norm_of(stats)
+    roots_z = begin_z(roots, roots_out, 1)
 
     def activate(p, _):
         normed = (first[pixel_rows(p), :] - mean_one) * scale_one
@@ -273,24 +277,36 @@
         return 0
 
     lax.fori_loop(0, side, conv_line, 0)
+    roots_z = pass_z(roots_out, roots_z)
     norm_sums(second)
     pack_two[...] = jnp.concatenate([packed(total_of(0)), packed(total_of(1))], axis=0)
     stats = settled(exchange(pack_two, held_two), held_two)
     mean_two, scale_two = norm_of(stats)
-
-    def pool(p, sums):
-        pooled, slopes, slopes_normed = sums
+    for copy in roots_z:
+        copy.wait()
+    across_half = roots_out.shape[-1] // 2
+    left, right = pl.ds(0, across_half), pl.ds(across_half, across_half)
+    part = roots_out.at[:, y, x, core, :, left]
+    roots_a = [copies.start(part, part, peer) for peer in mates_x]
+    part = roots_out.at[:, y, x, core, :, right]
+    roots_b = [copies.start(part, part, mate_y)]
+
+    pooling[...] = jnp.zeros(pooling.shape, f32)
+
+    def pool(p, _):
         normed = (second[pixel_rows(p), :] - mean_two) * scale_two
         pre = gain_two * normed + shift_two
         sigma = sigmoid(pre)
         kept = across(valid[pixel_rows(p), :])
         slope = sigma * (1.0 + pre * (1.0 - sigma)) * kept
-        return pooled + pre * sigma * kept, slopes + slope, slopes_normed + slope * normed
-
-    nothing = jnp.zeros((slots, width), f32)
-    pooled, slopes, slopes_normed = lax.fori_loop(0, pixels, pool, (nothing, nothing, nothing))
+        pooling[0] += pre * sigma * kept
+        pooling[1] += slope
+        pooling[2] += slope * normed
+        return 0
+
+    lax.fori_loop(0, pixels, pool, 0)
     divide = across(divisor[...])
-    pooled_low[...] = (pooled / divide).astype(low)
+    pooled_low[...] = (pooling[0] / divide).astype(low)
     logits = dot(pooled_low[...], head_low[...], 1, 0) + bias[...]
     classes = logits.shape[1]
     index = lax.broadcasted_iota(jnp.int32, (slots, classes), 1)
@@ -313,8 +329,8 @@
     at_class = lax.broadcasted_iota(jnp.int32, (1, classes), 1)
     bias_sum = jnp.where(at_class == classes - 1, loss, jnp.where(at_class == classes - 2, jnp.sum(use), bias_sum))
     pack_three[...] = jnp.concatenate(
-        [packed(jnp.sum(d_act[...] * slopes, axis=0, keepdims=True)),
-         packed(jnp.sum(d_act[...] * slopes_normed, axis=0, keepdims=True)), packed(bias_sum)], axis=0)
+        [packed(jnp.sum(d_act[...] * pooling[1], axis=0, keepdims=True)),
+         packed(jnp.sum(d_act[...] * pooling[2], axis=0, keepdims=True)), packed(bias_sum)], axis=0)
     going = exchange(pack_three, held_three)
 
     def to_head(m, _):
@@ -328,6 +344,14 @@
     totals_two = settled(going, held_three)
     shift_grad, gain_grad = unpacked(totals_two[:rows]), unpacked(totals_two[rows : 2 * rows])
     factor = gain_two * scale_two / count
+    for copy in roots_a:
+        copy.wait()
+    part = roots_out.at[:, y, :, core, :, left]
+    roots_a = [copies.start(part, part, mate_y)]
+    for copy in roots_b:
+        copy.wait()
+    part = roots_out.at[:, :, x, core, :, right]
+    roots_b = [copies.start(part, part, peer) for peer in mates_x]
 
     def leave_second(p, _):
         normed = (second[pixel_rows(p), :] - mean_two) * scale_two
@@ -354,6 +378,10 @@
         return 0
 
     lax.fori_loop(0, side, spread_line, 0)
+    for copy in roots_a + roots_b:
+        copy.wait()
+    part = roots_out.at[:, :, :, core]
+    roots_core = copies.start(part, part, mate)
 
     def enter_first(p, _):
         normed = (first[pixel_rows(p), :] - mean_one) * scale_one
@@ -389,12 +417,7 @@
             leaving[t - 2].wait()
         shifted = hidden_pad.at[pl.ds(rim + offset, body_rows)]
 
-        def tap_rows(m, _, slot=slot, shifted=shifted):
-            rows_out = pl.ds(pl.multiple_of(m * 256, 256), 256)
-            grad_buf[slot, rows_out, :] = dot(turned_grad[rows_out, :], shifted[...], 1, 0)
-            return 0
-
-        lax.fori_loop(0, width // 256, tap_rows, 0)
+        grad_buf[slot] = dot(turned_grad[...], shifted[...], 1, 0)
         leaving.append(leave(slot, spatial_out.at[:, pl.ds(t * width, width)], 7 + slot))
 
     totals_one = settled(going, held_four)
@@ -426,6 +449,7 @@
         leaving.append(leave(slot, reduce_out.at[:, pl.ds(t * width, width)], 7 + slot))
     totals_out[...] = jnp.concatenate([totals_two, totals_one], axis=0)
     head_copy.wait()
+    roots_core.wait()
     for copy in leaving[-2:]:
         copy.wait()
 
@@ -443,7 +467,7 @@
     quarters = lambda a: a.reshape(nx, 2, rows, a.shape[1])
     held = lambda k: pltpu.VMEM((n * nb, k, 128), f32)
     pack = lambda k: pltpu.VMEM((k, 128), f32)
-    count = 2 * (nz - 1) + 2 * (n - 1) + 2 * (1 + (nx - 1) + 1) + 4 * (n * nb - 1)
+    count = 2 * (nz - 1) + 2 * (n - 1) + (1 + (nx - 1) + 1) + (2 * nx + 1) + 4 * (n * nb - 1)
     two = 2 * width // 128
     three = two + classes // 128
     weight = lambda size: pltpu.VMEM((nz, 2, nx, 2, rows, size), low)
@@ -471,6 +495,7 @@
             pack(two + 8), pack(two), pack(three), pack(two),
             held(two + 8), held(two), held(three), held(two),
             pltpu.VMEM((2, 8, width), f32),
+            pltpu.VMEM((3, slots, width), f32),
             pltpu.VMEM((slots, width), low),
             pltpu.VMEM((slots, classes), low),
             pltpu.VMEM((slots, width), f32),
@@ -484,153 +509,179 @@
     return spatial, reduce, head, totals[:three], totals[three:], roots_full.reshape(width, roots.shape[1])
 
 
-def settle_kernel(wire, spatial, reduce, head, mask, full, own, sums_a, sums_b, core_a, core_b, x_a, x_b, y_a, y_b,
-                  z_a, z_b, sx_a, sx_b, sy_a, sy_b, sz_a, sz_b, final, final_low, send, recv, local):
+def settle_kernel(
+    chunks, spatial, reduce, head, mask, full, own, sums, core_in, first_in, first_out, second_in, near_in, across_in,
+    final, final_low, send, recv, local,
+):
     (z, y, x, core), (nz, ny, nx, nc) = place()
-    greet([at(k, y, x, core) for k in turned(z, nz)] + [at(z, 1 - y, x, core)]
-          + [at(z, y, k, core) for k in turned(x, nx)] + [at(z, y, x, 1 - core)])
+    half = nz // 2
+    across_z = lax.rem(z + half, nz)
+    base_z = z // half * half
+    near_z = [base_z + lax.rem(lax.rem(z, half) + k, half) for k in range(1, half)]
+    others_x = turned(x, nx)
+    mate, mate_y = at(z, y, x, 1 - core), at(z, 1 - y, x, core)
+    mates_x = [at(z, y, k, core) for k in others_x]
+    mates_near = [at(k, y, x, core) for k in near_z]
+    mate_across = at(across_z, y, x, core)
+    greet([mate, mate_y, mate_across] + mates_x + mates_near)
     copies = Copies(send, recv)
-    half = sums_a.shape[-1]
-    tail = spatial.shape[-1] - half
-    mate, mate_y = at(z, y, x, 1 - core), at(z, 1 - y, x, core)
-    mates_x, mates_z = turned(x, nx), turned(z, nz)
-    groups = [(i, j, k) for i in range(nz) for j in range(ny) for k in range(nx)]
-    pieces_a = [(spatial.at[:, :, :, :, :, pl.ds(0, half)], 0, half)]
-    pieces_b = [(spatial.at[:, :, :, :, :, pl.ds(half, tail)], 0, tail), (reduce, tail, reduce.shape[-1]),
-                (head, tail + reduce.shape[-1], head.shape[-1])]
-
-    def begin(pieces, sums, landing, sem):
-        remote, kept = [], []
-        for source, start, size in pieces:
-            columns = pl.ds(start, size)
-            remote.append(copies.start(source.at[:, :, :, 1 - core], landing.at[:, :, :, :, columns], mate))
-            copy = pltpu.make_async_copy(source.at[:, :, :, core], sums.at[:, :, :, :, columns], local.at[sem + len(kept)])
-            copy.start()
-            kept.append(copy)
-        return remote + kept
-
-    def ship(source, staged, landing, peer):
-        if staged.dtype == jnp.float32:
-            return copies.start(source, landing, peer)
-        for i in range(staged.shape[0]):
-            staged[i] = source[i].astype(staged.dtype)
-        return copies.start(staged, landing, peer)
-
-    def add(sums, landing):
-        for i in range(landing.shape[0]):
-            sums[i] += landing[i].astype(jnp.float32)
-
-    first_a = begin(pieces_a, sums_a, core_a, 0)
-    first_b = begin(pieces_b, sums_b, core_b, len(pieces_a))
-    for first, sums, landing in ((first_a, sums_a, core_a), (first_b, sums_b, core_b)):
-        for copy in first:
-            copy.wait()
-        for i, j, k in groups:
-            sums[i, j, k] += landing[i, j, k]
-        if sums is sums_a:
-            going_a = []
-            for t, k in enumerate(mates_x):
-                for j in range(ny):
-                    going_a.append(ship(sums.at[:, j, k], sx_a.at[t, j], x_a.at[t, j], at(z, y, k, core)))
-        else:
-            going_b = [ship(sums.at[:, 1 - y, k], sy_b.at[k], y_b.at[k], mate_y) for k in range(nx)]
-    for copy in going_a:
-        copy.wait()
-    for t in range(nx - 1):
-        for j in range(ny):
-            add(sums_a.at[:, j, x], x_a.at[t, j])
-    going_a = [ship(sums_a.at[:, 1 - y, x], sy_a, y_a, mate_y)]
-    for copy in going_b:
-        copy.wait()
-    for k in range(nx):
-        add(sums_b.at[:, y, k], y_b.at[k])
-    going_b = [ship(sums_b.at[:, y, k], sx_b.at[t], x_b.at[t], at(z, y, k, core)) for t, k in enumerate(mates_x)]
-    for copy in going_a:
-        copy.wait()
-    add(sums_a.at[:, y, x], y_a)
-    going_a = [ship(sums_a.at[pl.ds(k, 1), y, x], sz_a.at[pl.ds(t, 1)], z_a.at[pl.ds(t, 1)], at(k, y, x, core))
-               for t, k in enumerate(mates_z)]
-    for copy in going_b:
-        copy.wait()
-    for t in range(nx - 1):
-        add(sums_b.at[:, y, x], x_b.at[t])
-    going_b = [ship(sums_b.at[pl.ds(k, 1), y, x], sz_b.at[pl.ds(t, 1)], z_b.at[pl.ds(t, 1)], at(k, y, x, core))
-               for t, k in enumerate(mates_z)]
-    for going, sums, landing, start in ((going_a, sums_a, z_a, 0), (going_b, sums_b, z_b, half)):
+    f32 = jnp.float32
+    sources = ((spatial, 0), (reduce, spatial.shape[-1]), (head, spatial.shape[-1] + reduce.shape[-1]))
+    wide = full.shape[-1]
+    used_local = [0]
+
+    def keep(source, target):
+        copy = pltpu.make_async_copy(source, target, local.at[used_local[0]])
+        used_local[0] += 1
+        copy.start()
+        return copy
+
+    def wait(going):
         for copy in going:
             copy.wait()
-        value = sums[z, y, x]
-        for t in range(nz - 1):
-            value = value + landing[t].astype(jnp.float32)
-        columns = pl.ds(start, half)
-        final[:, columns] = value * mask[:, columns]
-
-    wide = full.shape[-1]
-    final_low[...] = final[:, :wide].astype(final_low.dtype)
-    keep = pltpu.make_async_copy(final_low, full.at[z, y, x, core], local.at[4])
-    keep.start()
-    keep_own = pltpu.make_async_copy(final, own.at[x, core], local.at[5])
-    keep_own.start()
-    up = [copies.start(final_low, full.at[z, y, x, core], at(k, y, x, core)) for k in mates_z]
-    rows_x = [copies.start(final, own.at[x, core], at(z, y, k, core)) for k in mates_x]
-    keep.wait()
-    for copy in up:
-        copy.wait()
-    left, right = pl.ds(0, wide // 2), pl.ds(wide // 2, wide // 2)
-    part = full.at[:, y, x, core, :, left]
-    going_a = [copies.start(part, part, at(z, y, k, core)) for k in mates_x]
-    part = full.at[:, y, x, core, :, right]
-    going_b = [copies.start(part, part, mate_y)]
-    keep_own.wait()
-    for copy in rows_x:
-        copy.wait()
-    part = own.at[:, core]
-    rows_core = copies.start(part, part, mate)
-    for copy in going_a:
-        copy.wait()
-    part = full.at[:, y, :, core, :, left]
-    going_a = [copies.start(part, part, mate_y)]
-    for copy in going_b:
-        copy.wait()
-    part = full.at[:, :, x, core, :, right]
-    going_b = [copies.start(part, part, at(z, y, k, core)) for k in mates_x]
-    for copy in going_a:
-        copy.wait()
-    part = full.at[:, :, :, core, :, left]
-    last = [copies.start(part, part, mate)]
-    for copy in going_b:
-        copy.wait()
-    part = full.at[:, :, :, core, :, right]
-    last += [copies.start(part, part, mate), rows_core]
-    for copy in last:
-        copy.wait()
-
-
-def settle(spatial, reduce, head, mask, wire):
+
+    def chunk(start, size, x_first):
+        columns = pl.ds(start, size)
+        going = []
+        for source, first_column in sources:
+            begin, end = max(start, first_column), min(start + size, first_column + source.shape[-1])
+            if begin < end:
+                taken, landed = pl.ds(begin - first_column, end - begin), pl.ds(begin, end - begin)
+                going.append(copies.start(source.at[:, :, :, 1 - core, :, taken], core_in.at[:, :, :, :, landed], mate))
+                going.append(keep(source.at[:, :, :, core, :, taken], sums.at[:, :, :, :, landed]))
+        yield
+        wait(going)
+        for i in range(nz):
+            for j in range(ny):
+                for k in range(nx):
+                    sums[i, j, k, :, columns] += core_in[i, j, k, :, columns]
+        going = []
+        if x_first:
+            for t, k in enumerate(others_x):
+                for i in range(nz):
+                    for j in range(ny):
+                        first_out[t, i, j, :, columns] = sums[i, j, k, :, columns].astype(first_out.dtype)
+                going.append(copies.start(first_out.at[t, :, :, :, columns], first_in.at[t, :, :, :, columns], mates_x[t]))
+        else:
+            for i in range(nz):
+                for k in range(nx):
+                    first_out[k // ny, i, k % ny, :, columns] = sums[i, 1 - y, k, :, columns].astype(first_out.dtype)
+            for t in range(nx // ny):
+                going.append(copies.start(first_out.at[t, :, :, :, columns], first_in.at[t, :, :, :, columns], mate_y))
+        yield
+        wait(going)
+        going = []
+        if x_first:
+            for t in range(nx - 1):
+                for i in range(nz):
+                    for j in range(ny):
+                        sums[i, j, x, :, columns] += first_in[t, i, j, :, columns].astype(f32)
+            going.append(copies.start(sums.at[:, 1 - y, x, :, columns], second_in.at[0, :, :, columns], mate_y))
+        else:
+            for i in range(nz):
+                for k in range(nx):
+                    sums[i, y, k, :, columns] += first_in[k // ny, i, k % ny, :, columns].astype(f32)
+            for t, k in enumerate(others_x):
+                going.append(copies.start(sums.at[:, y, k, :, columns], second_in.at[t, :, :, columns], mates_x[t]))
+        yield
+        wait(going)
+        for t in range(1 if x_first else nx - 1):
+            for i in range(nz):
+                sums[i, y, x, :, columns] += second_in[t, i, :, columns]
+        going = []
+        for t, k in enumerate(near_z):
+            for h in range(2):
+                there = lax.rem(k + h * half, nz)
+                going.append(copies.start(sums.at[there, y, x, :, columns], near_in.at[t, h, :, columns], mates_near[t]))
+        yield
+        wait(going)
+        for t in range(half - 1):
+            for h in range(2):
+                sums[lax.rem(z + h * half, nz), y, x, :, columns] += near_in[t, h, :, columns]
+        going = [copies.start(sums.at[across_z, y, x, :, columns], across_in.at[:, columns], mate_across)]
+        yield
+        wait(going)
+        total = (sums[z, y, x, :, columns] + across_in[:, columns]) * mask[:, columns]
+        final[:, columns] = total
+        kept = keep(final.at[:, columns], own.at[x, core, :, columns])
+        rows_x = [copies.start(final.at[:, columns], own.at[x, core, :, columns], peer) for peer in mates_x]
+        low_size = min(start + size, wide) - start
+        if low_size > 0:
+            low_columns = pl.ds(start, low_size)
+            final_low[:, low_columns] = total[:, :low_size].astype(final_low.dtype)
+            source = final_low.at[:, low_columns]
+            place_at = full.at[z, y, x, core, :, low_columns]
+            going = [keep(source, place_at)] + [copies.start(source, place_at, peer) for peer in [mate_across] + mates_near]
+        yield
+        wait([kept] + rows_x)
+        part = own.at[:, core, :, columns]
+        rows_core = [copies.start(part, part, mate)]
+        if low_size > 0:
+            wait(going)
+            part = full.at[across_z, y, x, core, :, low_columns]
+            going = [copies.start(part, part, peer) for peer in mates_near]
+            yield
+            wait(going)
+            part = full.at[:, y, x, core, :, low_columns]
+            going = [copies.start(part, part, peer) for peer in (mates_x if x_first else [mate_y])]
+            yield
+            wait(going)
+            part = full.at[:, y, :, core, :, low_columns] if x_first else full.at[:, :, x, core, :, low_columns]
+            going = [copies.start(part, part, peer) for peer in ([mate_y] if x_first else mates_x)]
+            yield
+            wait(going)
+            part = full.at[:, :, :, core, :, low_columns]
+            rows_core.append(copies.start(part, part, mate))
+        yield
+        wait(rows_core)
+
+    waiting, active = [chunk(*c) for c in chunks], []
+    while waiting or active:
+        for _ in range(2):
+            if waiting:
+                active.append(waiting.pop(0))
+        for going in list(active):
+            try:
+                next(going)
+            except StopIteration:
+                active.remove(going)
+
+
+def settle(spatial, reduce, head, mask, wire, pairs):
     nz, nx = lax.axis_size("chan") // 2, lax.axis_size("batch") // 2
     width = spatial.shape[0]
     rows = width // (4 * nz * nx)
     total = spatial.shape[1] + reduce.shape[1] + head.shape[1]
-    wide, half = spatial.shape[1] + reduce.shape[1], total // 2
+    wide = spatial.shape[1] + reduce.shape[1]
     split = lambda a: a.reshape(nz, 2, nx, 2, rows, a.shape[1])
-    f32 = jnp.float32
-    big = pltpu.VMEM((nz, 2, nx, rows, half), f32)
-    shapes = [(nx - 1, 2, nz, rows, half), (nx - 1, nz, rows, half), (nz, rows, half), (nx, nz, rows, half),
-              (nz - 1, rows, half), (nz - 1, rows, half)]
-    landing = [pltpu.VMEM(s, wire) for s in shapes]
-    staging = [pltpu.VMEM(s if wire != f32 else s[:-2] + (8, 128), wire) for s in shapes]
-    count = 4 + 2 * (nx - 1) + nx + 1 + (nx - 1) + 2 * (nz - 1) + (nz - 1) + (nx - 1) + 2 * nx + 1 + 2
+    f32, low = jnp.float32, jnp.bfloat16
+    cuts = [128 * (total // 128 * i // (2 * pairs)) for i in range(2 * pairs + 1)]
+    chunks = [(a, b - a, i % 2 == 0) for i, (a, b) in enumerate(zip(cuts[:-1], cuts[1:]))]
+    first = max(nx - 1, nx // 2)
+    near = nz // 2 - 1
+    count = len(chunks) * (max(nx - 1, nx // 2) + max(nx - 1, 1) + 2 * near + 1 + (nx - 1) + 1 + near + 1 + near + nx + 1)
+    count += len(chunks) + 3
     full, own = pl.pallas_call(
-        functools.partial(settle_kernel, wire),
+        functools.partial(settle_kernel, chunks),
         out_shape=(
-            jax.ShapeDtypeStruct((nz, 2, nx, 2, rows, wide), jnp.bfloat16),
+            jax.ShapeDtypeStruct((nz, 2, nx, 2, rows, wide), low),
             jax.ShapeDtypeStruct((nx, 2, rows, total), f32),
         ),
         in_specs=[ANY, ANY, ANY, VMEM],
         out_specs=(ANY, ANY),
-        scratch_shapes=[big, big, big, big] + landing + staging
-        + [pltpu.VMEM((rows, total), f32), pltpu.VMEM((rows, wide), jnp.bfloat16), DMA((count,)), DMA((count,)), DMA((6,))],
-        compiler_params=pltpu.CompilerParams(collective_id=1, has_side_effects=True, vmem_limit_bytes=56 << 20),
+        scratch_shapes=[
+            pltpu.VMEM((nz, 2, nx, rows, total), f32),
+            pltpu.VMEM((nz, 2, nx, rows, total), f32),
+            pltpu.VMEM((first, nz, 2, rows, total), wire),
+            pltpu.VMEM((first, nz, 2, rows, total), wire),
+            pltpu.VMEM((max(nx - 1, 1), nz, rows, total), f32),
+            pltpu.VMEM((near, 2, rows, total), f32),
+            pltpu.VMEM((rows, total), f32),
+            pltpu.VMEM((rows, total), f32),
+            pltpu.VMEM((rows, wide), low),
+            DMA((count,)), DMA((count,)), DMA((3 * len(chunks) + 3,)),
+        ],
+        compiler_params=pltpu.CompilerParams(collective_id=1, has_side_effects=True, vmem_limit_bytes=58 << 20),
         name="settle",
     )(split(spatial), split(reduce), split(head), mask)
     return full.reshape(width, wide), own.reshape(2 * nx * rows, total)
@@ -720,7 +771,7 @@
         jnp.pad(head_bias, (0, padded - classes), constant_values=-1e30)[None])
 
     mask_rows = jnp.concatenate([spatial_float, reduce_float, jnp.ones((rows_out, padded), f32)], axis=1)
-    full, own = settle(spatial_local, reduce_local, head_local, own_part(mask_rows, 0, "batch"), jnp.float32)
+    full, own = settle(spatial_local, reduce_local, head_local, own_part(mask_rows, 0, "batch"), jnp.float32, 6)
     spatial_grad = own[:, : 9 * width]
     reduce_grad = own[:, 9 * width : 9 * width + c_in]
     head_grad = own[:, 9 * width + c_in : 9 * width + c_in + classes]
@@ -985,5 +1036,5 @@
         P(None, "chan"),
     )
     chan, batch = mesh.shape["chan"], mesh.shape["batch"]
-    fits = chan % 2 == 0 and batch % 2 == 0 and WIDTH % (16 * chan * batch) == 0 and SLOTS_DEV % (16 * chan) == 0
+    fits = chan % 4 == 0 and batch % 2 == 0 and WIDTH % (16 * chan * batch) == 0 and SLOTS_DEV % (16 * chan) == 0
     return jax.shard_map(body if fits else plain_body, mesh=mesh, in_specs=in_specs, out_specs=out_specs, check_vma=False)

time: 739 us -> 585 us (0.79)
  Pallas kernels: 626 us -> 475 us
    pallas_call x1, Pallas kernels: 437 us -> 344 us  [local_step(): pl.pallas_call(step_kernel, out_shape=(shape((width, 9 * width), f32), sh...]
    pallas_call x1, Pallas kernels: 176 us -> 122 us  [settle(): pl.pallas_call(functools.partial(settle_kernel, chunks), out_shape=(jax.S...]
where the time goes in v3:
time: 585 us; the launch traced here: 578 us
  Pallas kernels  475 us (81%)
  local copies, waits for them, and re-layouts  62 us (11%)
  matrix products  28.6 us (5%)
  other arithmetic  11.1 us (2%)
    pallas_call x1, Pallas kernels, local_step(): pl.pallas_call(step_kernel, out_shape=(shape((width, 9 * width), f32), sh...  344 us
    pallas_call x1, Pallas kernels, settle(): pl.pallas_call(functools.partial(settle_kernel, chunks), out_shape=(jax.S...  122 us
    dot_general x6, matrix products, product(): return jnp.einsum(spec, left, right, preferred_element_type=jnp.float32)  28.6 us
    another operation x2, local copies, waits for them, and re-layouts, body(): blocks_of = lambda a: a.reshape(a.shape[0], -1, width).transpose(1, 0, 2)  20.4 us
    another operation x1, local copies, waits for them, and re-layouts, body(): right_full = roots_full.reshape(width, -1, width)  12.7 us

profile of v3, /device:TPU:0, one launch (start us, length us, event | category | flops | bytes accessed | tf_op | source)
XLA Modules:
  0.0 577.6 jit_solution(7829006508067741811)
XLA Ops:
  0.7 0.9 convert_reduce_fusion
  3.0 0.9 convert_bitcast_fusion.1
  3.9 1.4 broadcast_in_dim.18.valid
  7.6 8.3 %copy.45 = bf16[8,48,49,256]{3,1,2,0:T(8,128)(2,1)} copy(bf16[8,48,49,256]{3,1,0,2:T(8,128)(2,1)} %bitcast.49) | data formatting | bytes 19267584 | tf_op jit(solution)/shard_map/reshape | solution.py:759
  16.6 1.5 reshape_reshape.9.roots
  18.2 0.9 copy-done.2
  19.4 1.0 fusion.13
  21.0 344.2 %step.1 = (f32[512,4608]{1,0:T(8,128)}, f32[512,2048]{1,0:T(8,128)}, f32[512,1024]{1,0:T(8,128)}, f32[24,128]{1,0:T(8,128)}, bf16[4,2,2,2,16,7680]{5,4,3,2,1,0:T...) custom-call(bf16[8,7,336,256]{3,2,1,0:T(8,128)(2,1)} %bitcast.46, bf16[2,2,16,7680]{3,2,1,0:T(8,128)(2,1)} %bitcast.57, ...), custom_call_target="tpu_custom_call" | custom-call | tf_op jit(solution)/shard_map/step/pallas_call | solution.py:474
  366.9 0.8 fusion.19.mask
  367.7 122.1 %settle.1 = (bf16[4,2,2,2,16,6656]{5,4,3,2,1,0:T(8,128)(2,1)}, f32[2,2,16,7680]{3,2,1,0:T(8,128)}) custom-call(f32[4,2,2,2,16,4608]{5,4,3,2,1,0:T(8,128)} %bitcast.50, f32[4,2,2,2,16,2048]{5,4,3,2,1,0:T(8,128)} %bitcast.52, f32[4,2,2,2,16,1024]{5,4,3,2,1,0:T(8,128)} %bitcast.62, f32[16,7680]{1,0:T(8,128)} %fusion.19.mask), custom_call_target="tpu_custom_call" | custom-call | tf_op jit(solution)/shard_map/settle/pallas_call | solution.py:664
  489.8 12.9 %reshape_reshape.10 = bf16[512,13,512]{2,1,0:T(8,128)(2,1)} reshape(bf16[4,2,2,2,16,6656]{5,4,3,2,1,0:T(8,128)(2,1)} %get-tuple-element.29) | data formatting | bytes 13631488 | tf_op jit(solution)/shard_map/reshape;reshape | solution.py:786
  502.8 7.5 %copy.68 = bf16[512,13,512]{2,0,1:T(8,128)(2,1)S(1)} copy(bf16[512,13,512]{2,1,0:T(8,128)(2,1)} %reshape_reshape.10) | data formatting | bytes 13631488 | tf_op jit(solution)/shard_map/reshape;reshape | solution.py:786
  510.7 1.3 copy-done.8
  512.0 3.0 multiply_add_fusion
  515.1 1.5 slice.104
  516.8 1.3 copy-done.22
  518.1 3.4 multiply_add_fusion.1
  521.4 1.2 fusion.14
  522.6 1.4 bitcast_add_fusion
  524.0 12.7 %reshape_reshape.11 = bf16[512,13,512]{2,1,0:T(8,128)(2,1)} reshape(bf16[4,2,2,2,16,6656]{5,4,3,2,1,0:T(8,128)(2,1)} %get-tuple-element.30) | data formatting | bytes 13631488 | tf_op jit(solution)/shard_map/reshape;reshape | solution.py:783
  536.7 10.8 %fusion = f32[13,64,512]{2,1,0:T(8,128)S(1)} fusion(bf16[512,13,512]{2,1,0:T(8,128)(2,1)} %reshape_reshape.11, f32[13,64,512]{2,1,0:T(8,128)S(1)} %bitcast_add_fusion), kind=kOutput, calls=%fused_computation.4 | convolution fusion | flops 437911552 | bytes 10223616 | tf_op jit(solution)/shard_map/tak,ktb->tab/dot_general | solution.py:714
  547.6 8.9 %multiply_reduce_fusion = (f32[13]{0:T(128)S(1)}, f32[13,64,512]{2,1,0:T(8,128)}) fusion(f32[13,64,512]{2,1,0:T(8,128)S(1)} %fusion, bf16[512,13,512]{2,1,0:T(8,128)(2,1)S(1)} %copy-done, f32[13,64,512]{2,1,0:T(8,128)S(1)} %bitcast_add_fusion), kind=kOutput, calls=%fused_computation.18 | convolution fusion | flops 437911552 | bytes 11927604 | tf_op jit(solution)/shard_map/tak,ktb->tab/dot_general | solution.py:714
  557.1 8.2 %chan_sum.1 = f32[16,128]{1,0:T(8,128)} custom-call(f32[16,128]{1,0:T(8,128)} %pad.22.own), custom_call_target="tpu_custom_call" | custom-call | tf_op jit(solution)/shard_map/chan_sum/pallas_call | solution.py:72
  565.3 0.8 sqrt_reduce_fusion
  566.2 1.7 broadcast_divide_fusion
  568.1 1.2 copy-done.4
  569.3 1.3 multiply_subtract_fusion
  570.7 0.9 copy-done.7
  571.6 0.9 multiply_subtract_fusion.1
  572.5 1.1 slice.86
  573.6 1.0 multiply_subtract_fusion.2
  574.6 0.8 slice.85
  (77 shorter events, 10.3 us)
Async XLA Ops:
  6.2 9.7 %copy-start.15 = (f32[8,512]{1,0:T(8,128)}, f32[8,512]{1,0:T(8,128)S(1)}, u32[]{:S(2)}) copy-start(f32[8,512]{1,0:T(8,128)S(1)} %dynamic_update_slice.3.norms) | copy-start | bytes 49156
  7.6 8.3 %copy-start.9 = (f32[13,64,512]{2,1,0:T(8,128)S(1)}, f32[13,64,512]{2,1,0:T(8,128)}, u32[]{:S(2)}) copy-start(f32[13,64,512]{2,1,0:T(8,128)} %param.33) | copy-start | bytes 5111812
  16.1 2.0 copy-start.1
  16.1 2.0 copy-start.3
  18.1 1.0 copy-start.2
  18.1 1.2 copy-start.6
  18.1 1.3 copy-start.11
  19.3 1.1 copy-start.16
  21.0 345.0 %copy-start.17 = (f32[4,64]{1,0:T(4,128)S(1)}, f32[4,64]{1,0:T(4,128)}, u32[]{:S(2)}) copy-start(f32[4,64]{1,0:T(4,128)} %param.29) | copy-start | bytes 3076
  21.0 345.0 %copy-start.20 = (f32[4,64]{1,0:T(4,128)S(1)}, f32[4,64]{1,0:T(4,128)}, u32[]{:S(2)}) copy-start(f32[4,64]{1,0:T(4,128)} %param.38) | copy-start | bytes 3076
  21.0 345.0 %copy-start.21 = (f32[4,64]{1,0:T(4,128)S(1)}, f32[4,64]{1,0:T(4,128)}, u32[]{:S(2)}) copy-start(f32[4,64]{1,0:T(4,128)} %param.39) | copy-start | bytes 3076
  510.6 1.5 copy-start.8
  516.6 1.5 copy-start.22
  518.1 3.4 copy-start.10
  536.7 10.8 %copy-start = (bf16[512,13,512]{2,1,0:T(8,128)(2,1)S(1)}, bf16[512,13,512]{2,1,0:T(8,128)(2,1)}, u32[]{:S(2)}) copy-start(bf16[512,13,512]{2,1,0:T(8,128)(2,1)} %reshape_reshape.11) | copy-start | bytes 20447236
  568.0 1.3 copy-start.4
  570.6 1.0 copy-start.7
  570.6 1.9 copy-start.5
  571.6 2.0 copy-start.12
  571.6 2.0 copy-start.13
  571.6 2.0 copy-start.14
  573.6 2.5 copy-start.18
  573.6 2.5 copy-start.19

commit v4 on v3

--- a/solution.py
+++ b/solution.py
@@ -10,6 +10,7 @@
 SIDE = 7
 SLOTS_DEV = 384
 STEP = 10
+ORDERS = ("xyz", "xy")
 
 WIDTH = 512
 EPS = 1e-05
@@ -53,31 +54,6 @@
         self.used += 1
         copy.start()
         return copy
-
-
-def chan_sum_kernel(own, total, held, send, recv):
-    c, n = lax.axis_index("chan"), lax.axis_size("chan")
-    peers = [{"chan": other} for other in turned(c, n)]
-    greet(peers)
-    copies = Copies(send, recv)
-    started = [copies.start(own, held.at[k + 1], peer) for k, peer in enumerate(peers)]
-    held[0] = own[...]
-    for copy in started:
-        copy.wait()
-    total[...] = jnp.sum(held[...], axis=0)
-
-
-def chan_sum(rows, cid):
-    n = lax.axis_size("chan")
-    return pl.pallas_call(
-        chan_sum_kernel,
-        out_shape=jax.ShapeDtypeStruct(rows.shape, jnp.float32),
-        in_specs=[VMEM],
-        out_specs=VMEM,
-        scratch_shapes=[pltpu.VMEM((n,) + rows.shape, jnp.float32), DMA((n - 1,)), DMA((n - 1,))],
-        compiler_params=pltpu.CompilerParams(collective_id=cid, has_side_effects=True),
-        name="chan_sum",
-    )(rows)
 
 
 def dot(left, right, left_dim, right_dim):
@@ -141,7 +117,8 @@
 
     weights_z = pass_z(weights_out, begin_z(weights, weights_out, 0))
     norm_copies = [copies.start(norms, norms_held.at[k + 1], {"chan": other}) for k, other in enumerate(others)]
-    image_copies = [copies.start(images.at[k], own_images.at[c, :, pl.ds(0, line)], {"chan": k}) for k in others]
+    image_copies = [[copies.start(images.at[k, j], own_images.at[c, j, pl.ds(0, line)], {"chan": k}) for k in others]
+                    for j in range(side)]
     own = pltpu.make_async_copy(images.at[c], own_images.at[c, :, pl.ds(0, line)], local.at[2])
     own.start()
     norms_held[0] = norms[...]
@@ -212,26 +189,7 @@
             copy.wait()
         return jnp.sum(held[...], axis=0)
 
-    for k in range(n):
-        source = lax.rem(c + n - k, n)
-        if k == 0:
-            own.wait()
-        else:
-            image_copies[k - 1].wait()
-        columns = pl.ds(pl.multiple_of(source * depth, depth), depth)
-
-        def reduce_line(j, _, k=k, source=source, columns=columns):
-            value = dot(own_images[source, j, pl.ds(0, line), :], reduce_low[:, columns], 1, 1)
-            if k:
-                value = first[line_rows(j), :] + value
-            first[line_rows(j), :] = value
-            return 0
-
-        lax.fori_loop(0, side, reduce_line, 0)
-
-    def norm_sums(ref):
-        partial[...] = jnp.zeros(partial.shape, f32)
-
+    def add_to_sums(ref):
         def add(p, _):
             value = ref[pixel_rows(p), :]
             kept = value * across(valid[pixel_rows(p), :])
@@ -239,9 +197,16 @@
             partial[1] += fold(kept * value)
             return 0
 
-        lax.fori_loop(0, pixels, add, 0)
-
-    norm_sums(first)
+        return add
+
+    own.wait()
+    partial[...] = jnp.zeros(partial.shape, f32)
+    for j in range(side):
+        for copy in image_copies[j]:
+            copy.wait()
+        block = jnp.concatenate([own_images[k, j, pl.ds(0, line), :] for k in range(n)], axis=1)
+        first[pl.ds(j * line, line), :] = dot(block, reduce_low[...], 1, 1)
+        lax.fori_loop(j * side, (j + 1) * side, add_to_sums(first), 0)
     all_valid = jnp.sum(valid[...], axis=0, keepdims=True)
     pack_one[...] = jnp.concatenate(
         [packed(total_of(0)), packed(total_of(1)), all_valid, jnp.zeros((7, 128), f32)], axis=0)
@@ -278,7 +243,8 @@
 
     lax.fori_loop(0, side, conv_line, 0)
     roots_z = pass_z(roots_out, roots_z)
-    norm_sums(second)
+    partial[...] = jnp.zeros(partial.shape, f32)
+    lax.fori_loop(0, pixels, add_to_sums(second), 0)
     pack_two[...] = jnp.concatenate([packed(total_of(0)), packed(total_of(1))], axis=0)
     stats = settled(exchange(pack_two, held_two), held_two)
     mean_two, scale_two = norm_of(stats)
@@ -467,7 +433,7 @@
     quarters = lambda a: a.reshape(nx, 2, rows, a.shape[1])
     held = lambda k: pltpu.VMEM((n * nb, k, 128), f32)
     pack = lambda k: pltpu.VMEM((k, 128), f32)
-    count = 2 * (nz - 1) + 2 * (n - 1) + (1 + (nx - 1) + 1) + (2 * nx + 1) + 4 * (n * nb - 1)
+    count = 2 * (nz - 1) + (SIDE + 1) * (n - 1) + (1 + (nx - 1) + 1) + (2 * nx + 1) + 4 * (n * nb - 1)
     two = 2 * width // 128
     three = two + classes // 128
     weight = lambda size: pltpu.VMEM((nz, 2, nx, 2, rows, size), low)
@@ -510,7 +476,8 @@
 
 
 def settle_kernel(
-    chunks, spatial, reduce, head, mask, full, own, sums, core_in, first_in, first_out, second_in, near_in, across_in,
+    chunks, spatial, reduce, head, mask, left_root, roots, own, left_part, right_part, outer_out, size,
+    full, factors, lefts, rights, outers, squares, held, sums, core_in, first_in, second_in, near_in, across_in,
     final, final_low, send, recv, local,
 ):
     (z, y, x, core), (nz, ny, nx, nc) = place()
@@ -523,9 +490,13 @@
     mates_x = [at(z, y, k, core) for k in others_x]
     mates_near = [at(k, y, x, core) for k in near_z]
     mate_across = at(across_z, y, x, core)
-    greet([mate, mate_y, mate_across] + mates_x + mates_near)
+    c, n = lax.axis_index("chan"), lax.axis_size("chan")
+    others = [{"chan": k} for k in turned(c, n)]
+    greet(others + mates_x + [mate])
     copies = Copies(send, recv)
-    f32 = jnp.float32
+    f32, low = jnp.float32, jnp.bfloat16
+    rows, width = left_root.shape[1:]
+    tiles_one = reduce.shape[-1] // width
     sources = ((spatial, 0), (reduce, spatial.shape[-1]), (head, spatial.shape[-1] + reduce.shape[-1]))
     wide = full.shape[-1]
     used_local = [0]
@@ -536,11 +507,35 @@
         copy.start()
         return copy
 
+    roots_in = [keep(roots, factors)]
+    pick = (lax.broadcasted_iota(jnp.int32, (rows, width), 1)
+            == lax.broadcasted_iota(jnp.int32, (rows, width), 0) + c * rows).astype(low)
+    squares[...] = jnp.zeros(squares.shape, f32)
+    outgoing = []
+
+    def two_parts(value):
+        high = value.astype(low)
+        return [high, (value - high.astype(f32)).astype(low)]
+
+    def multiply(t, columns):
+        grad = full[:, :, :, :, :, columns].reshape(width, width)
+        mine = full[z, y, :, :, :, columns].reshape(rows, width)
+        first = dot(jnp.concatenate([mine, pick], axis=0), grad, 1, 1)
+        lefts[t] = first[:rows]
+        second = dot(jnp.concatenate([first[rows:].astype(low)] + two_parts(left_root[t]), axis=0), grad, 1, 0)
+        rights[t] = second[:rows]
+        inner = second[rows : 2 * rows] + second[2 * rows :]
+        third = dot(jnp.concatenate(two_parts(inner), axis=0), factors[:, t * width : (t + 1) * width], 1, 0)
+        value = third[:rows] + third[rows:]
+        outers[t] = value
+        squares[t : t + 1, :] = jnp.full((1, 128), jnp.sum(value * value), f32)
+        outgoing.extend(keep(a.at[t], b.at[t]) for a, b in ((lefts, left_part), (rights, right_part), (outers, outer_out)))
+
     def wait(going):
         for copy in going:
             copy.wait()
 
-    def chunk(start, size, x_first):
+    def enter(start, size):
         columns = pl.ds(start, size)
         going = []
         for source, first_column in sources:
@@ -555,19 +550,94 @@
             for j in range(ny):
                 for k in range(nx):
                     sums[i, j, k, :, columns] += core_in[i, j, k, :, columns]
+
+    def settled(start, last_in, columns):
+        total = (sums[z, y, x, :, columns] + last_in) * mask[:, columns]
+        final[:, columns] = total
+        kept = [keep(final.at[:, columns], own.at[x, core, :, columns])]
+        kept += [copies.start(final.at[:, columns], own.at[x, core, :, columns], peer) for peer in mates_x]
+        if start < wide:
+            final_low[:, columns] = total.astype(low)
+            return kept, [keep(final_low.at[:, columns], full.at[z, y, x, core, :, columns])]
+        return kept, []
+
+    def own_core(kept, columns):
+        wait(kept)
+        part = own.at[:, core, :, columns]
+        return copies.start(part, part, mate)
+
+    def block_of(start, columns):
+        t = start // width
+        if roots_in:
+            roots_in.pop().wait()
+        taps = spatial.shape[-1] // width
+        multiply(t + tiles_one if t < taps else t - taps, columns)
+
+    def chunk_z(start, size):
+        columns = pl.ds(start, size)
+        yield from enter(start, size)
         going = []
+        for t, k in enumerate(near_z):
+            for h in range(2):
+                there = lax.rem(k + h * half, nz)
+                going.append(copies.start(
+                    sums.at[there, :, :, :, columns], first_in.at[t, pl.ds(2 * h, 2), :, :, columns], mates_near[t]))
+        yield
+        wait(going)
+        for t in range(half - 1):
+            for h in range(2):
+                for j in range(ny):
+                    for k in range(nx):
+                        sums[lax.rem(z + h * half, nz), j, k, :, columns] += first_in[t, 2 * h + j, k, :, columns]
+        landing = [second_in.at[0, pl.ds(nx * j, nx), :, columns] for j in range(ny)]
+        going = [copies.start(sums.at[across_z, j, :, :, columns], landing[j], mate_across) for j in range(ny)]
+        yield
+        wait(going)
+        for j in range(ny):
+            for k in range(nx):
+                sums[z, j, k, :, columns] += second_in[0, nx * j + k, :, columns]
+        going = [copies.start(sums.at[z, :, k, :, columns], near_in.at[t, :, :, columns], mates_x[t])
+                 for t, k in enumerate(others_x)]
+        yield
+        wait(going)
+        for t in range(nx - 1):
+            for j in range(ny):
+                sums[z, j, x, :, columns] += near_in[t, j, :, columns]
+        going = [copies.start(sums.at[z, 1 - y, x, :, columns], across_in.at[:, columns], mate_y)]
+        yield
+        wait(going)
+        kept, going = settled(start, across_in[:, columns], columns)
+        going += [copies.start(final_low.at[:, columns], full.at[z, y, x, core, :, columns], peer) for peer in mates_x]
+        yield
+        last = [own_core(kept, columns)]
+        wait(going)
+        part = full.at[z, y, :, core, :, columns]
+        going = [copies.start(part, part, mate_y)]
+        yield
+        wait(going)
+        part = full.at[z, :, :, core, :, columns]
+        going = [copies.start(part, part, peer) for peer in [mate_across] + mates_near]
+        yield
+        wait(going)
+        part = full.at[across_z, :, :, core, :, columns]
+        going = [copies.start(part, part, peer) for peer in mates_near]
+        yield
+        wait(going)
+        part = full.at[:, :, :, core, :, columns]
+        last.append(copies.start(part, part, mate))
+        yield
+        wait(last)
+        block_of(start, columns)
+
+    def chunk(start, size, x_first):
+        columns = pl.ds(start, size)
+        yield from enter(start, size)
         if x_first:
-            for t, k in enumerate(others_x):
-                for i in range(nz):
-                    for j in range(ny):
-                        first_out[t, i, j, :, columns] = sums[i, j, k, :, columns].astype(first_out.dtype)
-                going.append(copies.start(first_out.at[t, :, :, :, columns], first_in.at[t, :, :, :, columns], mates_x[t]))
+            going = [copies.start(sums.at[:, :, k, :, columns], first_in.at[t, :, :, :, columns], mates_x[t])
+                     for t, k in enumerate(others_x)]
         else:
-            for i in range(nz):
-                for k in range(nx):
-                    first_out[k // ny, i, k % ny, :, columns] = sums[i, 1 - y, k, :, columns].astype(first_out.dtype)
-            for t in range(nx // ny):
-                going.append(copies.start(first_out.at[t, :, :, :, columns], first_in.at[t, :, :, :, columns], mate_y))
+            going = [copies.start(sums.at[:, 1 - y, pl.ds(ny * t, ny), :, columns], first_in.at[t, :, :, :, columns], mate_y)
+                     for t in range(nx // ny)]
         yield
         wait(going)
         going = []
@@ -575,12 +645,12 @@
             for t in range(nx - 1):
                 for i in range(nz):
                     for j in range(ny):
-                        sums[i, j, x, :, columns] += first_in[t, i, j, :, columns].astype(f32)
+                        sums[i, j, x, :, columns] += first_in[t, i, j, :, columns]
             going.append(copies.start(sums.at[:, 1 - y, x, :, columns], second_in.at[0, :, :, columns], mate_y))
         else:
             for i in range(nz):
                 for k in range(nx):
-                    sums[i, y, k, :, columns] += first_in[k // ny, i, k % ny, :, columns].astype(f32)
+                    sums[i, y, k, :, columns] += first_in[k // ny, i, k % ny, :, columns]
             for t, k in enumerate(others_x):
                 going.append(copies.start(sums.at[:, y, k, :, columns], second_in.at[t, :, :, columns], mates_x[t]))
         yield
@@ -601,90 +671,158 @@
         going = [copies.start(sums.at[across_z, y, x, :, columns], across_in.at[:, columns], mate_across)]
         yield
         wait(going)
-        total = (sums[z, y, x, :, columns] + across_in[:, columns]) * mask[:, columns]
-        final[:, columns] = total
-        kept = keep(final.at[:, columns], own.at[x, core, :, columns])
-        rows_x = [copies.start(final.at[:, columns], own.at[x, core, :, columns], peer) for peer in mates_x]
-        low_size = min(start + size, wide) - start
-        if low_size > 0:
-            low_columns = pl.ds(start, low_size)
-            final_low[:, low_columns] = total[:, :low_size].astype(final_low.dtype)
-            source = final_low.at[:, low_columns]
-            place_at = full.at[z, y, x, core, :, low_columns]
-            going = [keep(source, place_at)] + [copies.start(source, place_at, peer) for peer in [mate_across] + mates_near]
-        yield
-        wait([kept] + rows_x)
-        part = own.at[:, core, :, columns]
-        rows_core = [copies.start(part, part, mate)]
-        if low_size > 0:
+        kept, going = settled(start, across_in[:, columns], columns)
+        if start < wide:
+            going += [copies.start(final_low.at[:, columns], full.at[z, y, x, core, :, columns], peer)
+                      for peer in [mate_across] + mates_near]
+        yield
+        rows_core = [own_core(kept, columns)]
+        if start < wide:
             wait(going)
-            part = full.at[across_z, y, x, core, :, low_columns]
+            part = full.at[across_z, y, x, core, :, columns]
             going = [copies.start(part, part, peer) for peer in mates_near]
             yield
             wait(going)
-            part = full.at[:, y, x, core, :, low_columns]
+            part = full.at[:, y, x, core, :, columns]
             going = [copies.start(part, part, peer) for peer in (mates_x if x_first else [mate_y])]
             yield
             wait(going)
-            part = full.at[:, y, :, core, :, low_columns] if x_first else full.at[:, :, x, core, :, low_columns]
+            part = full.at[:, y, :, core, :, columns] if x_first else full.at[:, :, x, core, :, columns]
             going = [copies.start(part, part, peer) for peer in ([mate_y] if x_first else mates_x)]
             yield
             wait(going)
-            part = full.at[:, :, :, core, :, low_columns]
+            part = full.at[:, :, :, core, :, columns]
             rows_core.append(copies.start(part, part, mate))
         yield
         wait(rows_core)
-
-    waiting, active = [chunk(*c) for c in chunks], []
-    while waiting or active:
-        for _ in range(2):
-            if waiting:
-                active.append(waiting.pop(0))
-        for going in list(active):
+        if start < wide:
+            block_of(start, columns)
+
+    rounds = [[chunk_z(*c[:2]) if c[2] == "z" and c[0] < wide else chunk(*c[:2], c[2] != "y") for c in some] for some in chunks]
+    begun, active = [], []
+    while rounds or begun or active:
+        active += begun
+        begun = rounds.pop(0) if rounds else []
+        for going in begun:
+            next(going)
+        for going in active[::-1]:
             try:
                 next(going)
             except StopIteration:
                 active.remove(going)
-
-
-def settle(spatial, reduce, head, mask, wire, pairs):
-    nz, nx = lax.axis_size("chan") // 2, lax.axis_size("batch") // 2
-    width = spatial.shape[0]
+    going = [copies.start(squares, held.at[k + 1], peer) for k, peer in enumerate(others)]
+    held[0] = squares[...]
+    wait(going + outgoing)
+    size[...] = jnp.sqrt(jnp.sum(held[...], axis=0) / (width * width) + 1e-06)
+
+
+def settle(spatial, reduce, head, mask, left_root, roots):
+    nz, nx, n = lax.axis_size("chan") // 2, lax.axis_size("batch") // 2, lax.axis_size("chan")
+    blocks, own_rows, width = left_root.shape
     rows = width // (4 * nz * nx)
     total = spatial.shape[1] + reduce.shape[1] + head.shape[1]
     wide = spatial.shape[1] + reduce.shape[1]
     split = lambda a: a.reshape(nz, 2, nx, 2, rows, a.shape[1])
     f32, low = jnp.float32, jnp.bfloat16
-    cuts = [128 * (total // 128 * i // (2 * pairs)) for i in range(2 * pairs + 1)]
-    chunks = [(a, b - a, i % 2 == 0) for i, (a, b) in enumerate(zip(cuts[:-1], cuts[1:]))]
+    kinds = ORDERS if nx == 2 and nz == 4 else ("xy",)
+    chunks, start = [], 0
+    while start < total:
+        some = [(start + i * width, width, kind) for i, kind in enumerate(kinds[len(chunks) % len(kinds)])]
+        chunks.append([c for c in some if c[0] < total])
+        start += len(some) * width
+    near = nz // 2 - 1
     first = max(nx - 1, nx // 2)
-    near = nz // 2 - 1
-    count = len(chunks) * (max(nx - 1, nx // 2) + max(nx - 1, 1) + 2 * near + 1 + (nx - 1) + 1 + near + 1 + near + nx + 1)
-    count += len(chunks) + 3
-    full, own = pl.pallas_call(
+    count = (total // width) * (4 + first + max(nx - 1, 1) + 2 * near + 1 + (nx - 1) + 1 + near + 1 + near + nx + 1) + n
+    product = jax.ShapeDtypeStruct((blocks, own_rows, width), f32)
+    padded = (blocks + 7) // 8 * 8
+    own, left_part, right_part, outer, size = pl.pallas_call(
         functools.partial(settle_kernel, chunks),
         out_shape=(
-            jax.ShapeDtypeStruct((nz, 2, nx, 2, rows, wide), low),
-            jax.ShapeDtypeStruct((nx, 2, rows, total), f32),
+            jax.ShapeDtypeStruct((nx, 2, rows, total), f32), product, product, product,
+            jax.ShapeDtypeStruct((padded, 128), f32),
         ),
-        in_specs=[ANY, ANY, ANY, VMEM],
-        out_specs=(ANY, ANY),
+        in_specs=[ANY, ANY, ANY, VMEM, VMEM, ANY],
+        out_specs=(ANY,) * 4 + (VMEM,),
         scratch_shapes=[
+            pltpu.VMEM((nz, 2, nx, 2, rows, wide), low),
+            pltpu.VMEM(roots.shape, low),
+            pltpu.VMEM(product.shape, f32),
+            pltpu.VMEM(product.shape, f32),
+            pltpu.VMEM(product.shape, f32),
+            pltpu.VMEM((padded, 128), f32),
+            pltpu.VMEM((n, padded, 128), f32),
             pltpu.VMEM((nz, 2, nx, rows, total), f32),
             pltpu.VMEM((nz, 2, nx, rows, total), f32),
-            pltpu.VMEM((first, nz, 2, rows, total), wire),
-            pltpu.VMEM((first, nz, 2, rows, total), wire),
+            pltpu.VMEM((first, nz, 2, rows, total), f32),
             pltpu.VMEM((max(nx - 1, 1), nz, rows, total), f32),
             pltpu.VMEM((near, 2, rows, total), f32),
             pltpu.VMEM((rows, total), f32),
             pltpu.VMEM((rows, total), f32),
             pltpu.VMEM((rows, wide), low),
-            DMA((count,)), DMA((count,)), DMA((3 * len(chunks) + 3,)),
+            DMA((count,)), DMA((count,)), DMA((7 * (total // width) + 4,)),
         ],
-        compiler_params=pltpu.CompilerParams(collective_id=1, has_side_effects=True, vmem_limit_bytes=58 << 20),
+        compiler_params=pltpu.CompilerParams(collective_id=1, has_side_effects=True, vmem_limit_bytes=60 << 20),
         name="settle",
-    )(split(spatial), split(reduce), split(head), mask)
-    return full.reshape(width, wide), own.reshape(2 * nx * rows, total)
+    )(split(spatial), split(reduce), split(head), mask, left_root, roots)
+    return own.reshape(own_rows, total), left_part, right_part, outer, size
+
+
+def finish_kernel(
+    tiles_one, own, head_a, head_b, left_part, right_part, outer, size, left_stats, right_stats,
+    reduce_weight, spatial_weight, reduce_mask, spatial_mask, head_weight, head_first, head_second,
+    reduce_grad, spatial_grad, reduce_new, spatial_new, left_new, right_new, head_new, head_first_new, head_second_new,
+):
+    t = pl.program_id(0)
+    left_new[0] = 0.95 * left_stats[0] + left_part[0]
+    right_new[0] = 0.95 * right_stats[0] + right_part[0]
+    step = outer[0] / jnp.concatenate([size[pl.ds(t, 1), :]] * (outer.shape[-1] // 128), axis=1)
+
+    def leave(weight, mask, grad, new):
+        grad[...] = own[...]
+        new[...] = weight[...] - 0.02 * mask[...].astype(jnp.float32) * (step + 0.1 * weight[...])
+
+    @pl.when(t < tiles_one)
+    def _():
+        leave(reduce_weight, reduce_mask, reduce_grad, reduce_new)
+
+    @pl.when(t >= tiles_one)
+    def _():
+        leave(spatial_weight, spatial_mask, spatial_grad, spatial_new)
+
+    @pl.when(t == 0)
+    def _():
+        head_grad = jnp.concatenate([head_a[...], head_b[...]], axis=1)[:, : head_weight.shape[1]]
+        head_new[...], head_first_new[...], head_second_new[...] = adam_step(
+            head_weight[...], head_grad, head_first[...], head_second[...], 0.04, 0.1)
+
+
+def finish(own, left_part, right_part, outer, size, left_stats, right_stats,
+           reduce_weight, spatial_weight, reduce_mask, spatial_mask, head_weight, head_first, head_second):
+    blocks, rows, width = left_stats.shape
+    tiles_one, taps = reduce_weight.shape[1] // width, spatial_weight.shape[1] // width
+    columns = lambda index: pl.BlockSpec((rows, width), lambda t: (0, index(t)))
+    of_block = pl.BlockSpec((1, rows, width), lambda t: (t, 0, 0))
+    whole = lambda a: pl.BlockSpec(a.shape, lambda t: (0, 0))
+    of_reduce = columns(lambda t: jnp.minimum(t, tiles_one - 1))
+    of_spatial = columns(lambda t: jnp.maximum(t - tiles_one, 0))
+    like = lambda a: jax.ShapeDtypeStruct(a.shape, jnp.float32)
+    return pl.pallas_call(
+        functools.partial(finish_kernel, tiles_one),
+        grid=(blocks,),
+        out_shape=(like(reduce_weight), like(spatial_weight), like(reduce_weight), like(spatial_weight),
+                   like(left_stats), like(left_stats), like(head_weight), like(head_weight), like(head_weight)),
+        in_specs=[
+            columns(lambda t: jnp.where(t < tiles_one, taps + t, t - tiles_one)),
+            columns(lambda t: taps + tiles_one), columns(lambda t: taps + tiles_one + 1),
+            of_block, of_block, of_block, whole(size), of_block, of_block,
+            of_reduce, of_spatial, of_reduce, of_spatial, whole(head_weight), whole(head_weight), whole(head_weight),
+        ],
+        out_specs=(of_reduce, of_spatial, of_reduce, of_spatial, of_block, of_block,
+                   whole(head_weight), whole(head_weight), whole(head_weight)),
+        compiler_params=pltpu.CompilerParams(vmem_limit_bytes=60 << 20),
+        name="finish",
+    )(own, own, own, left_part, right_part, outer, size, left_stats, right_stats,
+      reduce_weight, spatial_weight, reduce_mask, spatial_mask, head_weight, head_first, head_second)
 
 
 def silu_slope(pre):
@@ -703,21 +841,6 @@
 def own_part(array, axis, name="chan"):
     size = array.shape[axis] // lax.axis_size(name)
     return lax.dynamic_slice_in_dim(array, lax.axis_index(name) * size, size, axis)
-
-
-def two_parts(array):
-    high = array.astype(jnp.bfloat16)
-    return high, (array - high.astype(jnp.float32)).astype(jnp.bfloat16)
-
-
-def product(spec, left, right):
-    return jnp.einsum(spec, left, right, preferred_element_type=jnp.float32)
-
-
-def conv_grid(grid, taps, spec):
-    return lax.conv_general_dilated(
-        grid, taps, (1, 1), ((1, 1), (1, 1)), dimension_numbers=spec, preferred_element_type=jnp.float32
-    )
 
 
 def body(
@@ -771,36 +894,16 @@
         jnp.pad(head_bias, (0, padded - classes), constant_values=-1e30)[None])
 
     mask_rows = jnp.concatenate([spatial_float, reduce_float, jnp.ones((rows_out, padded), f32)], axis=1)
-    full, own = settle(spatial_local, reduce_local, head_local, own_part(mask_rows, 0, "batch"), jnp.float32, 6)
-    spatial_grad = own[:, : 9 * width]
-    reduce_grad = own[:, 9 * width : 9 * width + c_in]
-    head_grad = own[:, 9 * width + c_in : 9 * width + c_in + classes]
+    own, *products = settle(spatial_local, reduce_local, head_local, own_part(mask_rows, 0, "batch"), left_root, roots_full)
     of_norms = jnp.stack([a.reshape(-1) for a in (sums_one[4:], sums_one[:4], sums_two[4:8], sums_two[:4])])
     norm_gain_gradient = own_part(of_norms, 1)
     of_head = sums_two[8:].reshape(-1)
     bias_grad = of_head[:classes]
     loss_sum, slot_count = of_head[-1], of_head[-2]
-    right_full = roots_full.reshape(width, -1, width)
-
-    tiles_one = c_in // width
-    blocks_of = lambda a: a.reshape(a.shape[0], -1, width).transpose(1, 0, 2)
-    in_order = lambda a: jnp.concatenate([a[9:], a[:9]], axis=0)
-    blocks = in_order(blocks_of(own[:, : 9 * width + c_in])).astype(low)
-    blocks_full = in_order(blocks_of(full))
-    left_new = 0.95 * left_stats + product("tak,tbk->tab", blocks, blocks_full)
-    right_new = 0.95 * right_stats + product("tki,tkb->tib", own_part(blocks_full, 2), blocks_full)
-    left_high, left_rest = two_parts(left_root)
-    inner = product("tak,tkb->tab", left_high, blocks_full) + product("tak,tkb->tab", left_rest, blocks_full)
-    inner_high, inner_rest = two_parts(inner)
-    outer = product("tak,ktb->tab", inner_high, right_full) + product("tak,ktb->tab", inner_rest, right_full)
-    squares = jnp.pad(jnp.sum(outer * outer, axis=(1, 2))[:, None] * jnp.ones((1, 128), f32), ((0, 3), (0, 0)))
-    squares = chan_sum(squares, 6)[: 9 + tiles_one, 0]
-    step = outer / jnp.sqrt(squares / (width * width) + 1e-06)[:, None, None]
-    step_one = step[:tiles_one].transpose(1, 0, 2).reshape(rows_out, c_in)
-    step_two = step[tiles_one:].transpose(1, 0, 2).reshape(rows_out, 9 * width)
-    reduce_new = reduce_weight - 0.02 * reduce_float * (step_one + 0.1 * reduce_weight)
-    spatial_new = spatial_weight - 0.02 * spatial_float * (step_two + 0.1 * spatial_weight)
-    head_new, head_first_new, head_second_new = adam_step(head_weight, head_grad, head_first, head_second, 0.04, 0.1)
+    (reduce_grad, spatial_grad, reduce_new, spatial_new, left_new, right_new, head_new, head_first_new,
+     head_second_new) = finish(
+        own, *products, left_stats, right_stats, reduce_weight, spatial_weight, reduce_mask, spatial_mask,
+        head_weight, head_first, head_second)
     bias_new, bias_first_new, bias_second_new = adam_step(head_bias, bias_grad, bias_first, bias_second, 0.1, 0.0)
     norm_new, norm_first_new, norm_second_new = adam_step(
         norm_params, norm_gain_gradient, norm_first, norm_second, 0.1, 0.0)
@@ -827,6 +930,13 @@
 
 FULL_PRECISION = lax.Precision.HIGHEST
 BOTH = ("chan", "batch")
+
+
+def conv_grid(grid, taps, spec):
+    return lax.conv_general_dilated(
+        grid, taps, (1, 1), ((1, 1), (1, 1)), dimension_numbers=spec,
+        preferred_element_type=jnp.float32,
+    )
 
 
 def plain_norm_forward(pre_norm, gain, shift, valid):

time: 585 us -> 492 us (0.84); the launches traced: 578 us -> 492 us
  local copies, waits for them, and re-layouts: 62 us -> 19.2 us
  matrix products: 28.6 us -> 0 us
  Pallas kernels: 475 us -> 466 us
    another operation x4 -> x0, local copies, waits for them, and re-layouts: 33.2 us -> none  [the longest x2 20.4 us: body(): blocks_of = lambda a: a.reshape(a.shape[0], -1, width).transpose(1, 0, 2)]
    dot_general x6 -> x0, matrix products: 28.6 us -> none  [product(): return jnp.einsum(spec, left, right, preferred_element_type=jnp.float32)]
    pallas_call x1, Pallas kernels: 122 us -> 115 us  [settle(): pl.pallas_call(functools.partial(settle_kernel, chunks), out_shape=(jax.S...]
    pallas_call x1, Pallas kernels: 344 us -> 338 us  [local_step(): pl.pallas_call(step_kernel, out_shape=(shape((width, 9 * width), f32), sh...]
where the time goes in v4:
time: 492 us
  Pallas kernels  466 us (95%)
  local copies, waits for them, and re-layouts  19.2 us (4%)
  other arithmetic  5.39 us (1%)
    pallas_call x1, Pallas kernels, local_step(): pl.pallas_call(step_kernel, out_shape=(shape((width, 9 * width), f32), sh...  338 us
    pallas_call x1, Pallas kernels, settle(): pl.pallas_call(functools.partial(settle_kernel, chunks), out_shape=(jax.S...  115 us
    pallas_call x1, Pallas kernels, finish(): pl.pallas_call(functools.partial(finish_kernel, tiles_one), grid=(blocks,...  12.7 us

profile of v4, /device:TPU:0, one launch (start us, length us, event | category | flops | bytes accessed | tf_op | source)
XLA Modules:
  0.0 491.7 jit_solution(17328992778297351872)
XLA Ops:
  0.7 0.9 convert_reduce_fusion
  1.6 0.7 broadcast_in_dim.38.used
  2.3 0.7 broadcast_in_dim.39.divisor
  3.0 0.9 convert_bitcast_fusion.1
  3.9 0.1 broadcast_in_dim.17
  3.9 1.4 broadcast_in_dim.36.valid
  5.3 0.8 dynamic_slice.13
  6.1 0.7 broadcast_in_dim.37.labels
  6.8 0.7 pad.13
  7.5 0.1 dynamic_update_slice.3.norms
  7.6 0.0 copy-start.6
  7.6 8.3 %copy.39 = bf16[8,48,49,256]{3,1,2,0:T(8,128)(2,1)} copy(bf16[8,48,49,256]{3,1,0,2:T(8,128)(2,1)} %bitcast.27) | data formatting | bytes 19267584 | tf_op jit(solution)/shard_map/reshape | solution.py:882
  15.9 0.1 convert_bitcast_fusion
  16.1 0.5 copy.40
  16.6 1.5 reshape_reshape.3.roots
  18.1 0.1 multiply_convert_fusion
  18.2 0.9 copy-done.2
  19.1 0.2 copy-done.3
  19.3 0.1 multiply_convert_fusion.1
  19.4 0.0 copy-done.5
  19.4 1.0 fusion.1
  20.4 0.6 pad.14
  21.0 338.2 %step.1 = (f32[512,4608]{1,0:T(8,128)}, f32[512,2048]{1,0:T(8,128)}, f32[512,1024]{1,0:T(8,128)}, f32[24,128]{1,0:T(8,128)}, bf16[4,2,2,2,16,7680]{5,4,3,2,1,0:T...) custom-call(bf16[8,7,336,256]{3,2,1,0:T(8,128)(2,1)} %bitcast.23, bf16[2,2,16,7680]{3,2,1,0:T(8,128)(2,1)} %bitcast.31, ...), custom_call_target="tpu_custom_call" | custom-call | tf_op jit(solution)/shard_map/step/pallas_call | solution.py:440
  359.2 0.8 fusion.11
  360.0 0.7 multiply_subtract_fusion.1
  360.7 0.1 convert_element_type.32
  360.9 0.8 fusion.3.mask
  361.7 115.4 %settle.1 = (f32[2,2,16,7680]{3,2,1,0:T(8,128)}, f32[13,64,512]{2,1,0:T(8,128)}, f32[13,64,512]{2,1,0:T(8,128)}, f32[13,64,512]{2,1,0:T(8,128)}, f32[16,128]{1,0:T(8,128)}) custom-call(f32[4,2,2,2,16,4608]{5,4,3,2,1,0:T(8,128)} %bitcast.28, f32[4,2,2,2,16,2048]{5,4,3,2,1,0:T(8,128)} %bitcast.30, f32[4,2,2,2,16,1024]{5,4,3,2,1,0:T(8,128)} %bitcast.32, ...), custom_call_target="tpu_custom_call" | custom-call | tf_op jit(solution)/shard_map/settle/pallas_call | solution.py:738
  477.1 12.7 %finish.1 = (f32[64,2048]{1,0:T(8,128)}, f32[64,4608]{1,0:T(8,128)}, f32[64,2048]{1,0:T(8,128)}, f32[64,4608]{1,0:T(8,128)}, f32[13,64,512]{2,1,0:T(8,128)}, /*i...) custom-call(f32[64,7680]{1,0:T(8,128)} %bitcast.24, f32[64,7680]{1,0:T(8,128)} %bitcast.25, ...), custom_call_target="tpu_custom_call" | custom-call | tf_op jit(solution)/shard_map/finish/pallas_call | solution.py:809
  489.9 0.7 slice_bitcast_fusion
  490.5 0.6 multiply_subtract_fusion
  491.2 0.6 fusion.12
  (29 shorter events, 0.1 us)
Async XLA Ops:
  7.6 8.3 %copy-start.6 = (f32[8,512]{1,0:T(8,128)}, f32[8,512]{1,0:T(8,128)S(1)}, u32[]{:S(2)}) copy-start(f32[8,512]{1,0:T(8,128)S(1)} %dynamic_update_slice.3.norms) | copy-start | bytes 49156
  7.6 8.3 %copy-start.4 = (f32[13,64,512]{2,1,0:T(8,128)S(1)}, f32[13,64,512]{2,1,0:T(8,128)}, u32[]{:S(2)}) copy-start(f32[13,64,512]{2,1,0:T(8,128)} %param.33) | copy-start | bytes 5111812
  16.1 2.0 copy-start
  16.1 2.0 copy-start.1
  18.1 1.0 copy-start.2
  18.1 1.2 copy-start.3
  18.1 1.3 copy-start.5
  19.3 1.1 copy-start.7
  21.0 339.0 %copy-start.8 = (f32[4,64]{1,0:T(4,128)S(1)}, f32[4,64]{1,0:T(4,128)}, u32[]{:S(2)}) copy-start(f32[4,64]{1,0:T(4,128)} %param.29) | copy-start | bytes 3076
  21.0 339.0 %copy-start.11 = (f32[4,64]{1,0:T(4,128)S(1)}, f32[4,64]{1,0:T(4,128)}, u32[]{:S(2)}) copy-start(f32[4,64]{1,0:T(4,128)} %param.38) | copy-start | bytes 3076
  21.0 339.0 %copy-start.12 = (f32[4,64]{1,0:T(4,128)S(1)}, f32[4,64]{1,0:T(4,128)}, u32[]{:S(2)}) copy-start(f32[4,64]{1,0:T(4,128)} %param.39) | copy-start | bytes 3076
  477.1 13.4 %copy-start.9 = (f32[1000]{0:T(1024)S(1)}, f32[1000]{0:T(1024)}, u32[]{:S(2)}) copy-start(f32[1000]{0:T(1024)} %param.36) | copy-start | bytes 12004
  477.1 13.4 %copy-start.10 = (f32[1000]{0:T(1024)S(1)}, f32[1000]{0:T(1024)}, u32[]{:S(2)}) copy-start(f32[1000]{0:T(1024)} %param.37) | copy-start | bytes 12004

commit v5 on v4

--- a/solution.py
+++ b/solution.py
@@ -74,10 +74,10 @@
 
 def step_kernel(
     images, weights, roots, norms, valid, labels, used, divisor, bias,
-    spatial_out, reduce_out, head_out, totals_out, weights_out, roots_out,
+    taps_out, reduce_out, head_out, totals_out, weights_out, roots_out,
     own_images, first, second, hidden_pad, grad_pad, turned_grad, taps, reduce_low, head_low,
     norms_held, pack_one, pack_two, pack_three, pack_four, held_one, held_two, held_three, held_four,
-    partial, pooling, pooled_low, d_logits, d_act, head_buf, grad_buf, send, recv, local,
+    tap_sums, core_in, first_in, partial, pooling, pooled_low, d_logits, d_act, head_buf, grad_buf, send, recv, local,
 ):
     (z, y, x, core), (nz, ny, nx, nc) = place()
     c, n = lax.axis_index("chan"), lax.axis_size("chan")
@@ -344,11 +344,6 @@
         return 0
 
     lax.fori_loop(0, side, spread_line, 0)
-    for copy in roots_a + roots_b:
-        copy.wait()
-    part = roots_out.at[:, :, :, core]
-    roots_core = copies.start(part, part, mate)
-
     def enter_first(p, _):
         normed = (first[pixel_rows(p), :] - mean_one) * scale_one
         pre = gain_one * normed + shift_one
@@ -375,17 +370,43 @@
         copy.start()
         return copy
 
-    leaving = []
+    half = nz // 2
+    near = z // half * half + lax.rem(z + 1, half)
+    kinds = "".join(chunk_rounds(9))
+    core_going, first_going = [], []
+
+    def part_of(t, mine):
+        if kinds[t] == "x":
+            return [(tap_sums.at[t, :, :, x if mine else lax.rem(x + 1, nx)], first_in.at[t])]
+        if kinds[t] == "y":
+            return [(tap_sums.at[t, :, y if mine else 1 - y], first_in.at[t])]
+        return [(tap_sums.at[t, (z // half * half + lax.rem(z, half) if mine else near) % half + h * half],
+                 first_in.at[t, pl.ds(2 * h, 2)]) for h in range(2)]
+
+    def over_core(t):
+        core_going[t].wait()
+        for i in range(nz):
+            tap_sums[t, i] += core_in[t, i]
+        peer = {"x": at(z, y, lax.rem(x + 1, nx), core), "y": mate_y, "z": at(near, y, x, core)}[kinds[t]]
+        first_going.append([copies.start(source, target, peer) for source, target in part_of(t, False)])
+
     for t in range(9):
         offset = (t // 3 - 1) * wide_line + (t % 3 - 1) * slots
         slot = t % 2
-        if t >= 2:
-            leaving[t - 2].wait()
         shifted = hidden_pad.at[pl.ds(rim + offset, body_rows)]
-
-        grad_buf[slot] = dot(turned_grad[...], shifted[...], 1, 0)
-        leaving.append(leave(slot, spatial_out.at[:, pl.ds(t * width, width)], 7 + slot))
-
+        grad_buf[slot] = dot(turned_grad[...], shifted[...], 1, 0).reshape(grad_buf.shape[1:])
+        core_going.append(copies.start(grad_buf.at[slot, :, :, :, 1 - core], core_in.at[t], mate))
+        for i in range(nz):
+            tap_sums[t, i] = grad_buf[slot, i, :, :, core]
+        if t:
+            over_core(t - 1)
+    over_core(8)
+    leaving = []
+
+    for copy in roots_a + roots_b:
+        copy.wait()
+    part = roots_out.at[:, :, :, core]
+    roots_core = copies.start(part, part, mate)
     totals_one = settled(going, held_four)
     shift_sum, gain_sum = unpacked(totals_one[:rows]), unpacked(totals_one[rows : 2 * rows])
     factor_one = gain_one * scale_one / count
@@ -402,17 +423,23 @@
     per = width // depth
     for t in range(n // per):
         slot = (9 + t) % 2
-        leaving[9 + t - 2].wait()
-
-        def source_rows(m, _, slot=slot, t=t):
-            rows_out = pl.ds(pl.multiple_of(m * 256, 256), 256)
-            for k in range(per):
-                block = own_images[t * per + k].reshape(body_rows, depth)
-                grad_buf[slot, rows_out, k * depth : (k + 1) * depth] = dot(turned_grad[rows_out, :], block, 1, 0)
-            return 0
-
-        lax.fori_loop(0, width // 256, source_rows, 0)
-        leaving.append(leave(slot, reduce_out.at[:, pl.ds(t * width, width)], 7 + slot))
+        if t >= 2:
+            leaving[t - 2].wait()
+        block = jnp.concatenate([own_images[t * per + k].reshape(body_rows, depth) for k in range(per)], axis=1)
+        grad_buf[slot] = dot(turned_grad[...], block, 1, 0).reshape(grad_buf.shape[1:])
+        leaving.append(leave(slot, reduce_out.at[:, :, :, :, :, pl.ds(t * width, width)], 7 + slot))
+    taps_going = []
+    for t in range(9):
+        for copy in first_going[t]:
+            copy.wait()
+        for h, (kept, landed) in enumerate(part_of(t, True)):
+            kept[...] += landed[...]
+            copy = pltpu.make_async_copy(
+                kept, taps_out.at[t, pl.ds(2 * h, 2)] if kinds[t] == "z" else taps_out.at[t], local.at[9 + 2 * t + h])
+            copy.start()
+            taps_going.append(copy)
+    for copy in taps_going:
+        copy.wait()
     totals_out[...] = jnp.concatenate([totals_two, totals_one], axis=0)
     head_copy.wait()
     roots_core.wait()
@@ -433,15 +460,15 @@
     quarters = lambda a: a.reshape(nx, 2, rows, a.shape[1])
     held = lambda k: pltpu.VMEM((n * nb, k, 128), f32)
     pack = lambda k: pltpu.VMEM((k, 128), f32)
-    count = 2 * (nz - 1) + (SIDE + 1) * (n - 1) + (1 + (nx - 1) + 1) + (2 * nx + 1) + 4 * (n * nb - 1)
+    count = 2 * (nz - 1) + (SIDE + 1) * (n - 1) + (1 + (nx - 1) + 1) + (2 * nx + 1) + 4 * (n * nb - 1) + 27
     two = 2 * width // 128
     three = two + classes // 128
     weight = lambda size: pltpu.VMEM((nz, 2, nx, 2, rows, size), low)
     spatial, reduce, head, totals, weights_full, roots_full = pl.pallas_call(
         step_kernel,
         out_shape=(
-            shape((width, 9 * width), f32),
-            shape((width, n * depth), f32),
+            shape((9, nz, 2, rows, width), f32),
+            shape((nz, 2, nx, 2, rows, n * depth), f32),
             shape((width, classes), f32),
             shape((two + three, 128), f32),
             gathered(weights),
@@ -460,14 +487,17 @@
             pltpu.VMEM((n,) + norms.shape, f32),
             pack(two + 8), pack(two), pack(three), pack(two),
             held(two + 8), held(two), held(three), held(two),
+            pltpu.VMEM((9, nz, 2, nx, rows, width), f32),
+            pltpu.VMEM((9, nz, 2, nx, rows, width), f32),
+            pltpu.VMEM((9, nz, 2, rows, width), f32),
             pltpu.VMEM((2, 8, width), f32),
             pltpu.VMEM((3, slots, width), f32),
             pltpu.VMEM((slots, width), low),
             pltpu.VMEM((slots, classes), low),
             pltpu.VMEM((slots, width), f32),
             pltpu.VMEM((width, classes), f32),
-            pltpu.VMEM((2, width, width), f32),
-            DMA((count,)), DMA((count,)), DMA((9,)),
+            pltpu.VMEM((2, nz, 2, nx, 2, rows, width), f32),
+            DMA((count,)), DMA((count,)), DMA((27,)),
         ],
         compiler_params=pltpu.CompilerParams(collective_id=0, has_side_effects=True, vmem_limit_bytes=60 << 20),
         name="step",
@@ -475,8 +505,16 @@
     return spatial, reduce, head, totals[:three], totals[three:], roots_full.reshape(width, roots.shape[1])
 
 
+def chunk_rounds(count):
+    rounds = []
+    while count > 0:
+        rounds.append(ORDERS[len(rounds) % len(ORDERS)][:count])
+        count -= len(rounds[-1])
+    return rounds
+
+
 def settle_kernel(
-    chunks, spatial, reduce, head, mask, left_root, roots, own, left_part, right_part, outer_out, size,
+    chunks, taps, reduce, head, mask, left_root, roots, own, left_part, right_part, outer_out, size,
     full, factors, lefts, rights, outers, squares, held, sums, core_in, first_in, second_in, near_in, across_in,
     final, final_low, send, recv, local,
 ):
@@ -497,8 +535,9 @@
     f32, low = jnp.float32, jnp.bfloat16
     rows, width = left_root.shape[1:]
     tiles_one = reduce.shape[-1] // width
-    sources = ((spatial, 0), (reduce, spatial.shape[-1]), (head, spatial.shape[-1] + reduce.shape[-1]))
-    wide = full.shape[-1]
+    n_taps = taps.shape[0]
+    sources = ((reduce, n_taps * width), (head, n_taps * width + reduce.shape[-1]))
+    wide = n_taps * width + reduce.shape[-1]
     used_local = [0]
 
     def keep(source, target):
@@ -570,25 +609,30 @@
         t = start // width
         if roots_in:
             roots_in.pop().wait()
-        taps = spatial.shape[-1] // width
-        multiply(t + tiles_one if t < taps else t - taps, columns)
+        multiply(t + tiles_one if t < n_taps else t - n_taps, columns)
 
     def chunk_z(start, size):
         columns = pl.ds(start, size)
-        yield from enter(start, size)
-        going = []
-        for t, k in enumerate(near_z):
-            for h in range(2):
-                there = lax.rem(k + h * half, nz)
-                going.append(copies.start(
-                    sums.at[there, :, :, :, columns], first_in.at[t, pl.ds(2 * h, 2), :, :, columns], mates_near[t]))
-        yield
-        wait(going)
-        for t in range(half - 1):
-            for h in range(2):
-                for j in range(ny):
-                    for k in range(nx):
-                        sums[lax.rem(z + h * half, nz), j, k, :, columns] += first_in[t, 2 * h + j, k, :, columns]
+        if start < n_taps * width:
+            going = [keep(taps.at[start // width, pl.ds(2 * h, 2)], sums.at[lax.rem(z, half) + h * half, :, :, :, columns])
+                     for h in range(2)]
+            yield
+            wait(going)
+        else:
+            yield from enter(start, size)
+            going = []
+            for t, k in enumerate(near_z):
+                for h in range(2):
+                    there = lax.rem(k, half) + h * half
+                    going.append(copies.start(
+                        sums.at[there, :, :, :, columns], first_in.at[t, pl.ds(2 * h, 2), :, :, columns], mates_near[t]))
+            yield
+            wait(going)
+            for t in range(half - 1):
+                for h in range(2):
+                    for j in range(ny):
+                        for k in range(nx):
+                            sums[lax.rem(z, half) + h * half, j, k, :, columns] += first_in[t, 2 * h + j, k, :, columns]
         landing = [second_in.at[0, pl.ds(nx * j, nx), :, columns] for j in range(ny)]
         going = [copies.start(sums.at[across_z, j, :, :, columns], landing[j], mate_across) for j in range(ny)]
         yield
@@ -631,26 +675,29 @@
 
     def chunk(start, size, x_first):
         columns = pl.ds(start, size)
-        yield from enter(start, size)
-        if x_first:
-            going = [copies.start(sums.at[:, :, k, :, columns], first_in.at[t, :, :, :, columns], mates_x[t])
-                     for t, k in enumerate(others_x)]
+        if start < n_taps * width:
+            going = [keep(taps.at[start // width], sums.at[:, :, x, :, columns] if x_first else sums.at[:, y, :, :, columns])]
+            yield
+            wait(going)
         else:
-            going = [copies.start(sums.at[:, 1 - y, pl.ds(ny * t, ny), :, columns], first_in.at[t, :, :, :, columns], mate_y)
-                     for t in range(nx // ny)]
-        yield
-        wait(going)
+            yield from enter(start, size)
+            if x_first:
+                going = [copies.start(sums.at[:, :, k, :, columns], first_in.at[t, :, :, :, columns], mates_x[t])
+                         for t, k in enumerate(others_x)]
+            else:
+                going = [copies.start(sums.at[:, 1 - y, :, :, columns], first_in.at[0, :, :, :, columns], mate_y)]
+            yield
+            wait(going)
+            for i in range(nz):
+                for j in range(2):
+                    if x_first:
+                        sums[i, j, x, :, columns] += first_in[0, i, j, :, columns]
+                    else:
+                        sums[i, y, j, :, columns] += first_in[0, i, j, :, columns]
         going = []
         if x_first:
-            for t in range(nx - 1):
-                for i in range(nz):
-                    for j in range(ny):
-                        sums[i, j, x, :, columns] += first_in[t, i, j, :, columns]
             going.append(copies.start(sums.at[:, 1 - y, x, :, columns], second_in.at[0, :, :, columns], mate_y))
         else:
-            for i in range(nz):
-                for k in range(nx):
-                    sums[i, y, k, :, columns] += first_in[k // ny, i, k % ny, :, columns]
             for t, k in enumerate(others_x):
                 going.append(copies.start(sums.at[:, y, k, :, columns], second_in.at[t, :, :, columns], mates_x[t]))
         yield
@@ -716,20 +763,18 @@
     size[...] = jnp.sqrt(jnp.sum(held[...], axis=0) / (width * width) + 1e-06)
 
 
-def settle(spatial, reduce, head, mask, left_root, roots):
+def settle(taps, reduce, head, mask, left_root, roots):
     nz, nx, n = lax.axis_size("chan") // 2, lax.axis_size("batch") // 2, lax.axis_size("chan")
     blocks, own_rows, width = left_root.shape
     rows = width // (4 * nz * nx)
-    total = spatial.shape[1] + reduce.shape[1] + head.shape[1]
-    wide = spatial.shape[1] + reduce.shape[1]
+    wide = taps.shape[0] * width + reduce.shape[-1]
+    total = wide + head.shape[1]
     split = lambda a: a.reshape(nz, 2, nx, 2, rows, a.shape[1])
     f32, low = jnp.float32, jnp.bfloat16
-    kinds = ORDERS if nx == 2 and nz == 4 else ("xy",)
     chunks, start = [], 0
-    while start < total:
-        some = [(start + i * width, width, kind) for i, kind in enumerate(kinds[len(chunks) % len(kinds)])]
-        chunks.append([c for c in some if c[0] < total])
-        start += len(some) * width
+    for kinds in chunk_rounds(total // width):
+        chunks.append([(start + i * width, width, kind) for i, kind in enumerate(kinds)])
+        start += len(kinds) * width
     near = nz // 2 - 1
     first = max(nx - 1, nx // 2)
     count = (total // width) * (4 + first + max(nx - 1, 1) + 2 * near + 1 + (nx - 1) + 1 + near + 1 + near + nx + 1) + n
@@ -763,7 +808,7 @@
         ],
         compiler_params=pltpu.CompilerParams(collective_id=1, has_side_effects=True, vmem_limit_bytes=60 << 20),
         name="settle",
-    )(split(spatial), split(reduce), split(head), mask, left_root, roots)
+    )(taps, reduce, split(head), mask, left_root, roots)
     return own.reshape(own_rows, total), left_part, right_part, outer, size
 
 
@@ -888,13 +933,13 @@
         jnp.zeros((8, width), f32), jnp.pad(norm_params, ((0, 4), (0, 0))), lax.axis_index("chan") * rows_out, 1)
     mask_own = own_part(pixel_mask, 0).astype(f32)
     filled = jnp.sum(mask_own, axis=1)
-    spatial_local, reduce_local, head_local, sums_two, sums_one, roots_full = local_step(
+    taps_local, reduce_local, head_local, sums_two, sums_one, roots_full = local_step(
         by_pixel, weights, roots, norms, spread_out(mask_own.T.reshape(-1)), spread_out(own_part(labels, 0)),
         spread_out((filled > 0.0).astype(f32)), spread_out(jnp.maximum(filled, 1.0)),
         jnp.pad(head_bias, (0, padded - classes), constant_values=-1e30)[None])
 
     mask_rows = jnp.concatenate([spatial_float, reduce_float, jnp.ones((rows_out, padded), f32)], axis=1)
-    own, *products = settle(spatial_local, reduce_local, head_local, own_part(mask_rows, 0, "batch"), left_root, roots_full)
+    own, *products = settle(taps_local, reduce_local, head_local, own_part(mask_rows, 0, "batch"), left_root, roots_full)
     of_norms = jnp.stack([a.reshape(-1) for a in (sums_one[4:], sums_one[:4], sums_two[4:8], sums_two[:4])])
     norm_gain_gradient = own_part(of_norms, 1)
     of_head = sums_two[8:].reshape(-1)
@@ -1146,5 +1191,5 @@
         P(None, "chan"),
     )
     chan, batch = mesh.shape["chan"], mesh.shape["batch"]
-    fits = chan % 4 == 0 and batch % 2 == 0 and WIDTH % (16 * chan * batch) == 0 and SLOTS_DEV % (16 * chan) == 0
+    fits = chan == 8 and batch == 4 and WIDTH % (16 * chan * batch) == 0 and SLOTS_DEV % (16 * chan) == 0
     return jax.shard_map(body if fits else plain_body, mesh=mesh, in_specs=in_specs, out_specs=out_specs, check_vma=False)

time: 492 us -> 473 us (0.961)
  Pallas kernels: 466 us -> 447 us
    pallas_call x1, Pallas kernels: 115 us -> 97 us  [settle(): pl.pallas_call(functools.partial(settle_kernel, chunks), out_shape=(jax.S...]
where the time goes in v5:
time: 473 us
  Pallas kernels  447 us (95%)
  local copies, waits for them, and re-layouts  19.2 us (4%)
  other arithmetic  5.39 us (1%)
    pallas_call x1, Pallas kernels, local_step(): pl.pallas_call(step_kernel, out_shape=(shape((9, nz, 2, rows, width), f32...  338 us
    pallas_call x1, Pallas kernels, settle(): pl.pallas_call(functools.partial(settle_kernel, chunks), out_shape=(jax.S...  97 us
    pallas_call x1, Pallas kernels, finish(): pl.pallas_call(functools.partial(finish_kernel, tiles_one), grid=(blocks,...  12.7 us

profile of v5, /device:TPU:0, one launch (start us, length us, event | category | flops | bytes accessed | tf_op | source)
XLA Modules:
  0.0 472.7 jit_solution(188620685257670408)
XLA Ops:
  0.7 0.9 convert_reduce_fusion
  1.6 0.7 broadcast_in_dim.38.used
  2.3 0.7 broadcast_in_dim.39.divisor
  3.0 0.9 convert_bitcast_fusion.1
  3.9 0.1 broadcast_in_dim.17
  3.9 1.4 broadcast_in_dim.36.valid
  5.3 0.8 dynamic_slice.13
  6.1 0.7 broadcast_in_dim.37.labels
  6.8 0.7 pad.13
  7.5 0.1 dynamic_update_slice.3.norms
  7.6 0.0 copy-start.6
  7.6 8.3 %copy.39 = bf16[8,48,49,256]{3,1,2,0:T(8,128)(2,1)} copy(bf16[8,48,49,256]{3,1,0,2:T(8,128)(2,1)} %bitcast.25) | data formatting | bytes 19267584 | tf_op jit(solution)/shard_map/reshape | solution.py:927
  15.9 0.1 convert_bitcast_fusion
  16.1 0.5 copy.40
  16.6 1.5 reshape_reshape.3.roots
  18.1 0.1 multiply_convert_fusion
  18.2 0.9 copy-done.2
  19.1 0.2 copy-done.3
  19.3 0.1 multiply_convert_fusion.1
  19.4 0.0 copy-done.5
  19.4 1.0 fusion.1
  20.4 0.6 pad.14
  21.0 337.6 %step.1 = (f32[9,4,2,16,512]{4,3,2,1,0:T(8,128)}, f32[4,2,2,2,16,2048]{5,4,3,2,1,0:T(8,128)}, f32[512,1024]{1,0:T(8,128)}, f32[24,128]{1,0:T(8,128)}, bf16[4,2,2...) custom-call(bf16[8,7,336,256]{3,2,1,0:T(8,128)(2,1)} %bitcast.21, ...), custom_call_target="tpu_custom_call" | custom-call | tf_op jit(solution)/shard_map/step/pallas_call | solution.py:467
  358.6 0.8 fusion.11
  359.4 0.7 multiply_subtract_fusion.1
  360.1 0.1 convert_element_type.32
  360.2 0.8 fusion.3.mask
  361.1 97.0 %settle.1 = (f32[2,2,16,7680]{3,2,1,0:T(8,128)}, f32[13,64,512]{2,1,0:T(8,128)}, f32[13,64,512]{2,1,0:T(8,128)}, f32[13,64,512]{2,1,0:T(8,128)}, f32[16,128]{1,0:T(8,128)}) custom-call(f32[9,4,2,16,512]{4,3,2,1,0:T(8,128)} %get-tuple-element.37.taps, f32[4,2,2,2,16,2048]{5,4,3,2,1,0:T(8,128)} %get-tuple-element.38.reduce, ...), custom_call_target="tpu_custom_call" | custom-call | tf_op jit(solution)/shard_map/settle/pallas_call | solution.py:783
  458.1 12.7 %finish.1 = (f32[64,2048]{1,0:T(8,128)}, f32[64,4608]{1,0:T(8,128)}, f32[64,2048]{1,0:T(8,128)}, f32[64,4608]{1,0:T(8,128)}, f32[13,64,512]{2,1,0:T(8,128)}, /*i...) custom-call(f32[64,7680]{1,0:T(8,128)} %bitcast.22, f32[64,7680]{1,0:T(8,128)} %bitcast.23, ...), custom_call_target="tpu_custom_call" | custom-call | tf_op jit(solution)/shard_map/finish/pallas_call | solution.py:854
  470.8 0.7 slice_bitcast_fusion
  471.5 0.6 multiply_subtract_fusion
  472.1 0.6 fusion.12
  (29 shorter events, 0.1 us)
Async XLA Ops:
  7.6 8.3 %copy-start.6 = (f32[8,512]{1,0:T(8,128)}, f32[8,512]{1,0:T(8,128)S(1)}, u32[]{:S(2)}) copy-start(f32[8,512]{1,0:T(8,128)S(1)} %dynamic_update_slice.3.norms) | copy-start | bytes 49156
  7.6 8.3 %copy-start.4 = (f32[13,64,512]{2,1,0:T(8,128)S(1)}, f32[13,64,512]{2,1,0:T(8,128)}, u32[]{:S(2)}) copy-start(f32[13,64,512]{2,1,0:T(8,128)} %param.33) | copy-start | bytes 5111812
  16.1 2.0 copy-start
  16.1 2.0 copy-start.1
  18.1 1.0 copy-start.2
  18.1 1.2 copy-start.3
  18.1 1.3 copy-start.5
  19.3 1.1 copy-start.7
  21.0 338.4 %copy-start.8 = (f32[4,64]{1,0:T(4,128)S(1)}, f32[4,64]{1,0:T(4,128)}, u32[]{:S(2)}) copy-start(f32[4,64]{1,0:T(4,128)} %param.29) | copy-start | bytes 3076
  21.0 338.4 %copy-start.11 = (f32[4,64]{1,0:T(4,128)S(1)}, f32[4,64]{1,0:T(4,128)}, u32[]{:S(2)}) copy-start(f32[4,64]{1,0:T(4,128)} %param.38) | copy-start | bytes 3076
  21.0 338.4 %copy-start.12 = (f32[4,64]{1,0:T(4,128)S(1)}, f32[4,64]{1,0:T(4,128)}, u32[]{:S(2)}) copy-start(f32[4,64]{1,0:T(4,128)} %param.39) | copy-start | bytes 3076
  458.1 13.4 %copy-start.9 = (f32[1000]{0:T(1024)S(1)}, f32[1000]{0:T(1024)}, u32[]{:S(2)}) copy-start(f32[1000]{0:T(1024)} %param.36) | copy-start | bytes 12004
  458.1 13.4 %copy-start.10 = (f32[1000]{0:T(1024)S(1)}, f32[1000]{0:T(1024)}, u32[]{:S(2)}) copy-start(f32[1000]{0:T(1024)} %param.37) | copy-start | bytes 12004

commit v6 on v5

--- a/solution.py
+++ b/solution.py
@@ -73,10 +73,10 @@
 
 
 def step_kernel(
-    images, weights, roots, norms, valid, labels, used, divisor, bias,
+    images, weights, roots, own_norms, pixel_mask, all_labels, bias,
     taps_out, reduce_out, head_out, totals_out, weights_out, roots_out,
     own_images, first, second, hidden_pad, grad_pad, turned_grad, taps, reduce_low, head_low,
-    norms_held, pack_one, pack_two, pack_three, pack_four, held_one, held_two, held_three, held_four,
+    valid, used, divisor, norms, norms_held, pack_one, pack_two, pack_three, pack_four, held_one, held_two, held_three, held_four,
     tap_sums, core_in, first_in, partial, pooling, pooled_low, d_logits, d_act, head_buf, grad_buf, send, recv, local,
 ):
     (z, y, x, core), (nz, ny, nx, nc) = place()
@@ -115,6 +115,11 @@
         part = target.at[across_z, y, x, core]
         return [copies.start(part, part, at(k, y, x, core)) for k in near_z]
 
+    lane = lax.broadcasted_iota(jnp.int32, norms.shape, 1)
+    own_width = own_norms.shape[1]
+    mine = (lane >= c * own_width) & (lane < (c + 1) * own_width)
+    norms[...] = jnp.where(mine, jnp.concatenate([own_norms[...]] * n, axis=1), 0.0)
+
     weights_z = pass_z(weights_out, begin_z(weights, weights_out, 0))
     norm_copies = [copies.start(norms, norms_held.at[k + 1], {"chan": other}) for k, other in enumerate(others)]
     image_copies = [[copies.start(images.at[k, j], own_images.at[c, j, pl.ds(0, line)], {"chan": k}) for k in others]
@@ -122,6 +127,14 @@
     own = pltpu.make_async_copy(images.at[c], own_images.at[c, :, pl.ds(0, line)], local.at[2])
     own.start()
     norms_held[0] = norms[...]
+
+    own_slots = pl.ds(pl.multiple_of(c * slots, slots), slots)
+    mask = pixel_mask[own_slots, :].astype(f32)
+    for p in range(pixels):
+        valid[p * slots : (p + 1) * slots, :] = jnp.broadcast_to(mask[:, p : p + 1], (slots, 128))
+    filled = jnp.broadcast_to(jnp.sum(mask, axis=1, keepdims=True), (slots, 128))
+    used[...] = (filled > 0.0).astype(f32)
+    divisor[...] = jnp.maximum(filled, 1.0)
 
     def clear(i, _):
         rows = pl.ds(pl.multiple_of(i * slots, slots), slots)
@@ -276,7 +289,7 @@
     logits = dot(pooled_low[...], head_low[...], 1, 0) + bias[...]
     classes = logits.shape[1]
     index = lax.broadcasted_iota(jnp.int32, (slots, classes), 1)
-    onehot = (index == labels[:, :1]).astype(f32)
+    onehot = (index == all_labels[own_slots, :]).astype(f32)
     top = jnp.max(logits, axis=1, keepdims=True)
     log_total = jnp.log(jnp.sum(jnp.exp(logits - top), axis=1, keepdims=True)) + top
     picked = jnp.sum(onehot * logits, axis=1, keepdims=True)
@@ -447,10 +460,10 @@
         copy.wait()
 
 
-def local_step(images, weights, roots, norms, valid, labels, used, divisor, bias):
+def local_step(images, weights, roots, norms, pixel_mask, labels, bias):
     n, nb = lax.axis_size("chan"), lax.axis_size("batch")
     nz, nx = n // 2, nb // 2
-    slots, width = used.shape[0], norms.shape[1]
+    slots, width = pixel_mask.shape[0] // n, norms.shape[1] * n
     line, depth, classes = SIDE * slots, images.shape[-1], bias.shape[1]
     f32, low = jnp.float32, jnp.bfloat16
     rows = weights.shape[0] // nb
@@ -474,7 +487,7 @@
             gathered(weights),
             gathered(roots),
         ),
-        in_specs=[ANY, ANY, ANY, VMEM, VMEM, VMEM, VMEM, VMEM, VMEM],
+        in_specs=[ANY, ANY, ANY, VMEM, VMEM, VMEM, VMEM],
         out_specs=(ANY, ANY, ANY, VMEM, ANY, ANY),
         scratch_shapes=[
             pltpu.VMEM((n, SIDE, line + slots, depth), low),
@@ -484,7 +497,11 @@
             pltpu.VMEM(grids, low),
             pltpu.VMEM((width, SIDE * (line + slots)), low),
             weight(9 * width), weight(n * depth), weight(classes),
-            pltpu.VMEM((n,) + norms.shape, f32),
+            pltpu.VMEM((SIDE * line, 128), f32),
+            pltpu.VMEM((slots, 128), f32),
+            pltpu.VMEM((slots, 128), f32),
+            pltpu.VMEM((norms.shape[0], width), f32),
+            pltpu.VMEM((n, norms.shape[0], width), f32),
             pack(two + 8), pack(two), pack(three), pack(two),
             held(two + 8), held(two), held(three), held(two),
             pltpu.VMEM((9, nz, 2, nx, rows, width), f32),
@@ -501,7 +518,7 @@
         ],
         compiler_params=pltpu.CompilerParams(collective_id=0, has_side_effects=True, vmem_limit_bytes=60 << 20),
         name="step",
-    )(images.reshape(n, SIDE, line, depth), quarters(weights), quarters(roots), norms, valid, labels, used, divisor, bias)
+    )(images.reshape(n, SIDE, line, depth), quarters(weights), quarters(roots), norms, pixel_mask, labels, bias)
     return spatial, reduce, head, totals[:three], totals[three:], roots_full.reshape(width, roots.shape[1])
 
 
@@ -813,61 +830,85 @@
 
 
 def finish_kernel(
-    tiles_one, own, head_a, head_b, left_part, right_part, outer, size, left_stats, right_stats,
-    reduce_weight, spatial_weight, reduce_mask, spatial_mask, head_weight, head_first, head_second,
-    reduce_grad, spatial_grad, reduce_new, spatial_new, left_new, right_new, head_new, head_first_new, head_second_new,
+    size, head_weight, head_first, head_second,
+    own, left_part, right_part, outer, left_stats, right_stats, reduce_weight, spatial_weight, reduce_mask, spatial_mask,
+    head_new, head_first_new, head_second_new,
+    reduce_grad, spatial_grad, reduce_new, spatial_new, left_new, right_new,
+    own_rows, lefts, rights, outers, left_kept, right_kept, weights, masks, arrive, leave,
 ):
-    t = pl.program_id(0)
-    left_new[0] = 0.95 * left_stats[0] + left_part[0]
-    right_new[0] = 0.95 * right_stats[0] + right_part[0]
-    step = outer[0] / jnp.concatenate([size[pl.ds(t, 1), :]] * (outer.shape[-1] // 128), axis=1)
-
-    def leave(weight, mask, grad, new):
-        grad[...] = own[...]
-        new[...] = weight[...] - 0.02 * mask[...].astype(jnp.float32) * (step + 0.1 * weight[...])
-
-    @pl.when(t < tiles_one)
-    def _():
-        leave(reduce_weight, reduce_mask, reduce_grad, reduce_new)
-
-    @pl.when(t >= tiles_one)
-    def _():
-        leave(spatial_weight, spatial_mask, spatial_grad, spatial_new)
-
-    @pl.when(t == 0)
-    def _():
-        head_grad = jnp.concatenate([head_a[...], head_b[...]], axis=1)[:, : head_weight.shape[1]]
-        head_new[...], head_first_new[...], head_second_new[...] = adam_step(
-            head_weight[...], head_grad, head_first[...], head_second[...], 0.04, 0.1)
+    blocks, rows, width = outers.shape
+    c_in, taps = reduce_weight.shape[1], spatial_weight.shape[1]
+    tiles_one = c_in // width
+    groups = [(0, tiles_one)] + [(t, min(t + 3, blocks)) for t in range(tiles_one, blocks, 3)]
+    every = [pltpu.make_async_copy(own, own_rows, arrive.at[0, 7])]
+    coming = []
+    for g, (begin, end) in enumerate(groups):
+        some, columns = pl.ds(begin, end - begin), pl.ds(begin * width, (end - begin) * width)
+        theirs = pl.ds((begin if g == 0 else begin - tiles_one) * width, (end - begin) * width)
+        pairs = [(a.at[some], b.at[some]) for a, b in (
+            (left_part, lefts), (right_part, rights), (outer, outers), (left_stats, left_kept), (right_stats, right_kept))]
+        pairs += [((reduce_weight if g == 0 else spatial_weight).at[:, theirs], weights.at[:, columns]),
+                  ((reduce_mask if g == 0 else spatial_mask).at[:, theirs], masks.at[:, columns])]
+        coming.append([pltpu.make_async_copy(a, b, arrive.at[g, i]) for i, (a, b) in enumerate(pairs)])
+    for copy in every + [copy for group in coming for copy in group]:
+        copy.start()
+    going = []
+
+    def out(source, target):
+        copy = pltpu.make_async_copy(source, target, leave.at[len(going)])
+        copy.start()
+        going.append(copy)
+
+    every[0].wait()
+    out(own_rows.at[:, pl.ds(0, taps)], spatial_grad)
+    out(own_rows.at[:, pl.ds(taps, c_in)], reduce_grad)
+    head_grad = own_rows[:, taps + c_in : taps + c_in + head_weight.shape[1]]
+    head_new[...], head_first_new[...], head_second_new[...] = adam_step(
+        head_weight[...], head_grad, head_first[...], head_second[...], 0.04, 0.1)
+    for g, (begin, end) in enumerate(groups):
+        for copy in coming[g]:
+            copy.wait()
+
+        def block(t, _):
+            columns = pl.ds(pl.multiple_of(t * width, width), width)
+            lefts[t] = 0.95 * left_kept[t] + lefts[t]
+            rights[t] = 0.95 * right_kept[t] + rights[t]
+            step = outers[t] / jnp.concatenate([size[pl.ds(t, 1), :]] * (width // 128), axis=1)
+            weight = weights[:, columns]
+            weights[:, columns] = weight - 0.02 * masks[:, columns].astype(jnp.float32) * (step + 0.1 * weight)
+            return 0
+
+        lax.fori_loop(begin, end, block, 0)
+        some, columns = pl.ds(begin, end - begin), pl.ds(begin * width, (end - begin) * width)
+        theirs = pl.ds((begin if g == 0 else begin - tiles_one) * width, (end - begin) * width)
+        out(lefts.at[some], left_new.at[some])
+        out(rights.at[some], right_new.at[some])
+        out(weights.at[:, columns], (reduce_new if g == 0 else spatial_new).at[:, theirs])
+    for copy in going:
+        copy.wait()
 
 
 def finish(own, left_part, right_part, outer, size, left_stats, right_stats,
            reduce_weight, spatial_weight, reduce_mask, spatial_mask, head_weight, head_first, head_second):
     blocks, rows, width = left_stats.shape
-    tiles_one, taps = reduce_weight.shape[1] // width, spatial_weight.shape[1] // width
-    columns = lambda index: pl.BlockSpec((rows, width), lambda t: (0, index(t)))
-    of_block = pl.BlockSpec((1, rows, width), lambda t: (t, 0, 0))
-    whole = lambda a: pl.BlockSpec(a.shape, lambda t: (0, 0))
-    of_reduce = columns(lambda t: jnp.minimum(t, tiles_one - 1))
-    of_spatial = columns(lambda t: jnp.maximum(t - tiles_one, 0))
     like = lambda a: jax.ShapeDtypeStruct(a.shape, jnp.float32)
-    return pl.pallas_call(
-        functools.partial(finish_kernel, tiles_one),
-        grid=(blocks,),
-        out_shape=(like(reduce_weight), like(spatial_weight), like(reduce_weight), like(spatial_weight),
-                   like(left_stats), like(left_stats), like(head_weight), like(head_weight), like(head_weight)),
-        in_specs=[
-            columns(lambda t: jnp.where(t < tiles_one, taps + t, t - tiles_one)),
-            columns(lambda t: taps + tiles_one), columns(lambda t: taps + tiles_one + 1),
-            of_block, of_block, of_block, whole(size), of_block, of_block,
-            of_reduce, of_spatial, of_reduce, of_spatial, whole(head_weight), whole(head_weight), whole(head_weight),
-        ],
-        out_specs=(of_reduce, of_spatial, of_reduce, of_spatial, of_block, of_block,
-                   whole(head_weight), whole(head_weight), whole(head_weight)),
+    wide = reduce_weight.shape[1] + spatial_weight.shape[1]
+    products = pltpu.VMEM(left_stats.shape, jnp.float32)
+    groups = 1 + -(-(spatial_weight.shape[1] // width) // 3)
+    head_new, head_first_new, head_second_new, *rest = pl.pallas_call(
+        finish_kernel,
+        out_shape=(like(head_weight), like(head_weight), like(head_weight), like(reduce_weight), like(spatial_weight),
+                   like(reduce_weight), like(spatial_weight), like(left_stats), like(left_stats)),
+        in_specs=[VMEM] * 4 + [ANY] * 10,
+        out_specs=(VMEM,) * 3 + (ANY,) * 6,
+        scratch_shapes=[pltpu.VMEM(own.shape, jnp.float32)] + [products] * 5
+        + [pltpu.VMEM((rows, wide), jnp.float32), pltpu.VMEM((rows, wide), jnp.int32),
+           DMA((groups, 8)), DMA((2 + 3 * groups,))],
         compiler_params=pltpu.CompilerParams(vmem_limit_bytes=60 << 20),
         name="finish",
-    )(own, own, own, left_part, right_part, outer, size, left_stats, right_stats,
-      reduce_weight, spatial_weight, reduce_mask, spatial_mask, head_weight, head_first, head_second)
+    )(size, head_weight, head_first, head_second, own, left_part, right_part, outer, left_stats, right_stats,
+      reduce_weight, spatial_weight, reduce_mask, spatial_mask)
+    return *rest, head_new, head_first_new, head_second_new
 
 
 def silu_slope(pre):
@@ -923,19 +964,13 @@
     reduce_float = reduce_mask.astype(f32)
     spatial_float = spatial_mask.astype(f32)
 
-    spread_out = lambda a: jnp.broadcast_to(a[:, None], (a.shape[0], 128))
     by_pixel = images.reshape(n, slots, pixels, channels).transpose(0, 2, 1, 3)
     weights = jnp.concatenate(
         [(spatial_weight * spatial_float).astype(low), (reduce_weight * reduce_float).astype(low),
          jnp.pad(head_weight.astype(low), ((0, 0), (0, padded - classes)))], axis=1)
     roots = input_side_roots.astype(low).transpose(1, 0, 2).reshape(rows_out, -1)
-    norms = lax.dynamic_update_slice_in_dim(
-        jnp.zeros((8, width), f32), jnp.pad(norm_params, ((0, 4), (0, 0))), lax.axis_index("chan") * rows_out, 1)
-    mask_own = own_part(pixel_mask, 0).astype(f32)
-    filled = jnp.sum(mask_own, axis=1)
     taps_local, reduce_local, head_local, sums_two, sums_one, roots_full = local_step(
-        by_pixel, weights, roots, norms, spread_out(mask_own.T.reshape(-1)), spread_out(own_part(labels, 0)),
-        spread_out((filled > 0.0).astype(f32)), spread_out(jnp.maximum(filled, 1.0)),
+        by_pixel, weights, roots, norm_params, pixel_mask, labels[:, None],
         jnp.pad(head_bias, (0, padded - classes), constant_values=-1e30)[None])
 
     mask_rows = jnp.concatenate([spatial_float, reduce_float, jnp.ones((rows_out, padded), f32)], axis=1)

time: 473 us -> 464 us (0.981)
  no operation moved by 1% of the time
where the time goes in v6:
time: 464 us
  Pallas kernels  443 us (95%)
  local copies, waits for them, and re-layouts  14.9 us (3%)
    pallas_call x1, Pallas kernels, local_step(): pl.pallas_call(step_kernel, out_shape=(shape((9, nz, 2, rows, width), f32...  336 us
    pallas_call x1, Pallas kernels, settle(): pl.pallas_call(functools.partial(settle_kernel, chunks), out_shape=(jax.S...  97.2 us
    pallas_call x1, Pallas kernels, finish(): pl.pallas_call(finish_kernel, out_shape=(like(head_weight), like(head_wei...  10.1 us

profile of v6, /device:TPU:0, one launch (start us, length us, event | category | flops | bytes accessed | tf_op | source)
XLA Modules:
  0.0 463.7 jit_solution(14924749317573202599)
XLA Ops:
  0.7 0.0 copy-start.2
  0.7 0.0 copy-start.3
  0.7 0.0 copy-start.1
  0.7 8.3 %copy.40 = bf16[8,48,49,256]{3,1,2,0:T(8,128)(2,1)} copy(bf16[8,48,49,256]{3,1,0,2:T(8,128)(2,1)} %bitcast.20) | data formatting | bytes 19267584 | tf_op jit(solution)/shard_map/reshape | solution.py:967
  9.0 1.1 convert_element_type.24
  10.1 0.1 multiply_convert_fusion.1
  10.2 0.2 copy-done
  10.4 0.1 multiply_convert_fusion
  10.5 0.0 copy-start.4
  10.5 1.0 fusion.1
  11.5 0.8 copy-done.4
  12.3 0.1 convert_bitcast_fusion
  12.4 0.0 copy-start.5
  12.4 0.0 copy-start.11
  12.4 0.0 copy-start.6
  12.4 0.5 copy.41
  12.9 1.5 reshape_reshape.3.roots
  14.5 0.8 copy.42.pixel_mask
  15.3 0.8 broadcast_in_dim.12.all_labels
  16.1 0.6 pad.9
  16.7 336.0 %step.1 = (f32[9,4,2,16,512]{4,3,2,1,0:T(8,128)}, f32[4,2,2,2,16,2048]{5,4,3,2,1,0:T(8,128)}, f32[512,1024]{1,0:T(8,128)}, f32[24,128]{1,0:T(8,128)}, bf16[4,2,2...) custom-call(bf16[8,7,336,256]{3,2,1,0:T(8,128)(2,1)} %bitcast.19, ...), custom_call_target="tpu_custom_call" | custom-call | tf_op jit(solution)/shard_map/step/pallas_call | solution.py:480
  352.7 0.7 slice_bitcast_fusion
  353.4 0.6 fusion.12
  354.0 0.1 convert_element_type.20
  354.1 0.8 fusion.3.mask
  355.0 97.2 %settle.1 = (f32[2,2,16,7680]{3,2,1,0:T(8,128)}, f32[13,64,512]{2,1,0:T(8,128)}, f32[13,64,512]{2,1,0:T(8,128)}, f32[13,64,512]{2,1,0:T(8,128)}, f32[16,128]{1,0:T(8,128)}) custom-call(f32[9,4,2,16,512]{4,3,2,1,0:T(8,128)} %get-tuple-element.37.taps, f32[4,2,2,2,16,2048]{5,4,3,2,1,0:T(8,128)} %get-tuple-element.38.reduce, ...), custom_call_target="tpu_custom_call" | custom-call | tf_op jit(solution)/shard_map/settle/pallas_call | solution.py:800
  452.2 0.0 copy-start.9
  452.2 0.0 copy-start.10
  452.2 0.0 copy-start.8
  452.2 10.1 %finish.1 = (f32[64,1000]{1,0:T(8,128)}, f32[64,1000]{1,0:T(8,128)}, f32[64,1000]{1,0:T(8,128)}, f32[64,2048]{1,0:T(8,128)}, f32[64,4608]{1,0:T(8,128)}, /*index...) custom-call(f32[16,128]{1,0:T(8,128)} %get-tuple-element.41.size, ...), custom_call_target="tpu_custom_call" | custom-call | tf_op jit(solution)/shard_map/finish/pallas_call | solution.py:898
  462.4 0.6 multiply_subtract_fusion
  463.0 0.7 multiply_subtract_fusion.1
  (20 shorter events, 0.1 us)
Async XLA Ops:
  0.7 9.4 %copy-start.2 = (s32[64,2048]{1,0:T(8,128)S(1)}, s32[64,2048]{1,0:T(8,128)}, u32[]{:S(2)}) copy-start(s32[64,2048]{1,0:T(8,128)} %reduce_mask.1) | copy-start | bytes 1572868
  0.7 9.4 %copy-start.3 = (f32[64,2048]{1,0:T(8,128)S(1)}, f32[64,2048]{1,0:T(8,128)}, u32[]{:S(2)}) copy-start(f32[64,2048]{1,0:T(8,128)} %reduce_weight.1) | copy-start | bytes 1572868
  0.7 9.5 %copy-start.1 = (f32[64,4608]{1,0:T(8,128)S(1)}, f32[64,4608]{1,0:T(8,128)}, u32[]{:S(2)}) copy-start(f32[64,4608]{1,0:T(8,128)} %spatial_weight.1) | copy-start | bytes 3538948
  9.0 1.3 copy-start
  10.5 1.8 copy-start.4
  12.4 2.1 copy-start.5
  12.4 2.9 copy-start.11
  12.4 3.6 copy-start.6
  452.2 10.2 %copy-start.9 = (f32[1000]{0:T(1024)S(1)}, f32[1000]{0:T(1024)}, u32[]{:S(2)}) copy-start(f32[1000]{0:T(1024)} %param.36) | copy-start | bytes 12004
  452.2 10.2 %copy-start.10 = (f32[1000]{0:T(1024)S(1)}, f32[1000]{0:T(1024)}, u32[]{:S(2)}) copy-start(f32[1000]{0:T(1024)} %param.37) | copy-start | bytes 12004
  452.2 10.8 %copy-start.7 = (f32[24,128]{1,0:T(8,128)S(1)}, f32[24,128]{1,0:T(8,128)}, u32[]{:S(2)}) copy-start(f32[24,128]{1,0:T(8,128)} %get-tuple-element.36) | copy-start | bytes 36868
  452.2 10.8 %copy-start.8 = (f32[4,64]{1,0:T(4,128)S(1)}, f32[4,64]{1,0:T(4,128)}, u32[]{:S(2)}) copy-start(f32[4,64]{1,0:T(4,128)} %own_norms.1) | copy-start | bytes 3076
  452.2 10.8 %copy-start.12 = (f32[4,64]{1,0:T(4,128)S(1)}, f32[4,64]{1,0:T(4,128)}, u32[]{:S(2)}) copy-start(f32[4,64]{1,0:T(4,128)} %param.38) | copy-start | bytes 3076
  452.2 10.8 %copy-start.13 = (f32[4,64]{1,0:T(4,128)S(1)}, f32[4,64]{1,0:T(4,128)}, u32[]{:S(2)}) copy-start(f32[4,64]{1,0:T(4,128)} %param.39) | copy-start | bytes 3076

commit v7 on v6

--- a/solution.py
+++ b/solution.py
@@ -73,8 +73,10 @@
 
 
 def step_kernel(
-    images, weights, roots, own_norms, pixel_mask, all_labels, bias,
-    taps_out, reduce_out, head_out, totals_out, weights_out, roots_out,
+    images, spatial_weight, spatial_mask, reduce_weight, reduce_mask, head_weight, input_roots,
+    own_norms, pixel_mask, all_labels, bias,
+    taps_out, reduce_out, head_out, totals_out, mask_out, weights_out, roots_out,
+    raw_spatial, raw_spatial_mask, raw_reduce, raw_reduce_mask, raw_head, raw_roots, weights, roots,
     own_images, first, second, hidden_pad, grad_pad, turned_grad, taps, reduce_low, head_low,
     valid, used, divisor, norms, norms_held, pack_one, pack_two, pack_three, pack_four, held_one, held_two, held_three, held_four,
     tap_sums, core_in, first_in, partial, pooling, pooled_low, d_logits, d_act, head_buf, grad_buf, send, recv, local,
@@ -95,19 +97,35 @@
         at(lax.rem(z + i, nz), lax.rem(y + j, ny), lax.rem(x + k, nx), lax.rem(core + m, nc))
         for i in range(nz) for j in range(ny) for k in range(nx) for m in range(nc) if i + j + k + m
     ]
+    row_count = weights.shape[0]
+    quarter = pl.ds(pl.multiple_of((x * nc + core) * row_count, row_count), row_count)
+    raw = ((spatial_weight, raw_spatial), (spatial_mask, raw_spatial_mask), (reduce_weight, raw_reduce),
+           (reduce_mask, raw_reduce_mask), (head_weight, raw_head))
+    raw = [pltpu.make_async_copy(a.at[quarter], b, local.at[9 + i]) for i, (a, b) in enumerate(raw)]
+    raw.append(pltpu.make_async_copy(input_roots.at[:, quarter], raw_roots, local.at[9 + len(raw)]))
+    for copy in raw:
+        copy.start()
     greet(everyone)
     copies = Copies(send, recv)
     others = turned(c, n)
+    for copy in raw:
+        copy.wait()
+    size_taps, size_reduce = raw_spatial.shape[1], raw_reduce.shape[1]
+    size_both = size_taps + size_reduce
+    weights[:, size_both:] = jnp.zeros((row_count, weights.shape[1] - size_both), low)
+    weights[:, :size_taps] = (raw_spatial[...] * raw_spatial_mask[...].astype(f32)).astype(low)
+    weights[:, size_taps:size_both] = (raw_reduce[...] * raw_reduce_mask[...].astype(f32)).astype(low)
+    weights[:, size_both : size_both + raw_head.shape[1]] = raw_head[...].astype(low)
     across_z = lax.rem(z + nz // 2, nz)
     near_z = [z // (nz // 2) * (nz // 2) + lax.rem(lax.rem(z, nz // 2) + k, nz // 2) for k in range(1, nz // 2)]
     mate, mate_y = at(z, y, x, 1 - core), at(z, 1 - y, x, core)
     mates_x = [at(z, y, k, core) for k in turned(x, nx)]
 
     def begin_z(source, target, sem):
-        keep = pltpu.make_async_copy(source.at[x, core], target.at[z, y, x, core], local.at[sem])
+        keep = pltpu.make_async_copy(source, target.at[z, y, x, core], local.at[sem])
         keep.start()
         peers = [at(k, y, x, core) for k in [across_z] + near_z]
-        return [keep] + [copies.start(source.at[x, core], target.at[z, y, x, core], peer) for peer in peers]
+        return [keep] + [copies.start(source, target.at[z, y, x, core], peer) for peer in peers]
 
     def pass_z(target, begun):
         for copy in begun:
@@ -127,6 +145,12 @@
     own = pltpu.make_async_copy(images.at[c], own_images.at[c, :, pl.ds(0, line)], local.at[2])
     own.start()
     norms_held[0] = norms[...]
+
+    for t in range(raw_roots.shape[0]):
+        roots[:, t * width : (t + 1) * width] = raw_roots[t].astype(low)
+    mask_out[:, :size_taps] = raw_spatial_mask[...].astype(f32)
+    mask_out[:, size_taps:size_both] = raw_reduce_mask[...].astype(f32)
+    mask_out[:, size_both:] = jnp.ones((row_count, mask_out.shape[1] - size_both), f32)
 
     own_slots = pl.ds(pl.multiple_of(c * slots, slots), slots)
     mask = pixel_mask[own_slots, :].astype(f32)
@@ -460,36 +484,43 @@
         copy.wait()
 
 
-def local_step(images, weights, roots, norms, pixel_mask, labels, bias):
+def local_step(images, spatial_weight, spatial_mask, reduce_weight, reduce_mask, head_weight, roots,
+               norms, pixel_mask, labels, bias):
     n, nb = lax.axis_size("chan"), lax.axis_size("batch")
     nz, nx = n // 2, nb // 2
     slots, width = pixel_mask.shape[0] // n, norms.shape[1] * n
     line, depth, classes = SIDE * slots, images.shape[-1], bias.shape[1]
     f32, low = jnp.float32, jnp.bfloat16
-    rows = weights.shape[0] // nb
+    rows = spatial_weight.shape[0] // nb
+    wide_weights, wide_roots = spatial_weight.shape[1] + reduce_weight.shape[1] + classes, roots.shape[0] * roots.shape[2]
     grids = ((SIDE * (SIDE + 1) + 2 * (SIDE + 2)) * slots, width)
     shape = jax.ShapeDtypeStruct
-    gathered = lambda a: shape((nz, 2, nx, 2, rows, a.shape[1]), a.dtype)
-    quarters = lambda a: a.reshape(nx, 2, rows, a.shape[1])
+    gathered = lambda size: shape((nz, 2, nx, 2, rows, size), low)
+    raw = lambda a: pltpu.VMEM((rows, a.shape[1]), a.dtype)
     held = lambda k: pltpu.VMEM((n * nb, k, 128), f32)
     pack = lambda k: pltpu.VMEM((k, 128), f32)
     count = 2 * (nz - 1) + (SIDE + 1) * (n - 1) + (1 + (nx - 1) + 1) + (2 * nx + 1) + 4 * (n * nb - 1) + 27
     two = 2 * width // 128
     three = two + classes // 128
     weight = lambda size: pltpu.VMEM((nz, 2, nx, 2, rows, size), low)
-    spatial, reduce, head, totals, weights_full, roots_full = pl.pallas_call(
+    taps, reduce, head, totals, mask, _, roots_full = pl.pallas_call(
         step_kernel,
         out_shape=(
             shape((9, nz, 2, rows, width), f32),
             shape((nz, 2, nx, 2, rows, n * depth), f32),
             shape((width, classes), f32),
             shape((two + three, 128), f32),
-            gathered(weights),
-            gathered(roots),
+            shape((rows, wide_weights), f32),
+            gathered(wide_weights),
+            gathered(wide_roots),
         ),
-        in_specs=[ANY, ANY, ANY, VMEM, VMEM, VMEM, VMEM],
-        out_specs=(ANY, ANY, ANY, VMEM, ANY, ANY),
+        in_specs=[ANY] * 7 + [VMEM] * 4,
+        out_specs=(ANY, ANY, ANY, VMEM, VMEM, ANY, ANY),
         scratch_shapes=[
+            raw(spatial_weight), raw(spatial_mask), raw(reduce_weight), raw(reduce_mask), raw(head_weight),
+            pltpu.VMEM((roots.shape[0], rows, width), f32),
+            pltpu.VMEM((rows, wide_weights), low),
+            pltpu.VMEM((rows, wide_roots), low),
             pltpu.VMEM((n, SIDE, line + slots, depth), low),
             pltpu.VMEM((SIDE * line, width), f32),
             pltpu.VMEM((SIDE * line, width), f32),
@@ -518,8 +549,9 @@
         ],
         compiler_params=pltpu.CompilerParams(collective_id=0, has_side_effects=True, vmem_limit_bytes=60 << 20),
         name="step",
-    )(images.reshape(n, SIDE, line, depth), quarters(weights), quarters(roots), norms, pixel_mask, labels, bias)
-    return spatial, reduce, head, totals[:three], totals[three:], roots_full.reshape(width, roots.shape[1])
+    )(images.reshape(n, SIDE, line, depth), spatial_weight, spatial_mask, reduce_weight, reduce_mask, head_weight, roots,
+      norms, pixel_mask, labels, bias)
+    return taps, reduce, head, totals[:three], totals[three:], mask, roots_full.reshape(width, wide_roots)
 
 
 def chunk_rounds(count):
@@ -959,22 +991,14 @@
     classes = head_weight.shape[1]
     padded = 1024
     slots = images.shape[0] // n
-    low = jnp.bfloat16
     f32 = jnp.float32
-    reduce_float = reduce_mask.astype(f32)
-    spatial_float = spatial_mask.astype(f32)
 
     by_pixel = images.reshape(n, slots, pixels, channels).transpose(0, 2, 1, 3)
-    weights = jnp.concatenate(
-        [(spatial_weight * spatial_float).astype(low), (reduce_weight * reduce_float).astype(low),
-         jnp.pad(head_weight.astype(low), ((0, 0), (0, padded - classes)))], axis=1)
-    roots = input_side_roots.astype(low).transpose(1, 0, 2).reshape(rows_out, -1)
-    taps_local, reduce_local, head_local, sums_two, sums_one, roots_full = local_step(
-        by_pixel, weights, roots, norm_params, pixel_mask, labels[:, None],
+    taps_local, reduce_local, head_local, sums_two, sums_one, mask_rows, roots_full = local_step(
+        by_pixel, spatial_weight, spatial_mask, reduce_weight, reduce_mask, head_weight, input_side_roots, norm_params, pixel_mask, labels[:, None],
         jnp.pad(head_bias, (0, padded - classes), constant_values=-1e30)[None])
 
-    mask_rows = jnp.concatenate([spatial_float, reduce_float, jnp.ones((rows_out, padded), f32)], axis=1)
-    own, *products = settle(taps_local, reduce_local, head_local, own_part(mask_rows, 0, "batch"), left_root, roots_full)
+    own, *products = settle(taps_local, reduce_local, head_local, mask_rows, left_root, roots_full)
     of_norms = jnp.stack([a.reshape(-1) for a in (sums_one[4:], sums_one[:4], sums_two[4:8], sums_two[:4])])
     norm_gain_gradient = own_part(of_norms, 1)
     of_head = sums_two[8:].reshape(-1)

time: 464 us -> 457 us (0.985)
  no operation moved by 1% of the time
where the time goes in v7:
time: 457 us; the launch traced here: 456 us
  Pallas kernels  443 us (97%)
  local copies, waits for them, and re-layouts  11.1 us (2%)
    pallas_call x1, Pallas kernels, local_step(): pl.pallas_call(step_kernel, out_shape=(shape((9, nz, 2, rows, width), f32...  336 us
    pallas_call x1, Pallas kernels, settle(): pl.pallas_call(functools.partial(settle_kernel, chunks), out_shape=(jax.S...  97 us
    pallas_call x1, Pallas kernels, finish(): pl.pallas_call(finish_kernel, out_shape=(like(head_weight), like(head_wei...  10.1 us

profile of v7, /device:TPU:0, one launch (start us, length us, event | category | flops | bytes accessed | tf_op | source)
XLA Modules:
  0.0 456.4 jit_solution(10859145817379083541)
XLA Ops:
  0.7 0.0 copy-start.6
  0.7 0.0 copy-start
  0.7 0.0 copy-start.1
  0.7 8.2 %copy.39 = bf16[8,48,49,256]{3,1,2,0:T(8,128)(2,1)} copy(bf16[8,48,49,256]{3,1,0,2:T(8,128)(2,1)} %bitcast.17) | data formatting | bytes 19267584 | tf_op jit(solution)/shard_map/reshape | solution.py:996
  8.9 0.0 copy-done.6
  8.9 0.8 broadcast_in_dim.8.all_labels
  9.7 0.0 copy-done
  9.7 0.8 copy.40.pixel_mask
  10.5 0.0 copy-done.1
  10.5 0.6 pad.4
  11.1 336.1 %step.1 = (f32[9,4,2,16,512]{4,3,2,1,0:T(8,128)}, f32[4,2,2,2,16,2048]{5,4,3,2,1,0:T(8,128)}, f32[512,1024]{1,0:T(8,128)}, f32[24,128]{1,0:T(8,128)}, f32[16,768...) custom-call(bf16[8,7,336,256]{3,2,1,0:T(8,128)(2,1)} %bitcast.16, ...), custom_call_target="tpu_custom_call" | custom-call | tf_op jit(solution)/shard_map/step/pallas_call | solution.py:506
  347.2 97.0 %settle.1 = (f32[2,2,16,7680]{3,2,1,0:T(8,128)}, f32[13,64,512]{2,1,0:T(8,128)}, f32[13,64,512]{2,1,0:T(8,128)}, f32[13,64,512]{2,1,0:T(8,128)}, f32[16,128]{1,0:T(8,128)}) custom-call(f32[9,4,2,16,512]{4,3,2,1,0:T(8,128)} %get-tuple-element.38.taps, f32[4,2,2,2,16,2048]{5,4,3,2,1,0:T(8,128)} %get-tuple-element.39.reduce, ...), custom_call_target="tpu_custom_call" | custom-call | tf_op jit(solution)/shard_map/settle/pallas_call | solution.py:832
  444.2 0.0 copy-start.2
  444.3 0.0 copy-start.3
  444.3 0.0 copy-start.7
  444.3 0.0 copy-start.8
  444.3 0.0 copy-start.4
  444.3 0.0 copy-start.5
  444.3 10.1 %finish.1 = (f32[64,1000]{1,0:T(8,128)}, f32[64,1000]{1,0:T(8,128)}, f32[64,1000]{1,0:T(8,128)}, f32[64,2048]{1,0:T(8,128)}, f32[64,4608]{1,0:T(8,128)}, /*index...) custom-call(f32[16,128]{1,0:T(8,128)} %get-tuple-element.43.size, ...), custom_call_target="tpu_custom_call" | custom-call | tf_op jit(solution)/shard_map/finish/pallas_call | solution.py:930
  454.4 0.0 copy-done.2
  454.5 0.0 copy-done.3
  454.5 0.0 copy-done.7
  454.5 0.0 copy-done.8
  454.5 0.7 multiply_subtract_fusion.1
  455.2 0.0 copy-done.4
  455.2 0.0 copy-done.5
  455.2 0.6 multiply_subtract_fusion
  455.8 0.6 fusion.8
  (2 shorter events, 0.0 us)
Async XLA Ops:
  0.7 8.3 %copy-start.6 = (s32[384]{0:T(512)S(1)}, s32[384]{0:T(512)}, u32[]{:S(2)}) copy-start(s32[384]{0:T(512)} %param.22) | copy-start | bytes 4612
  0.7 9.0 %copy-start = (s32[384,49]{0,1:T(8,128)S(1)}, s32[384,49]{0,1:T(8,128)}, u32[]{:S(2)}) copy-start(s32[384,49]{0,1:T(8,128)} %param.21) | copy-start | bytes 225796
  0.7 9.8 %copy-start.1 = (f32[1000]{0:T(1024)S(1)}, f32[1000]{0:T(1024)}, u32[]{:S(2)}) copy-start(f32[1000]{0:T(1024)} %param.28) | copy-start | bytes 12004
  444.2 10.2 %copy-start.2 = (f32[24,128]{1,0:T(8,128)S(1)}, f32[24,128]{1,0:T(8,128)}, u32[]{:S(2)}) copy-start(f32[24,128]{1,0:T(8,128)} %get-tuple-element.37) | copy-start | bytes 36868
  444.3 10.2 %copy-start.3 = (f32[4,64]{1,0:T(4,128)S(1)}, f32[4,64]{1,0:T(4,128)}, u32[]{:S(2)}) copy-start(f32[4,64]{1,0:T(4,128)} %own_norms.1) | copy-start | bytes 3076
  444.3 10.2 %copy-start.7 = (f32[4,64]{1,0:T(4,128)S(1)}, f32[4,64]{1,0:T(4,128)}, u32[]{:S(2)}) copy-start(f32[4,64]{1,0:T(4,128)} %param.38) | copy-start | bytes 3076
  444.3 10.2 %copy-start.8 = (f32[4,64]{1,0:T(4,128)S(1)}, f32[4,64]{1,0:T(4,128)}, u32[]{:S(2)}) copy-start(f32[4,64]{1,0:T(4,128)} %param.39) | copy-start | bytes 3076
  444.3 10.9 %copy-start.4 = (f32[1000]{0:T(1024)S(1)}, f32[1000]{0:T(1024)}, u32[]{:S(2)}) copy-start(f32[1000]{0:T(1024)} %param.36) | copy-start | bytes 12004
  444.3 10.9 %copy-start.5 = (f32[1000]{0:T(1024)S(1)}, f32[1000]{0:T(1024)}, u32[]{:S(2)}) copy-start(f32[1000]{0:T(1024)} %param.37) | copy-start | bytes 12004

commit v8 on v7

--- a/solution.py
+++ b/solution.py
@@ -39,7 +39,7 @@
     barrier = pltpu.get_barrier_semaphore()
     for peer in peers:
         pl.semaphore_signal(barrier, inc=1, device_id=peer, device_id_type=MESH)
-    pl.semaphore_wait(barrier, len(peers))
+    return lambda: pl.semaphore_wait(barrier, len(peers))
 
 
 class Copies:
@@ -105,7 +105,7 @@
     raw.append(pltpu.make_async_copy(input_roots.at[:, quarter], raw_roots, local.at[9 + len(raw)]))
     for copy in raw:
         copy.start()
-    greet(everyone)
+    greeted = greet(everyone)
     copies = Copies(send, recv)
     others = turned(c, n)
     for copy in raw:
@@ -116,6 +116,7 @@
     weights[:, :size_taps] = (raw_spatial[...] * raw_spatial_mask[...].astype(f32)).astype(low)
     weights[:, size_taps:size_both] = (raw_reduce[...] * raw_reduce_mask[...].astype(f32)).astype(low)
     weights[:, size_both : size_both + raw_head.shape[1]] = raw_head[...].astype(low)
+    greeted()
     across_z = lax.rem(z + nz // 2, nz)
     near_z = [z // (nz // 2) * (nz // 2) + lax.rem(lax.rem(z, nz // 2) + k, nz // 2) for k in range(1, nz // 2)]
     mate, mate_y = at(z, y, x, 1 - core), at(z, 1 - y, x, core)
@@ -579,7 +580,7 @@
     mate_across = at(across_z, y, x, core)
     c, n = lax.axis_index("chan"), lax.axis_size("chan")
     others = [{"chan": k} for k in turned(c, n)]
-    greet(others + mates_x + [mate])
+    greeted = greet(others + mates_x + [mate])
     copies = Copies(send, recv)
     f32, low = jnp.float32, jnp.bfloat16
     rows, width = left_root.shape[1:]
@@ -795,7 +796,10 @@
             block_of(start, columns)
 
     rounds = [[chunk_z(*c[:2]) if c[2] == "z" and c[0] < wide else chunk(*c[:2], c[2] != "y") for c in some] for some in chunks]
-    begun, active = [], []
+    begun, active = rounds.pop(0), []
+    for going in begun:
+        next(going)
+    greeted()
     while rounds or begun or active:
         active += begun
         begun = rounds.pop(0) if rounds else []

time: 457 us -> 454 us (level)
  no operation moved by 1% of the time
where the time goes in v8:
time: 454 us
  Pallas kernels  441 us (97%)
  local copies, waits for them, and re-layouts  11.1 us (2%)
    pallas_call x1, Pallas kernels, local_step(): pl.pallas_call(step_kernel, out_shape=(shape((9, nz, 2, rows, width), f32...  336 us
    pallas_call x1, Pallas kernels, settle(): pl.pallas_call(functools.partial(settle_kernel, chunks), out_shape=(jax.S...  94.8 us
    pallas_call x1, Pallas kernels, finish(): pl.pallas_call(finish_kernel, out_shape=(like(head_weight), like(head_wei...  10.1 us

profile of v8, /device:TPU:0, one launch (start us, length us, event | category | flops | bytes accessed | tf_op | source)
XLA Modules:
  0.0 454.1 jit_solution(17445643021964475784)
XLA Ops:
  0.7 0.0 copy-start.6
  0.7 0.0 copy-start
  0.7 0.0 copy-start.1
  0.7 8.2 %copy.39 = bf16[8,48,49,256]{3,1,2,0:T(8,128)(2,1)} copy(bf16[8,48,49,256]{3,1,0,2:T(8,128)(2,1)} %bitcast.17) | data formatting | bytes 19267584 | tf_op jit(solution)/shard_map/reshape | solution.py:1000
  8.9 0.0 copy-done.6
  8.9 0.8 broadcast_in_dim.8.all_labels
  9.7 0.0 copy-done
  9.7 0.8 copy.40.pixel_mask
  10.5 0.0 copy-done.1
  10.5 0.6 pad.4
  11.1 336.0 %step.1 = (f32[9,4,2,16,512]{4,3,2,1,0:T(8,128)}, f32[4,2,2,2,16,2048]{5,4,3,2,1,0:T(8,128)}, f32[512,1024]{1,0:T(8,128)}, f32[24,128]{1,0:T(8,128)}, f32[16,768...) custom-call(bf16[8,7,336,256]{3,2,1,0:T(8,128)(2,1)} %bitcast.16, ...), custom_call_target="tpu_custom_call" | custom-call | tf_op jit(solution)/shard_map/step/pallas_call | solution.py:507
  347.2 94.8 %settle.1 = (f32[2,2,16,7680]{3,2,1,0:T(8,128)}, f32[13,64,512]{2,1,0:T(8,128)}, f32[13,64,512]{2,1,0:T(8,128)}, f32[13,64,512]{2,1,0:T(8,128)}, f32[16,128]{1,0:T(8,128)}) custom-call(f32[9,4,2,16,512]{4,3,2,1,0:T(8,128)} %get-tuple-element.38.taps, f32[4,2,2,2,16,2048]{5,4,3,2,1,0:T(8,128)} %get-tuple-element.39.reduce, ...), custom_call_target="tpu_custom_call" | custom-call | tf_op jit(solution)/shard_map/settle/pallas_call | solution.py:836
  441.9 0.0 copy-start.2
  441.9 0.0 copy-start.3
  442.0 0.0 copy-start.7
  442.0 0.0 copy-start.8
  442.0 0.0 copy-start.4
  442.0 0.0 copy-start.5
  442.0 10.1 %finish.1 = (f32[64,1000]{1,0:T(8,128)}, f32[64,1000]{1,0:T(8,128)}, f32[64,1000]{1,0:T(8,128)}, f32[64,2048]{1,0:T(8,128)}, f32[64,4608]{1,0:T(8,128)}, /*index...) custom-call(f32[16,128]{1,0:T(8,128)} %get-tuple-element.43.size, ...), custom_call_target="tpu_custom_call" | custom-call | tf_op jit(solution)/shard_map/finish/pallas_call | solution.py:934
  452.1 0.0 copy-done.2
  452.2 0.0 copy-done.3
  452.2 0.0 copy-done.7
  452.2 0.0 copy-done.8
  452.2 0.7 multiply_subtract_fusion.1
  452.9 0.0 copy-done.4
  452.9 0.0 copy-done.5
  452.9 0.6 multiply_subtract_fusion
  453.5 0.6 fusion.8
  (2 shorter events, 0.0 us)
Async XLA Ops:
  0.7 8.3 %copy-start.6 = (s32[384]{0:T(512)S(1)}, s32[384]{0:T(512)}, u32[]{:S(2)}) copy-start(s32[384]{0:T(512)} %param.22) | copy-start | bytes 4612
  0.7 9.0 %copy-start = (s32[384,49]{0,1:T(8,128)S(1)}, s32[384,49]{0,1:T(8,128)}, u32[]{:S(2)}) copy-start(s32[384,49]{0,1:T(8,128)} %param.21) | copy-start | bytes 225796
  0.7 9.8 %copy-start.1 = (f32[1000]{0:T(1024)S(1)}, f32[1000]{0:T(1024)}, u32[]{:S(2)}) copy-start(f32[1000]{0:T(1024)} %param.28) | copy-start | bytes 12004
  441.9 10.2 %copy-start.2 = (f32[24,128]{1,0:T(8,128)S(1)}, f32[24,128]{1,0:T(8,128)}, u32[]{:S(2)}) copy-start(f32[24,128]{1,0:T(8,128)} %get-tuple-element.37) | copy-start | bytes 36868
  441.9 10.2 %copy-start.3 = (f32[4,64]{1,0:T(4,128)S(1)}, f32[4,64]{1,0:T(4,128)}, u32[]{:S(2)}) copy-start(f32[4,64]{1,0:T(4,128)} %own_norms.1) | copy-start | bytes 3076
  442.0 10.2 %copy-start.7 = (f32[4,64]{1,0:T(4,128)S(1)}, f32[4,64]{1,0:T(4,128)}, u32[]{:S(2)}) copy-start(f32[4,64]{1,0:T(4,128)} %param.38) | copy-start | bytes 3076
  442.0 10.2 %copy-start.8 = (f32[4,64]{1,0:T(4,128)S(1)}, f32[4,64]{1,0:T(4,128)}, u32[]{:S(2)}) copy-start(f32[4,64]{1,0:T(4,128)} %param.39) | copy-start | bytes 3076
  442.0 10.9 %copy-start.4 = (f32[1000]{0:T(1024)S(1)}, f32[1000]{0:T(1024)}, u32[]{:S(2)}) copy-start(f32[1000]{0:T(1024)} %param.36) | copy-start | bytes 12004
  442.0 10.9 %copy-start.5 = (f32[1000]{0:T(1024)S(1)}, f32[1000]{0:T(1024)}, u32[]{:S(2)}) copy-start(f32[1000]{0:T(1024)} %param.37) | copy-start | bytes 12004

commit v9 on v8

--- a/solution.py
+++ b/solution.py
@@ -875,7 +875,7 @@
     blocks, rows, width = outers.shape
     c_in, taps = reduce_weight.shape[1], spatial_weight.shape[1]
     tiles_one = c_in // width
-    groups = [(0, tiles_one)] + [(t, min(t + 3, blocks)) for t in range(tiles_one, blocks, 3)]
+    groups = [(0, tiles_one)] + [(t, min(t + 2, blocks)) for t in range(tiles_one, blocks, 2)]
     every = [pltpu.make_async_copy(own, own_rows, arrive.at[0, 7])]
     coming = []
     for g, (begin, end) in enumerate(groups):
@@ -930,7 +930,7 @@
     like = lambda a: jax.ShapeDtypeStruct(a.shape, jnp.float32)
     wide = reduce_weight.shape[1] + spatial_weight.shape[1]
     products = pltpu.VMEM(left_stats.shape, jnp.float32)
-    groups = 1 + -(-(spatial_weight.shape[1] // width) // 3)
+    groups = 1 + -(-(spatial_weight.shape[1] // width) // 2)
     head_new, head_first_new, head_second_new, *rest = pl.pallas_call(
         finish_kernel,
         out_shape=(like(head_weight), like(head_weight), like(head_weight), like(reduce_weight), like(spatial_weight),

time: 454 us -> 454 us (level)
  no operation moved by 1% of the time
where the time goes in v9:
time: 454 us
  Pallas kernels  441 us (97%)
  local copies, waits for them, and re-layouts  11.1 us (2%)
    pallas_call x1, Pallas kernels, local_step(): pl.pallas_call(step_kernel, out_shape=(shape((9, nz, 2, rows, width), f32...  336 us
    pallas_call x1, Pallas kernels, settle(): pl.pallas_call(functools.partial(settle_kernel, chunks), out_shape=(jax.S...  94.8 us
    pallas_call x1, Pallas kernels, finish(): pl.pallas_call(finish_kernel, out_shape=(like(head_weight), like(head_wei...  10.2 us

profile of v9, /device:TPU:0, one launch (start us, length us, event | category | flops | bytes accessed | tf_op | source)
XLA Modules:
  0.0 454.2 jit_solution(4228225019211177612)
XLA Ops:
  0.7 0.0 copy-start.6
  0.7 0.0 copy-start
  0.7 0.0 copy-start.1
  0.7 8.2 %copy.39 = bf16[8,48,49,256]{3,1,2,0:T(8,128)(2,1)} copy(bf16[8,48,49,256]{3,1,0,2:T(8,128)(2,1)} %bitcast.17) | data formatting | bytes 19267584 | tf_op jit(solution)/shard_map/reshape | solution.py:1000
  8.9 0.0 copy-done.6
  8.9 0.8 broadcast_in_dim.8.all_labels
  9.7 0.0 copy-done
  9.7 0.8 copy.40.pixel_mask
  10.5 0.0 copy-done.1
  10.5 0.6 pad.4
  11.1 336.0 %step.1 = (f32[9,4,2,16,512]{4,3,2,1,0:T(8,128)}, f32[4,2,2,2,16,2048]{5,4,3,2,1,0:T(8,128)}, f32[512,1024]{1,0:T(8,128)}, f32[24,128]{1,0:T(8,128)}, f32[16,768...) custom-call(bf16[8,7,336,256]{3,2,1,0:T(8,128)(2,1)} %bitcast.16, ...), custom_call_target="tpu_custom_call" | custom-call | tf_op jit(solution)/shard_map/step/pallas_call | solution.py:507
  347.2 94.8 %settle.1 = (f32[2,2,16,7680]{3,2,1,0:T(8,128)}, f32[13,64,512]{2,1,0:T(8,128)}, f32[13,64,512]{2,1,0:T(8,128)}, f32[13,64,512]{2,1,0:T(8,128)}, f32[16,128]{1,0:T(8,128)}) custom-call(f32[9,4,2,16,512]{4,3,2,1,0:T(8,128)} %get-tuple-element.38.taps, f32[4,2,2,2,16,2048]{5,4,3,2,1,0:T(8,128)} %get-tuple-element.39.reduce, ...), custom_call_target="tpu_custom_call" | custom-call | tf_op jit(solution)/shard_map/settle/pallas_call | solution.py:836
  441.9 0.0 copy-start.2
  441.9 0.0 copy-start.3
  442.0 0.0 copy-start.7
  442.0 0.0 copy-start.8
  442.0 0.0 copy-start.4
  442.0 0.0 copy-start.5
  442.0 10.2 %finish.1 = (f32[64,1000]{1,0:T(8,128)}, f32[64,1000]{1,0:T(8,128)}, f32[64,1000]{1,0:T(8,128)}, f32[64,2048]{1,0:T(8,128)}, f32[64,4608]{1,0:T(8,128)}, /*index...) custom-call(f32[16,128]{1,0:T(8,128)} %get-tuple-element.43.size, ...), custom_call_target="tpu_custom_call" | custom-call | tf_op jit(solution)/shard_map/finish/pallas_call | solution.py:934
  452.2 0.0 copy-done.2
  452.3 0.0 copy-done.3
  452.3 0.0 copy-done.7
  452.3 0.0 copy-done.8
  452.3 0.7 multiply_subtract_fusion.1
  453.0 0.0 copy-done.4
  453.0 0.0 copy-done.5
  453.0 0.6 multiply_subtract_fusion
  453.6 0.6 fusion.8
  (2 shorter events, 0.0 us)
Async XLA Ops:
  0.7 8.3 %copy-start.6 = (s32[384]{0:T(512)S(1)}, s32[384]{0:T(512)}, u32[]{:S(2)}) copy-start(s32[384]{0:T(512)} %param.22) | copy-start | bytes 4612
  0.7 9.0 %copy-start = (s32[384,49]{0,1:T(8,128)S(1)}, s32[384,49]{0,1:T(8,128)}, u32[]{:S(2)}) copy-start(s32[384,49]{0,1:T(8,128)} %param.21) | copy-start | bytes 225796
  0.7 9.8 %copy-start.1 = (f32[1000]{0:T(1024)S(1)}, f32[1000]{0:T(1024)}, u32[]{:S(2)}) copy-start(f32[1000]{0:T(1024)} %param.28) | copy-start | bytes 12004
  441.9 10.3 %copy-start.2 = (f32[24,128]{1,0:T(8,128)S(1)}, f32[24,128]{1,0:T(8,128)}, u32[]{:S(2)}) copy-start(f32[24,128]{1,0:T(8,128)} %get-tuple-element.37) | copy-start | bytes 36868
  441.9 10.3 %copy-start.3 = (f32[4,64]{1,0:T(4,128)S(1)}, f32[4,64]{1,0:T(4,128)}, u32[]{:S(2)}) copy-start(f32[4,64]{1,0:T(4,128)} %own_norms.1) | copy-start | bytes 3076
  442.0 10.3 %copy-start.7 = (f32[4,64]{1,0:T(4,128)S(1)}, f32[4,64]{1,0:T(4,128)}, u32[]{:S(2)}) copy-start(f32[4,64]{1,0:T(4,128)} %param.38) | copy-start | bytes 3076
  442.0 10.3 %copy-start.8 = (f32[4,64]{1,0:T(4,128)S(1)}, f32[4,64]{1,0:T(4,128)}, u32[]{:S(2)}) copy-start(f32[4,64]{1,0:T(4,128)} %param.39) | copy-start | bytes 3076
  442.0 11.0 %copy-start.4 = (f32[1000]{0:T(1024)S(1)}, f32[1000]{0:T(1024)}, u32[]{:S(2)}) copy-start(f32[1000]{0:T(1024)} %param.36) | copy-start | bytes 12004
  442.0 11.0 %copy-start.5 = (f32[1000]{0:T(1024)S(1)}, f32[1000]{0:T(1024)}, u32[]{:S(2)}) copy-start(f32[1000]{0:T(1024)} %param.37) | copy-start | bytes 12004
